TPU v7x, 512 devices: a whole 4x8x8 slice. The times are simulated.
512 devices in a mesh: dp: 8 (over y), seq: 64 (over x, z, core).
Axes of the slice: x: 4, y: 8, z: 8, core: 2. Of those that a mesh axis runs over, the one named last changes fastest.
Arguments:
- inputs: bfloat16 [8, 8704, 6144], P('dp', 'seq'), may hold values from -6 to 6
- w_project: bfloat16 [6144, 3, 128], P(('dp', 'seq')), may hold values from -0.078125 to 0.078125
- w_output: bfloat16 [6144, 128], P(('dp', 'seq')), may hold values from -0.078125 to 0.078125
- norm_gain: float32 [128], replicated, may hold values from 0.1 to 1.9
- out_grad: bfloat16 [8, 8704, 6144], P('dp', 'seq'), may hold values from -6 to 6
Outputs:
- input_grad: bfloat16 [8, 8704, 6144], P('dp', 'seq')
All inputs are finite; a program needn't handle non-finite values.
Results may differ from a plain program's by a relative error of at most 0.025.
Values may be sent and summed in bfloat16 or wider, within the bound.
No kernel may reach another device: no remote copies, remote signals or barrier semaphores. Data moves between devices by JAX's collectives and lax.ppermute only.
A program may use at most 64 MiB of HBM per device.

v0:
```python
import jax
import jax.numpy as jnp
from jax import lax
from jax.sharding import Mesh
from jax.sharding import PartitionSpec as P

SEQ = ("seq_0", "seq_1", "seq_2")
DP_SEQ = ("dp", "seq_0", "seq_1", "seq_2")


def filled_with(value, identity):
    return jnp.zeros_like(value) + jnp.asarray(identity, value.dtype)


def prefix_by_axis(value, axes, combine, identity, reverse):
    before = start = filled_with(value, identity)
    so_far = value
    for axis in reversed(axes):
        peers, place = (lax.axis_size(axis), lax.axis_index(axis))
        pieces = lax.all_gather(so_far.astype(jnp.bfloat16), axis)
        inside, so_far = (start, start)
        for k in reversed(range(peers)) if reverse else range(peers):
            passed = k > place if reverse else k < place
            so_far = combine(so_far, pieces[k].astype(value.dtype))
            inside = jnp.where(passed, so_far, inside)
        before = combine(inside, before)
    return before


def in_one_piece(arrays, axis, dim, along):
    columns = [a.reshape(*a.shape[:along], -1) for a in arrays]
    both = jnp.concatenate(columns, axis=along)
    whole, at, outs = (lax.all_gather(both, axis, axis=dim, tiled=True), 0, [])
    for a, column in zip(arrays, columns):
        section = whole[..., at : at + column.shape[along]]
        outs.append(section.reshape(*section.shape[:along], *a.shape[along:]))
        at += column.shape[along]
    return tuple(outs)


def contract(left, right, left_dim, right_dim):
    return lax.dot_general(
        left, right, (((left_dim,), (right_dim,)), ((), ())), preferred_element_type=jnp.float32
    )


def add_states(earlier, later):
    return earlier + later


def other_blocks(local, reverse):
    return prefix_by_axis(local, SEQ, add_states, jnp.zeros_like(local), reverse)


def per_device(inputs, w_project, w_output, norm_gain, out_grad):
    proj_full, out_full = in_one_piece((w_project, w_output), DP_SEQ, 0, 1)
    width = proj_full.shape[0]
    head = proj_full.shape[2]
    flat_proj = proj_full.reshape(width, 3 * head)
    tokens = inputs[0]
    grads_in = out_grad[0]
    count = tokens.shape[0]
    projected = jnp.dot(tokens, flat_proj, preferred_element_type=jnp.float32).astype(jnp.bfloat16)
    queries = projected[:, :head]
    key_rows = projected[:, head : 2 * head]
    value_rows = projected[:, 2 * head :]
    row_ids = lax.broadcasted_iota(jnp.int32, (count, count), 0)
    col_ids = lax.broadcasted_iota(jnp.int32, (count, count), 1)
    causal = row_ids >= col_ids
    scores = jnp.where(causal, contract(queries, key_rows, 1, 1), 0.0).astype(jnp.bfloat16)
    intra_part = jnp.dot(scores, value_rows, preferred_element_type=jnp.float32)
    local_state = contract(key_rows, value_rows, 0, 0)
    prior_state = other_blocks(local_state, False).astype(jnp.bfloat16)
    attended = intra_part + jnp.dot(queries, prior_state, preferred_element_type=jnp.float32)
    inv_rms = lax.rsqrt(jnp.mean(attended * attended, axis=-1, keepdims=True) + 1e-06)
    head_grad = jnp.dot(grads_in, out_full, preferred_element_type=jnp.float32)
    scaled = norm_gain * head_grad
    attn_grad = inv_rms * scaled - attended * inv_rms**3 * jnp.mean(
        attended * scaled, axis=-1, keepdims=True
    )
    attn_grad = attn_grad.astype(jnp.bfloat16)
    prob_grad = jnp.where(causal, contract(attn_grad, value_rows, 1, 1), 0.0).astype(jnp.bfloat16)
    local_grad = contract(queries, attn_grad, 0, 0)
    later_state = other_blocks(local_grad, True).astype(jnp.bfloat16)
    query_grad = jnp.dot(prob_grad, key_rows, preferred_element_type=jnp.float32) + contract(
        attn_grad, prior_state, 1, 1
    )
    key_grad = contract(prob_grad, queries, 0, 0) + contract(value_rows, later_state, 1, 1)
    value_grad = contract(scores, attn_grad, 0, 0) + jnp.dot(
        key_rows, later_state, preferred_element_type=jnp.float32
    )
    joined = jnp.concatenate([query_grad, key_grad, value_grad], axis=-1).astype(jnp.bfloat16)
    result = contract(joined, flat_proj, 1, 1).astype(jnp.bfloat16)
    return result[None]


def solution(mesh):
    split = Mesh(mesh.devices.reshape(mesh.shape["dp"], 4, 8, 2), ("dp", "seq_0", "seq_1", "seq_2"))
    in_specs = (P("dp", SEQ, None), P(DP_SEQ, None, None), P(DP_SEQ, None), P(), P("dp", SEQ, None))
    out_specs = P("dp", SEQ, None)
    return jax.shard_map(
        per_device, mesh=split, in_specs=in_specs, out_specs=out_specs, check_vma=False
    )
```

profile of v0, /device:TPU:8, one launch (start us, length us, event | category | flops | bytes accessed | tf_op | source)
XLA Modules:
  0.0 249.9 jit_solution(1982646119336549894)
XLA Ops:
  6.5 0.8 pad.5
  7.4 1.3 maximum_bitcast_fusion
  8.8 135.6 %all-gather.5.cloned.1.call-done = bf16[512,12,512]{2,1,0:T(8,128)(2,1)} async-done(((bf16[1,12,512]{2,1,0:T(8,128)(2,1)}), bf16[512,12,512]{2,1,0:T(8,128)(2,1)}) %all-gather.5.cloned.1.call-update) | async-done | bytes 6291472 | tf_op jit(solution)/shard_map/all_gather | solution.py:33
  144.3 10.9 %reshape.180 = bf16[6144,512]{1,0:T(8,128)(2,1)} reshape(bf16[512,12,512]{2,1,0:T(8,128)(2,1)} %all-gather.5.cloned.1.call-done) | data formatting | bytes 12582912
  155.3 3.5 %fusion.15 = bf16[136,384]{1,0:T(8,128)(2,1)S(1)} fusion(bf16[1,136,6144]{2,1,0:T(8,128)(2,1)S(1)} %copy-done, bf16[6144,512]{1,0:T(8,128)(2,1)} %reshape.180), kind=kOutput, calls=%fused_computation.14 | convolution fusion | flops 641780736 | bytes 6494208 | tf_op jit(solution)/shard_map/dot_general | solution.py:63
  158.8 0.2 fusion.13
  159.0 0.2 convolution_convert_fusion.2
  159.2 0.2 fusion.81
  159.4 1.9 all-gather
  161.3 24.8 %all_gather.34 = bf16[8,128,128]{2,1,0:T(8,128)(2,1)S(1)} all-gather(bf16[1,128,128]{2,1,0:T(8,128)(2,1)S(1)} %fusion.72), channel_id=1, replica_groups=mesh['dp'=8,'seq_0'=4,'seq_1'=8,'seq_2'=2] {'seq_1'}, dimensions={0}, use_global_device_ids=true | all-gather | bytes 294912 | tf_op jit(solution)/shard_map/all_gather | solution.py:20
  186.1 12.0 %all_gather.35 = bf16[4,128,128]{2,1,0:T(8,128)(2,1)S(1)} all-gather(bf16[1,128,128]{2,1,0:T(8,128)(2,1)S(1)} %fusion.71), channel_id=1, replica_groups=mesh['dp'=8,'seq_0'=4,'seq_1'=8,'seq_2'=2] {'seq_0'}, dimensions={0}, use_global_device_ids=true | all-gather | bytes 163840 | tf_op jit(solution)/shard_map/all_gather | solution.py:20
  198.1 0.6 fusion.25
  198.8 0.3 multiply_reduce_fusion.1
  199.3 0.2 fusion.94
  199.5 0.2 convolution_convert_fusion.1
  199.7 0.2 fusion.14
  199.9 0.2 fusion.89
  200.3 1.9 all-gather.1
  202.1 24.8 %all_gather.38 = bf16[8,128,128]{2,1,0:T(8,128)(2,1)S(1)} all-gather(bf16[1,128,128]{2,1,0:T(8,128)(2,1)S(1)} %fusion.73), channel_id=1, replica_groups=mesh['dp'=8,'seq_0'=4,'seq_1'=8,'seq_2'=2] {'seq_1'}, dimensions={0}, use_global_device_ids=true | all-gather | bytes 294912 | tf_op jit(solution)/shard_map/all_gather | solution.py:20
  227.0 12.0 %all_gather.39 = bf16[4,128,128]{2,1,0:T(8,128)(2,1)S(1)} all-gather(bf16[1,128,128]{2,1,0:T(8,128)(2,1)S(1)} %fusion.70), channel_id=1, replica_groups=mesh['dp'=8,'seq_0'=4,'seq_1'=8,'seq_2'=2] {'seq_0'}, dimensions={0}, use_global_device_ids=true | all-gather | bytes 163840 | tf_op jit(solution)/shard_map/all_gather | solution.py:20
  239.1 0.2 fusion.32
  239.3 0.2 fusion.31
  239.5 0.2 fusion.30
  239.6 3.4 %fusion = bf16[1,136,6144]{2,1,0:T(8,128)(2,1)} fusion(bf16[6144,512]{1,0:T(8,128)(2,1)S(1)} %copy-done.1, bf16[136,128]{1,0:T(8,128)(2,1)S(1)} %fusion.32, bf16[136,128]{1,0:T(8,128)(2,1)S(1)} %fusion.31, bf16[136,128]{1,0:T(8,128)(2,1)S(1)} %fusion.30), kind=kOutput, calls=%fused_computation.1 | convolution fusion | flops 642877440 | bytes 6494208 | tf_op jit(solution)/shard_map/dot_general | solution.py:42
  (20 shorter events, 0.6 us)
Async XLA Ops:
  6.5 148.7 %copy-start = (bf16[1,136,6144]{2,1,0:T(8,128)(2,1)S(1)}, bf16[1,136,6144]{2,1,0:T(8,128)(2,1)}, u32[]{:S(2)}) copy-start(bf16[1,136,6144]{2,1,0:T(8,128)(2,1)} %param.5) | copy-start | bytes 5013508
  6.5 137.8 %all-gather.5.cloned.1.call-start = ((), (), s32[]{:S(2)}) async-start(), calls=%async_computation | async-start | bytes 8404992 | tf_op jit(solution)/shard_map/all_gather | solution.py:33
  155.3 42.8 %copy-start.1 = (bf16[6144,512]{1,0:T(8,128)(2,1)S(1)}, bf16[6144,512]{1,0:T(8,128)(2,1)}, u32[]{:S(2)}) copy-start(bf16[6144,512]{1,0:T(8,128)(2,1)} %reshape.180) | copy-start | bytes 18874372
  155.3 42.8 %copy-start.2 = (bf16[1,136,6144]{2,1,0:T(8,128)(2,1)S(1)}, bf16[1,136,6144]{2,1,0:T(8,128)(2,1)}, u32[]{:S(2)}) copy-start(bf16[1,136,6144]{2,1,0:T(8,128)(2,1)} %param.9) | copy-start | bytes 5013508
  155.3 42.8 %copy-start.3 = (f32[128]{0:T(128)S(1)}, f32[128]{0:T(128)}, u32[]{:S(2)}) copy-start(f32[128]{0:T(128)} %param.8) | copy-start | bytes 1540
Sparse Core Ops, SparseCore 0:
  11.8 132.4 all-gather.4
where the time goes:
time: 250 us
  waiting for transfers between devices  136 us (54%)
  blocking collectives  77.4 us (31%)
  between operations  13.6 us (5%)
  local copies, waits for them, and re-layouts  11.8 us (5%)
  matrix products  9.8 us (4%)
    all_gather x1, waiting for transfers between devices, in_one_piece(): whole, at, outs = (lax.all_gather(both, axis, axis=dim, tiled=True), 0, [])  136 us
    all_gather x6, blocking collectives, prefix_by_axis(): pieces = lax.all_gather(so_far.astype(jnp.bfloat16), axis)  77.4 us
    unnamed x11, local copies, waits for them, and re-layouts  11.8 us
  transfers between devices with their start and end apart: 1, of which 1 were waited for; matrix products, arithmetic and copies ran while one was open for 0% of the time, Pallas kernels for 0%

commit v1 on v0

v1 whole, which is shorter than its diff:
```python
import jax
import jax.numpy as jnp
from jax import lax
from jax.sharding import Mesh
from jax.sharding import PartitionSpec as P

SEQ = ("x", "z", "core")
DP_SEQ = ("dp", "x", "z", "core")
ROWS = ("dp", "z")


def contract(left, right, left_dim, right_dim):
    return lax.dot_general(
        left, right, (((left_dim,), (right_dim,)), ((), ())), preferred_element_type=jnp.float32
    )


def spread(block, axes):
    peers = lax.axis_size(axes)
    return lax.all_to_all(
        jnp.broadcast_to(block[None], (peers, *block.shape)), axes, 0, 0, tiled=True
    )


def core_swap(block):
    return lax.ppermute(block, "core", [(0, 1), (1, 0)])


def by_core(mine, other):
    first = lax.axis_index("core") == 0
    return jnp.where(first, mine, other), jnp.where(first, other, mine)


def rows_in_order(block):
    xs, dps = lax.axis_size("x"), lax.axis_size("dp")
    head = block.shape[-1]
    return block.reshape(xs, dps, -1, head).swapaxes(0, 1).reshape(-1, head)


def other_blocks(local, reverse):
    head = local.shape[0]
    peers = lax.axis_size(SEQ)
    pieces = local.astype(jnp.bfloat16).reshape(peers, head // peers, head)
    pieces = lax.all_to_all(pieces, SEQ, 0, 0, tiled=True).reshape(peers, -1)
    to = lax.broadcasted_iota(jnp.int32, (peers, peers), 0)
    frm = lax.broadcasted_iota(jnp.int32, (peers, peers), 1)
    mask = ((frm > to) if reverse else (frm < to)).astype(jnp.bfloat16)
    sums = contract(mask, pieces, 1, 0).astype(jnp.bfloat16)
    sums = lax.all_to_all(sums.reshape(peers, head // peers, head), SEQ, 0, 0, tiled=True)
    return sums.reshape(head, head)


def per_device(inputs, w_project, w_output, norm_gain, out_grad):
    tokens = inputs[0]
    grads_in = out_grad[0]
    count = tokens.shape[0]
    bf16 = jnp.bfloat16

    to_first = jnp.concatenate([w_project[:, 1], w_project[:, 0]], axis=1)
    to_second = jnp.concatenate([w_project[:, 2], w_output], axis=1)
    pair = lax.all_to_all(jnp.stack([to_first, to_second]), "core", 0, 0, tiled=True)
    head = w_output.shape[1]
    pair = pair.reshape(-1, 2 * head)

    def gathered(block):
        plane = spread(block, ROWS).reshape(-1, head)
        return spread(plane, "x")

    kv_mine = gathered(pair[:, :head])
    qo_mine = gathered(pair[:, head:])
    w_key, w_value = by_core(kv_mine, core_swap(kv_mine))
    w_query, w_out = by_core(qo_mine, core_swap(qo_mine))
    w_query, w_key, w_value, w_out = map(rows_in_order, (w_query, w_key, w_value, w_out))

    key_rows = contract(tokens, w_key, 1, 0).astype(bf16)
    value_rows = contract(tokens, w_value, 1, 0).astype(bf16)
    local_state = contract(key_rows, value_rows, 0, 0)
    prior_state = other_blocks(local_state, False)

    queries = contract(tokens, w_query, 1, 0).astype(bf16)
    head_grad = contract(grads_in, w_out, 1, 0)
    row_ids = lax.broadcasted_iota(jnp.int32, (count, count), 0)
    col_ids = lax.broadcasted_iota(jnp.int32, (count, count), 1)
    causal = row_ids >= col_ids
    scores = jnp.where(causal, contract(queries, key_rows, 1, 1), 0.0).astype(bf16)
    attended = contract(scores, value_rows, 1, 0) + contract(queries, prior_state, 1, 0)
    inv_rms = lax.rsqrt(jnp.mean(attended * attended, axis=-1, keepdims=True) + 1e-06)
    scaled = norm_gain * head_grad
    attn_grad = inv_rms * scaled - attended * inv_rms**3 * jnp.mean(
        attended * scaled, axis=-1, keepdims=True
    )
    attn_grad = attn_grad.astype(bf16)
    local_grad = contract(queries, attn_grad, 0, 0)
    later_state = other_blocks(local_grad, True)
    prob_grad = jnp.where(causal, contract(attn_grad, value_rows, 1, 1), 0.0).astype(bf16)
    query_grad = contract(prob_grad, key_rows, 1, 0) + contract(attn_grad, prior_state, 1, 1)
    key_grad = contract(prob_grad, queries, 0, 0) + contract(value_rows, later_state, 1, 1)
    value_grad = contract(scores, attn_grad, 0, 0) + contract(key_rows, later_state, 1, 0)
    result = (
        contract(query_grad.astype(bf16), w_query, 1, 1)
        + contract(key_grad.astype(bf16), w_key, 1, 1)
        + contract(value_grad.astype(bf16), w_value, 1, 1)
    )
    return result.astype(bf16)[None]


def solution(mesh):
    split = Mesh(mesh.devices.reshape(mesh.shape["dp"], 4, 8, 2), DP_SEQ)
    in_specs = (P("dp", SEQ, None), P(DP_SEQ, None, None), P(DP_SEQ, None), P(), P("dp", SEQ, None))
    out_specs = P("dp", SEQ, None)
    return jax.shard_map(
        per_device, mesh=split, in_specs=in_specs, out_specs=out_specs, check_vma=False
    )
```

time: 250 us -> 197 us (0.79)
  the two profiles are of different devices: /device:TPU:8 before, /device:TPU:1 now
where the time goes in v1:
time: 197 us; the launch traced here: 196 us
  blocking collectives  77.4 us (39%)
  waiting for transfers between devices  40.3 us (20%)
  starting transfers between devices  39.9 us (20%)
  matrix products  27.6 us (14%)
  local copies, waits for them, and re-layouts  6.08 us (3%)
  other arithmetic  4.56 us (2%)
    all_to_all x3, blocking collectives, spread(): lax.all_to_all(jnp.broadcast_to(block[None], (peers, *block.shape)), axes...  67.1 us
    dot_general x18, matrix products, contract(): lax.dot_general(left, right, (((left_dim,), (right_dim,)), ((), ())), pre...  27.6 us
    all_to_all x2, waiting for transfers between devices, other_blocks(): lax.all_to_all(sums.reshape(peers, head // peers, head), SEQ, 0, 0, tiled...  16.3 us
    ppermute x2, starting transfers between devices, core_swap(): return lax.ppermute(block, 'core', [(0, 1), (1, 0)])  14.5 us
    all_to_all x2, waiting for transfers between devices, other_blocks(): pieces = lax.all_to_all(pieces, SEQ, 0, 0, tiled=True).reshape(peers, -1)  14.5 us
    all_to_all x2, starting transfers between devices, other_blocks(): pieces = lax.all_to_all(pieces, SEQ, 0, 0, tiled=True).reshape(peers, -1)  11.6 us
    all_to_all x1, blocking collectives, per_device(): lax.all_to_all(jnp.stack([to_first, to_second]), 'core', 0, 0, tiled=True)  10.3 us
    all_to_all x2, starting transfers between devices, other_blocks(): lax.all_to_all(sums.reshape(peers, head // peers, head), SEQ, 0, 0, tiled...  9.4 us
  transfers between devices with their start and end apart: 7, of which 6 were waited for; matrix products, arithmetic and copies ran while one was open for 5% of the time, Pallas kernels for 0%

profile of v1, /device:TPU:1, one launch (start us, length us, event | category | flops | bytes accessed | tf_op | source)
XLA Modules:
  0.0 196.0 jit_solution(6221075206939387023)
XLA Ops:
  1.6 10.3 %all_to_all.45 = bf16[2,12,256]{2,1,0:T(8,128)(2,1)S(1)} all-to-all(bf16[2,12,256]{2,1,0:T(8,128)(2,1)S(1)} %pad_maximum_fusion), channel_id=1, replica_groups=mesh['dp'=8,'x'=4,'z'=8,'core'=2] {'core'}, dimensions={0} | all-to-all | bytes 24576 | tf_op jit(solution)/shard_map/all_to_all | solution.py:61
  12.0 25.7 %all_to_all.46 = bf16[64,24,128]{2,1,0:T(8,128)(2,1)S(1)} all-to-all(bf16[64,24,128]{2,1,0:T(8,128)(2,1)S(1)} %broadcast_in_dim.19), channel_id=1, replica_groups=mesh['dp'=8,'x'=4,'z'=8,'core'=2] {'dp','z'}, dimensions={0} | all-to-all | bytes 786432 | tf_op jit(solution)/shard_map/all_to_all | solution.py:20
  37.7 20.7 %all_to_all.47 = bf16[64,24,128]{2,1,0:T(8,128)(2,1)S(1)} all-to-all(bf16[64,24,128]{2,1,0:T(8,128)(2,1)S(1)} %broadcast_in_dim.40), channel_id=1, replica_groups=mesh['dp'=8,'x'=4,'z'=8,'core'=2] {'dp','z'}, dimensions={0} | all-to-all | bytes 786432 | tf_op jit(solution)/shard_map/all_to_all | solution.py:20
  58.6 20.7 %all_to_all.48 = bf16[4,1536,128]{2,1,0:T(8,128)(2,1)S(1)} all-to-all(bf16[4,1536,128]{2,1,0:T(8,128)(2,1)S(1)} %broadcast_in_dim.39), channel_id=1, replica_groups=mesh['dp'=8,'x'=4,'z'=8,'core'=2] {'x'}, dimensions={0} | all-to-all | bytes 3145728 | tf_op jit(solution)/shard_map/all_to_all | solution.py:20
  80.7 4.4 %all-to-all-start.4 = ((bf16[4,1536,128]{2,1,0:T(8,128)(2,1)}), bf16[4,1536,128]{2,1,0:T(8,128)(2,1)}, u32[]{:S(2)}, u32[]{:S(2)}) async-start(bf16[4,1536,128]{2,1,0:T(8,128)(2,1)} %broadcast_in_dim.42), calls=%async_computation.4 | async-start | bytes 3145728 | tf_op jit(solution)/shard_map/all_to_all | solution.py:20
  85.0 6.7 %collective-permute-start = (bf16[4,1536,128]{2,1,0:T(8,128)(2,1)S(1)}, bf16[4,1536,128]{2,1,0:T(8,128)(2,1)}, u32[]{:S(2)}, u32[]{:S(2)}) collective-permute-start(bf16[4,1536,128]{2,1,0:T(8,128)(2,1)S(1)} %all_to_all.48), channel_id=1, source_target_pairs={{0,1},{1,0},{2,3},{3,2},{4,5},{5,4},{6,7},{7,6},{8,9},{9,8},{10,11... | collective-permute-start | bytes 4718600 | tf_op jit(solution)/shard_map/ppermute | solution.py:26
  91.7 9.1 %all-to-all-done.4 = bf16[4,1536,128]{2,1,0:T(8,128)(2,1)} async-done(((bf16[4,1536,128]{2,1,0:T(8,128)(2,1)}), bf16[4,1536,128]{2,1,0:T(8,128)(2,1)}, u32[]{:S(2)}, u32[]{:S(2)}) %all-to-all-start.4) | async-done | bytes 1572896 | tf_op jit(solution)/shard_map/all_to_all | solution.py:20
  100.8 7.9 %collective-permute-start.1 = (bf16[4,1536,128]{2,1,0:T(8,128)(2,1)}, bf16[4,1536,128]{2,1,0:T(8,128)(2,1)}, u32[]{:S(2)}, u32[]{:S(2)}) collective-permute-start(bf16[4,1536,128]{2,1,0:T(8,128)(2,1)} %all-to-all-done.4), channel_id=1, source_target_pairs={{0,1},{1,0},{2,3},{3,2},{4,5},{5,4},{6,7},{7,6},{8,9},{9,8},{10,11... | collective-permute-start | bytes 4718600 | tf_op jit(solution)/shard_map/ppermute | solution.py:26
  108.7 1.6 broadcast_select_fusion
  112.0 2.1 %broadcast_select_fusion.1 = (bf16[4,1536,128]{2,1,0:T(8,128)(2,1)S(1)}, bf16[4,1536,128]{2,1,0:T(8,128)(2,1)S(1)}) fusion(bf16[4,1536,128]{2,1,0:T(8,128)(2,1)} %collective-permute-done.1, bf16[4,1536,128]{2,1,0:T(8,128)(2,1)} %all-to-all-done.4, pred[]{:T(512)S(6)} %eq.4), kind=kLoop, calls=%fused_computation.13 | loop fusion | flops 1572864 | bytes 6291457 | tf_op jit(solution)/shard_map/jit(_where)/select_n | solution.py:31
  117.7 6.9 %all-to-all-start.5 = ((bf16[64,2,128]{2,1,0:T(2,128)(2,1)}), bf16[64,2,128]{2,1,0:T(2,128)(2,1)S(1)}, u32[]{:S(2)}, u32[]{:S(2)}) async-start(bf16[64,2,128]{2,1,0:T(2,128)(2,1)} %bitcast.17), calls=%async_computation.5 | async-start | bytes 65536 | tf_op jit(solution)/shard_map/all_to_all | solution.py:44
  124.7 2.5 %fusion.15 = f32[136,128]{1,0:T(8,128)S(1)} fusion(bf16[6144,128]{1,0:T(8,128)(2,1)} %bitcast.102, bf16[1,136,6144]{2,1,0:T(8,128)(2,1)} %param.9, f32[128]{0:T(128)S(1)} %copy-done.4), kind=kOutput, calls=%fused_computation.25 | convolution fusion | flops 213926912 | bytes 3314176 | tf_op jit(solution)/shard_map/dot_general | solution.py:13
  128.0 5.9 %all-to-all-done.5 = bf16[64,2,128]{2,1,0:T(2,128)(2,1)S(1)} async-done(((bf16[64,2,128]{2,1,0:T(2,128)(2,1)}), bf16[64,2,128]{2,1,0:T(2,128)(2,1)S(1)}, u32[]{:S(2)}, u32[]{:S(2)}) %all-to-all-start.5) | async-done | bytes 32800 | tf_op jit(solution)/shard_map/all_to_all | solution.py:44
  134.7 4.7 %all-to-all-start.6 = ((bf16[64,2,128]{2,1,0:T(2,128)(2,1)}), bf16[64,2,128]{2,1,0:T(2,128)(2,1)S(1)}, u32[]{:S(2)}, u32[]{:S(2)}) async-start(bf16[64,2,128]{2,1,0:T(2,128)(2,1)} %reshape.83), calls=%async_computation.6 | async-start | bytes 65536 | tf_op jit(solution)/shard_map/all_to_all | solution.py:49
  139.4 1.7 fusion.37
  141.1 7.7 %all-to-all-done.6 = bf16[64,2,128]{2,1,0:T(2,128)(2,1)S(1)} async-done(((bf16[64,2,128]{2,1,0:T(2,128)(2,1)}), bf16[64,2,128]{2,1,0:T(2,128)(2,1)S(1)}, u32[]{:S(2)}, u32[]{:S(2)}) %all-to-all-start.6) | async-done | bytes 32800 | tf_op jit(solution)/shard_map/all_to_all | solution.py:49
  150.1 1.7 fusion.40
  152.9 4.7 %all-to-all-start.7 = ((bf16[64,2,128]{2,1,0:T(2,128)(2,1)}), bf16[64,2,128]{2,1,0:T(2,128)(2,1)S(1)}, u32[]{:S(2)}, u32[]{:S(2)}) async-start(bf16[64,2,128]{2,1,0:T(2,128)(2,1)} %bitcast.24), calls=%async_computation.7 | async-start | bytes 65536 | tf_op jit(solution)/shard_map/all_to_all | solution.py:44
  158.4 8.6 %all-to-all-done.7 = bf16[64,2,128]{2,1,0:T(2,128)(2,1)S(1)} async-done(((bf16[64,2,128]{2,1,0:T(2,128)(2,1)}), bf16[64,2,128]{2,1,0:T(2,128)(2,1)S(1)}, u32[]{:S(2)}, u32[]{:S(2)}) %all-to-all-start.7) | async-done | bytes 32800 | tf_op jit(solution)/shard_map/all_to_all | solution.py:44
  167.8 4.7 %all-to-all-start.8 = ((bf16[64,2,128]{2,1,0:T(2,128)(2,1)}), bf16[64,2,128]{2,1,0:T(2,128)(2,1)S(1)}, u32[]{:S(2)}, u32[]{:S(2)}) async-start(bf16[64,2,128]{2,1,0:T(2,128)(2,1)} %reshape.89), calls=%async_computation.8 | async-start | bytes 65536 | tf_op jit(solution)/shard_map/all_to_all | solution.py:49
  173.3 8.6 %all-to-all-done.8 = bf16[64,2,128]{2,1,0:T(2,128)(2,1)S(1)} async-done(((bf16[64,2,128]{2,1,0:T(2,128)(2,1)}), bf16[64,2,128]{2,1,0:T(2,128)(2,1)S(1)}, u32[]{:S(2)}, u32[]{:S(2)}) %all-to-all-start.8) | async-done | bytes 32800 | tf_op jit(solution)/shard_map/all_to_all | solution.py:49
  181.9 4.4 %fusion.30 = f32[136,6144]{1,0:T(8,128)} fusion(bf16[6144,128]{1,0:T(8,128)(2,1)} %bitcast.101, f32[136,128]{1,0:T(8,128)} %fusion.39, bf16[128,136]{0,1:T(8,128)(2,1)S(1)} %fusion.27, bf16[128,128]{1,0:T(8,128)(2,1)S(1)} %bitcast.109), kind=kOutput, calls=%fused_computation.36 | convolution fusion | flops 218400768 | bytes 5052416 | tf_op jit(solution)/shard_map/dot_general | solution.py:13
  186.2 5.0 %convolution_add_fusion.1 = f32[136,6144]{1,0:T(8,128)} fusion(f32[136,6144]{1,0:T(8,128)} %fusion.30, bf16[6144,128]{1,0:T(8,128)(2,1)S(1)} %bitcast.97, f32[136,128]{1,0:T(8,128)} %fusion.38, bf16[136,128]{1,0:T(8,128)(2,1)S(1)} %subtract_convert_fusion, bf16[128,128]{1,0:T(8,128)(2,1)S(1)} %bitcast.112), kind=kOutput, calls=%fused_computation.1 | convolution fusion | flops 219236352 | bytes 8394752 | tf_op jit(solution)/shard_map/dot_general | solution.py:13
  191.2 4.8 %fusion.1 = bf16[1,136,6144]{2,1,0:T(8,128)(2,1)} fusion(f32[136,6144]{1,0:T(8,128)} %convolution_add_fusion.1, bf16[6144,128]{1,0:T(8,128)(2,1)} %bitcast.99, f32[136,128]{1,0:T(8,128)S(1)} %copy-done.3, bf16[128,136]{0,1:T(8,128)(2,1)S(1)} %fusion.24, bf16[128,128]{1,0:T(8,128)(2,1)S(1)} %bitcast.110), kind=kOutput, calls=%fused_computation.3 | convolution fusion | flops 220071936 | bytes 6723584 | tf_op jit(solution)/shard_map/dot_general | solution.py:13
  (45 shorter events, 14.8 us)
Async XLA Ops:
  0.0 114.4 %copy-start = (bf16[1,136,6144]{2,1,0:T(8,128)(2,1)S(1)}, bf16[1,136,6144]{2,1,0:T(8,128)(2,1)}, u32[]{:S(2)}) copy-start(bf16[1,136,6144]{2,1,0:T(8,128)(2,1)} %param.5) | copy-start | bytes 5013508
  80.7 20.1 %all-to-all-start.4 = ((bf16[4,1536,128]{2,1,0:T(8,128)(2,1)}), bf16[4,1536,128]{2,1,0:T(8,128)(2,1)}, u32[]{:S(2)}, u32[]{:S(2)}) async-start(bf16[4,1536,128]{2,1,0:T(8,128)(2,1)} %broadcast_in_dim.42), calls=%async_computation.4 | async-start | bytes 3145728 | tf_op jit(solution)/shard_map/all_to_all | solution.py:20
  85.0 23.6 %collective-permute-start = (bf16[4,1536,128]{2,1,0:T(8,128)(2,1)S(1)}, bf16[4,1536,128]{2,1,0:T(8,128)(2,1)}, u32[]{:S(2)}, u32[]{:S(2)}) collective-permute-start(bf16[4,1536,128]{2,1,0:T(8,128)(2,1)S(1)} %all_to_all.48), channel_id=1, source_target_pairs={{0,1},{1,0},{2,3},{3,2},{4,5},{5,4},{6,7},{7,6},{8,9},{9,8},{10,11... | collective-permute-start | bytes 4718600 | tf_op jit(solution)/shard_map/ppermute | solution.py:26
  100.8 11.2 %collective-permute-start.1 = (bf16[4,1536,128]{2,1,0:T(8,128)(2,1)}, bf16[4,1536,128]{2,1,0:T(8,128)(2,1)}, u32[]{:S(2)}, u32[]{:S(2)}) collective-permute-start(bf16[4,1536,128]{2,1,0:T(8,128)(2,1)} %all-to-all-done.4), channel_id=1, source_target_pairs={{0,1},{1,0},{2,3},{3,2},{4,5},{5,4},{6,7},{7,6},{8,9},{9,8},{10,11... | collective-permute-start | bytes 4718600 | tf_op jit(solution)/shard_map/ppermute | solution.py:26
  114.2 2.0 %copy-start.1 = (bf16[8,4,192,128]{3,2,1,0:T(8,128)(2,1)}, bf16[8,4,192,128]{3,2,1,0:T(8,128)(2,1)S(1)}, u32[]{:S(2)}) copy-start(bf16[8,4,192,128]{3,2,1,0:T(8,128)(2,1)S(1)} %copy.17) | copy-start | bytes 4718596
  114.4 1.3 copy-start.2
  116.3 8.4 %copy-start.4 = (f32[128]{0:T(128)S(1)}, f32[128]{0:T(128)}, u32[]{:S(2)}) copy-start(f32[128]{0:T(128)} %param.8) | copy-start | bytes 1540
  117.7 16.2 %all-to-all-start.5 = ((bf16[64,2,128]{2,1,0:T(2,128)(2,1)}), bf16[64,2,128]{2,1,0:T(2,128)(2,1)S(1)}, u32[]{:S(2)}, u32[]{:S(2)}) async-start(bf16[64,2,128]{2,1,0:T(2,128)(2,1)} %bitcast.17), calls=%async_computation.5 | async-start | bytes 65536 | tf_op jit(solution)/shard_map/all_to_all | solution.py:44
  134.7 14.1 %all-to-all-start.6 = ((bf16[64,2,128]{2,1,0:T(2,128)(2,1)}), bf16[64,2,128]{2,1,0:T(2,128)(2,1)S(1)}, u32[]{:S(2)}, u32[]{:S(2)}) async-start(bf16[64,2,128]{2,1,0:T(2,128)(2,1)} %reshape.83), calls=%async_computation.6 | async-start | bytes 65536 | tf_op jit(solution)/shard_map/all_to_all | solution.py:49
  152.9 14.1 %all-to-all-start.7 = ((bf16[64,2,128]{2,1,0:T(2,128)(2,1)}), bf16[64,2,128]{2,1,0:T(2,128)(2,1)S(1)}, u32[]{:S(2)}, u32[]{:S(2)}) async-start(bf16[64,2,128]{2,1,0:T(2,128)(2,1)} %bitcast.24), calls=%async_computation.7 | async-start | bytes 65536 | tf_op jit(solution)/shard_map/all_to_all | solution.py:44
  167.8 14.1 %all-to-all-start.8 = ((bf16[64,2,128]{2,1,0:T(2,128)(2,1)}), bf16[64,2,128]{2,1,0:T(2,128)(2,1)S(1)}, u32[]{:S(2)}, u32[]{:S(2)}) async-start(bf16[64,2,128]{2,1,0:T(2,128)(2,1)} %reshape.89), calls=%async_computation.8 | async-start | bytes 65536 | tf_op jit(solution)/shard_map/all_to_all | solution.py:49
  186.2 5.0 %copy-start.3 = (f32[136,128]{1,0:T(8,128)S(1)}, f32[136,128]{1,0:T(8,128)}, u32[]{:S(2)}) copy-start(f32[136,128]{1,0:T(8,128)} %fusion.40) | copy-start | bytes 208900

commit v2 on v1

v2 whole, which is shorter than its diff:
```python
import functools

import jax
import jax.numpy as jnp
from jax import lax
from jax.experimental import pallas as pl
from jax.experimental.pallas import tpu as pltpu
from jax.sharding import Mesh
from jax.sharding import PartitionSpec as P

SEQ = ("x", "z", "core")
DP_SEQ = ("dp", "x", "z", "core")
ROWS = ("dp", "z")
BF16 = jnp.bfloat16
F32 = jnp.float32
LIMIT = 40 * 1024 * 1024
SMEM = pl.BlockSpec(memory_space=pltpu.SMEM)
VMEM = pl.BlockSpec(memory_space=pltpu.VMEM)


def contract(left, right, left_dim, right_dim):
    return lax.dot_general(
        left, right, (((left_dim,), (right_dim,)), ((), ())), preferred_element_type=F32
    )


def cost(flops, moved):
    return pl.CostEstimate(flops=flops, bytes_accessed=moved, transcendentals=0)


def spread(block, axes):
    peers = lax.axis_size(axes)
    return lax.all_to_all(
        jnp.broadcast_to(block[None], (peers, *block.shape)), axes, 0, 0, tiled=True
    )


def after(value, *events):
    return lax.optimization_barrier((value, *events))[0]


def core_swap(block):
    return lax.ppermute(block, "core", [(0, 1), (1, 0)])


def columns_kernel(parts, place_ref, tokens_ref, *out_refs):
    width = tokens_ref.shape[1] // parts
    count = tokens_ref.shape[0]
    low = lax.broadcasted_iota(jnp.int32, (count, 128), 1) < 64
    for to in range(4):
        step = lax.rem(to - place_ref[0] + 4, 4)
        first = to * 192
        whole_at = first if to % 2 == 0 else first + 64
        half_at = (first + 128 if to % 2 == 0 else first) // 128 * 128

        pairs = []
        for p in range(parts // 2):
            even = tokens_ref[:, 2 * p * width + half_at : 2 * p * width + half_at + 128]
            odd = tokens_ref[:, (2 * p + 1) * width + half_at : (2 * p + 1) * width + half_at + 128]
            even, odd = even.astype(F32), odd.astype(F32)
            if to % 2 == 0:
                odd = pltpu.roll(odd, 64, 1)
            else:
                even = pltpu.roll(even, 64, 1)
            pairs.append(jnp.where(low, even, odd).astype(BF16))
        for k in range(4):

            @pl.when(step == k)
            def _(k=k, whole_at=whole_at, pairs=pairs):
                for p in range(parts):
                    out_refs[k][:, p * 128 : (p + 1) * 128] = tokens_ref[
                        :, p * width + whole_at : p * width + whole_at + 128
                    ]
                for p, pair in enumerate(pairs):
                    at = parts * 128 + p * 128
                    out_refs[k][:, at : at + 128] = pair


def split_columns(place, tokens, parts):
    count, depth = tokens.shape
    return pl.pallas_call(
        functools.partial(columns_kernel, parts),
        out_shape=[jax.ShapeDtypeStruct((count, depth // 4), BF16)] * 4,
        in_specs=[SMEM, VMEM],
        out_specs=[VMEM] * 4,
        compiler_params=pltpu.CompilerParams(vmem_limit_bytes=LIMIT),
        cost_estimate=cost(0, 4 * tokens.size),
    )(place, tokens)


def partial_kernel(parts, place_ref, t0, t1, t2, t3, mine_ref, other_ref, out_ref, held):
    rows = mine_ref.shape[0] // parts
    odd = lax.rem(place_ref[0], 2)
    whole_at, half_at = odd * 64, (1 - odd) * 128
    for p in range(parts):
        for n, ref in enumerate((mine_ref, other_ref)):
            columns = slice(n * 128, (n + 1) * 128)
            held[p * 128 : (p + 1) * 128, columns] = ref[
                pl.ds(pl.multiple_of(p * rows + whole_at, 64), 128), :
            ]
            at = parts * 128 + p * 64
            held[at : at + 64, columns] = ref[
                pl.ds(pl.multiple_of(p * rows + half_at, 64), 64), :
            ]
    for k, ref in enumerate((t0, t1, t2, t3)):
        source = lax.rem(place_ref[0] - k + 4, 4)
        out_ref[source] = contract(ref[...], held[...], 1, 0).astype(BF16)


def partial_sums(place, pieces, mine, other, parts):
    count, depth = pieces[0].shape
    return pl.pallas_call(
        functools.partial(partial_kernel, parts),
        out_shape=jax.ShapeDtypeStruct((4, count, 256), BF16),
        in_specs=[SMEM] + [VMEM] * 6,
        out_specs=VMEM,
        scratch_shapes=[pltpu.VMEM((depth, 256), BF16)],
        compiler_params=pltpu.CompilerParams(vmem_limit_bytes=LIMIT),
        cost_estimate=cost(8 * count * depth * 256, 8 * count * depth + 4 * depth * 128),
    )(place, *pieces, mine, other)


def state_kernel(place_ref, parts_ref, key_ref, value_ref, state_ref):
    total = parts_ref[0].astype(F32)
    for k in range(1, 4):
        total += parts_ref[k].astype(F32)
    total = total.astype(BF16)
    mine, other = total[:, :128], total[:, 128:]
    first = place_ref[1] == 0
    keys = jnp.where(first, mine, other)
    values = jnp.where(first, other, mine)
    key_ref[...] = keys
    value_ref[...] = values
    state_ref[...] = contract(keys, values, 0, 0).astype(BF16)


def keys_values_state(place, parts):
    count = parts.shape[1]
    row = jax.ShapeDtypeStruct((count, 128), BF16)
    return pl.pallas_call(
        state_kernel,
        out_shape=[row, row, jax.ShapeDtypeStruct((128, 128), BF16)],
        in_specs=[SMEM, VMEM],
        out_specs=[VMEM] * 3,
        compiler_params=pltpu.CompilerParams(vmem_limit_bytes=LIMIT),
        cost_estimate=cost(2 * count * 128 * 128, 2 * parts.size),
    )(place, parts)


def query_kernel(steps, place_ref, tokens_ref, grads_ref, mine_ref, other_ref, q_ref, hg_ref, qs, hs):
    step = pl.program_id(0)

    @pl.when(step == 0)
    def _():
        qs[...] = jnp.zeros_like(qs)
        hs[...] = jnp.zeros_like(hs)

    mine = mine_ref[...].reshape(-1, 128)
    other = other_ref[...].reshape(-1, 128)
    first = place_ref[1] == 0
    w_query = jnp.where(first, mine, other)
    w_out = jnp.where(first, other, mine)
    qs[...] += contract(tokens_ref[...], w_query, 1, 0)
    hs[...] += contract(grads_ref[...], w_out, 1, 0)

    @pl.when(step == steps - 1)
    def _():
        q_ref[...] = qs[...].astype(BF16)
        hg_ref[...] = hs[...]


def queries_head_grad(place, tokens, grads_in, mine, other):
    count, depth = tokens.shape
    xs, steps, rows, _ = mine.shape
    wide = pl.BlockSpec((count, depth // steps), lambda i: (0, i))
    weight = pl.BlockSpec((xs, 1, rows, 128), lambda i: (0, i, 0, 0))
    whole = pl.BlockSpec((count, 128), lambda i: (0, 0))
    return pl.pallas_call(
        functools.partial(query_kernel, steps),
        grid=(steps,),
        out_shape=[
            jax.ShapeDtypeStruct((count, 128), BF16),
            jax.ShapeDtypeStruct((count, 128), F32),
        ],
        in_specs=[SMEM, wide, wide, weight, weight],
        out_specs=[whole, whole],
        scratch_shapes=[pltpu.VMEM((count, 128), F32)] * 2,
        compiler_params=pltpu.CompilerParams(vmem_limit_bytes=LIMIT),
        cost_estimate=cost(4 * count * depth * 128, 4 * (tokens.size + mine.size)),
    )(place, tokens, grads_in, mine, other)


def causal_of(count):
    rows = lax.broadcasted_iota(jnp.int32, (count, count), 0)
    return rows >= lax.broadcasted_iota(jnp.int32, (count, count), 1)


def scores_kernel(q_ref, k_ref, v_ref, scores_ref, intra_ref):
    scores = contract(q_ref[...], k_ref[...], 1, 1)
    scores = jnp.where(causal_of(scores.shape[0]), scores, 0.0).astype(BF16)
    scores_ref[...] = scores
    intra_ref[...] = contract(scores, v_ref[...], 1, 0)


def inner_scores(queries, keys, values):
    count = queries.shape[0]
    return pl.pallas_call(
        scores_kernel,
        out_shape=[
            jax.ShapeDtypeStruct((count, count), BF16),
            jax.ShapeDtypeStruct((count, 128), F32),
        ],
        in_specs=[VMEM] * 3,
        out_specs=[VMEM] * 2,
        compiler_params=pltpu.CompilerParams(vmem_limit_bytes=LIMIT),
        cost_estimate=cost(4 * count * count * 128, 8 * count * 128),
    )(queries, keys, values)


def grad_kernel(q_ref, intra_ref, prior_ref, hg_ref, gain_ref, attn_ref, state_ref):
    queries = q_ref[...]
    attended = intra_ref[...] + contract(queries, prior_ref[...], 1, 0)
    inv_rms = lax.rsqrt(jnp.mean(attended * attended, axis=-1, keepdims=True) + 1e-06)
    scaled = gain_ref[...] * hg_ref[...]
    mean = jnp.mean(attended * scaled, axis=-1, keepdims=True)
    attn_grad = inv_rms * scaled - attended * (inv_rms * inv_rms * inv_rms) * mean
    attn_grad = attn_grad.astype(BF16)
    attn_ref[...] = attn_grad
    state_ref[...] = contract(queries, attn_grad, 0, 0).astype(BF16)


def attention_grad(queries, intra, prior, head_grad, gain):
    count = queries.shape[0]
    return pl.pallas_call(
        grad_kernel,
        out_shape=[
            jax.ShapeDtypeStruct((count, 128), BF16),
            jax.ShapeDtypeStruct((128, 128), BF16),
        ],
        in_specs=[VMEM] * 5,
        out_specs=[VMEM] * 2,
        compiler_params=pltpu.CompilerParams(vmem_limit_bytes=LIMIT),
        cost_estimate=cost(4 * count * 128 * 128, 16 * count * 128),
    )(queries, intra, prior, head_grad, gain)


def inner_kernel(q_ref, k_ref, v_ref, scores_ref, attn_ref, prior_ref, dq_ref, dk_ref, dv_ref):
    attn_grad = attn_ref[...]
    prob = contract(attn_grad, v_ref[...], 1, 1)
    prob = jnp.where(causal_of(prob.shape[0]), prob, 0.0).astype(BF16)
    dq_ref[...] = contract(prob, k_ref[...], 1, 0) + contract(attn_grad, prior_ref[...], 1, 1)
    dk_ref[...] = contract(prob, q_ref[...], 0, 0)
    dv_ref[...] = contract(scores_ref[...], attn_grad, 0, 0)


def inner_grads(queries, keys, values, scores, attn_grad, prior):
    count = queries.shape[0]
    row = jax.ShapeDtypeStruct((count, 128), F32)
    return pl.pallas_call(
        inner_kernel,
        out_shape=[row] * 3,
        in_specs=[VMEM] * 6,
        out_specs=[VMEM] * 3,
        compiler_params=pltpu.CompilerParams(vmem_limit_bytes=LIMIT),
        cost_estimate=cost(10 * count * count * 128, 20 * count * 128),
    )(queries, keys, values, scores, attn_grad, prior)


def output_kernel(
    place_ref, dq, dk, dv, k_ref, v_ref, later, q0, q1, kv_mine, kv_other, out_ref, joined
):
    first = place_ref[1] == 0

    @pl.when(pl.program_id(0) == 0)
    def _():
        key_grad = (dk[...] + contract(v_ref[...], later[...], 1, 1)).astype(BF16)
        value_grad = (dv[...] + contract(k_ref[...], later[...], 1, 0)).astype(BF16)
        joined[0] = dq[...].astype(BF16)
        joined[1] = jnp.where(first, key_grad, value_grad)
        joined[2] = jnp.where(first, value_grad, key_grad)

    w_query = jnp.where(first, q0[...].reshape(-1, 128), q1[...].reshape(-1, 128))
    total = contract(joined[0], w_query, 1, 1)
    total += contract(joined[1], kv_mine[...].reshape(-1, 128), 1, 1)
    total += contract(joined[2], kv_other[...].reshape(-1, 128), 1, 1)
    out_ref[...] = total.astype(BF16)


def output(place, dq, dk, dv, keys, values, later, qo_mine, qo_other, kv_mine, kv_other):
    count = dq.shape[0]
    xs, steps, rows, _ = qo_mine.shape
    depth = xs * steps * rows
    weight = pl.BlockSpec((xs, 1, rows, 128), lambda i, s: (0, i, 0, 0))
    on_first = pl.BlockSpec((xs, 1, rows, 128), lambda i, s: (0, i * (1 - s[1]), 0, 0))
    on_second = pl.BlockSpec((xs, 1, rows, 128), lambda i, s: (0, i * s[1], 0, 0))
    row = pl.BlockSpec((count, 128), lambda i, s: (0, 0))
    square = pl.BlockSpec((128, 128), lambda i, s: (0, 0))
    return pl.pallas_call(
        output_kernel,
        out_shape=jax.ShapeDtypeStruct((count, depth), BF16),
        grid_spec=pltpu.PrefetchScalarGridSpec(
            num_scalar_prefetch=1,
            grid=(steps,),
            in_specs=[row] * 5 + [square, on_first, on_second, weight, weight],
            out_specs=pl.BlockSpec((count, depth // steps), lambda i, s: (0, i)),
            scratch_shapes=[pltpu.VMEM((3, count, 128), BF16)],
        ),
        compiler_params=pltpu.CompilerParams(vmem_limit_bytes=LIMIT),
        cost_estimate=cost(6 * count * depth * 128, 2 * (3 * depth * 128 + count * depth)),
    )(place, dq, dk, dv, keys, values, later, qo_mine, qo_other, kv_mine, kv_other)


def deal(local):
    head = local.shape[0]
    peers = lax.axis_size(SEQ)
    pieces = local.reshape(peers, head // peers, head)
    return lax.all_to_all(pieces, SEQ, 0, 0, tiled=True)


def other_blocks(pieces, reverse):
    peers, _, head = pieces.shape
    pieces = pieces.reshape(peers, -1)
    to = lax.broadcasted_iota(jnp.int32, (peers, peers), 0)
    frm = lax.broadcasted_iota(jnp.int32, (peers, peers), 1)
    mask = ((frm > to) if reverse else (frm < to)).astype(BF16)
    sums = contract(mask, pieces, 1, 0).astype(BF16)
    sums = lax.all_to_all(sums.reshape(peers, head // peers, head), SEQ, 0, 0, tiled=True)
    return sums.reshape(head, head)


def per_device(inputs, w_project, w_output, norm_gain, out_grad):
    tokens = inputs[0]
    grads_in = out_grad[0]
    head = w_output.shape[1]
    dps, xs = lax.axis_size("dp"), lax.axis_size("x")
    place = jnp.stack([lax.axis_index("x"), lax.axis_index("core")]).astype(jnp.int32)

    to_first = jnp.concatenate([w_project[:, 1], w_project[:, 0]], axis=1)
    to_second = jnp.concatenate([w_project[:, 2], w_output], axis=1)
    pair = lax.all_to_all(jnp.stack([to_first, to_second]), "core", 0, 0, tiled=True)
    plane = spread(pair.reshape(-1, 2 * head), ROWS).reshape(-1, 2 * head)
    kv_plane, qo_plane = plane[:, :head], plane[:, head:]

    pieces = split_columns(place, tokens, dps)
    moved = [pieces[0]]
    for k in range(1, xs):
        moved.append(lax.ppermute(pieces[k], "x", [(i, (i + k) % xs) for i in range(xs)]))
    kv_near = after(kv_plane, pieces[0])
    kv_far = core_swap(kv_near)
    sums = partial_sums(place, moved, kv_near, kv_far, dps)
    qo_plane = after(qo_plane, sums)
    sums = lax.all_to_all(sums, "x", 0, 0, tiled=True)
    keys, values, local_state = keys_values_state(place, sums)
    state_pieces = deal(local_state)
    kv_plane = after(kv_plane, state_pieces)
    prior_state = other_blocks(state_pieces, False)

    def whole(block):
        return lax.all_gather(block, "x").reshape(xs, dps, -1, head)

    qo_mine = after(whole(qo_plane), state_pieces)
    qo_other = core_swap(qo_mine)

    queries, head_grad = queries_head_grad(place, tokens, grads_in, qo_mine, qo_other)
    scores, intra = inner_scores(queries, keys, values)
    attn_grad, local_grad = attention_grad(
        queries, intra, prior_state, head_grad, norm_gain.reshape(1, head)
    )
    grad_pieces = deal(local_grad)
    kv_mine = after(whole(kv_plane), grad_pieces)
    kv_other = core_swap(kv_mine)
    later_state = other_blocks(grad_pieces, True)
    grads = inner_grads(queries, keys, values, scores, attn_grad, prior_state)
    result = output(
        place, *grads, keys, values, later_state, qo_mine, qo_other, kv_mine, kv_other
    )
    return result[None]


def solution(mesh):
    split = Mesh(mesh.devices.reshape(mesh.shape["dp"], 4, 8, 2), DP_SEQ)
    in_specs = (P("dp", SEQ, None), P(DP_SEQ, None, None), P(DP_SEQ, None), P(), P("dp", SEQ, None))
    out_specs = P("dp", SEQ, None)
    return jax.shard_map(
        per_device, mesh=split, in_specs=in_specs, out_specs=out_specs, check_vma=False
    )
```

time: 197 us -> 171 us (0.87)
  blocking collectives: 77.4 us -> 37.7 us
  matrix products: 27.6 us -> 0.26 us
  Pallas kernels: 0 us -> 15.6 us
  starting transfers between devices: 39.9 us -> 55.4 us
  between operations: 0.26 us -> 13.6 us
  local copies, waits for them, and re-layouts: 6.08 us -> 16.4 us
  waiting for transfers between devices: 40.3 us -> 30.4 us
  other arithmetic: 4.56 us -> 0.79 us
    all_to_all x3 -> x2, blocking collectives: 67.1 us -> 27.4 us  [the longest x1 17.3 us: deal(): return lax.all_to_all(pieces, SEQ, 0, 0, tiled=True)]
    dot_general x18 -> x2, matrix products: 27.6 us -> 0.26 us  [contract(): lax.dot_general(left, right, (((left_dim,), (right_dim,)), ((), ())), pre...]
    pallas_call x0 -> x8, Pallas kernels: none -> 15.6 us  [the longest x1 5.51 us: output(): pl.pallas_call(output_kernel, out_shape=jax.ShapeDtypeStruct((count, dept...]
    unnamed x11 -> x29, local copies, waits for them, and re-layouts: 0.68 us -> 11.4 us
    ppermute x0 -> x3, starting transfers between devices: none -> 10.5 us  [per_device(): lax.ppermute(pieces[k], 'x', [(i, (i + k) % xs) for i in range(xs)])]
    all_to_all x2, waiting for transfers between devices: 16.3 us -> 7.57 us  [other_blocks(): lax.all_to_all(sums.reshape(peers, head // peers, head), SEQ, 0, 0, tiled...]
    all_to_all x1, starting transfers between devices: 4.35 us -> 11.2 us  [spread(): lax.all_to_all(jnp.broadcast_to(block[None], (peers, *block.shape)), axes...]
    all_to_all x2 -> x1, waiting for transfers between devices: 14.5 us -> 8.34 us  [deal(): return lax.all_to_all(pieces, SEQ, 0, 0, tiled=True)]
  transfers between devices with their start and end apart: 7 -> 12, of which waited for: 6 -> 6; matrix products, arithmetic and copies ran while one was open for 5% -> 2% of each run, Pallas kernels for 0% -> 5%
where the time goes in v2:
time: 171 us; the launch traced here: 170 us
  starting transfers between devices  55.4 us (32%)
  blocking collectives  37.7 us (22%)
  waiting for transfers between devices  30.4 us (18%)
  local copies, waits for them, and re-layouts  16.4 us (10%)
  Pallas kernels  15.6 us (9%)
  between operations  13.6 us (8%)
    all_to_all x1, blocking collectives, deal(): return lax.all_to_all(pieces, SEQ, 0, 0, tiled=True)  17.3 us
    all_to_all x2, starting transfers between devices, other_blocks(): lax.all_to_all(sums.reshape(peers, head // peers, head), SEQ, 0, 0, tiled...  13.4 us
    unnamed x29, local copies, waits for them, and re-layouts  11.4 us
    all_to_all x1, starting transfers between devices, spread(): lax.all_to_all(jnp.broadcast_to(block[None], (peers, *block.shape)), axes...  11.2 us
    ppermute x3, starting transfers between devices, per_device(): lax.ppermute(pieces[k], 'x', [(i, (i + k) % xs) for i in range(xs)])  10.5 us
    all_to_all x1, starting transfers between devices, deal(): return lax.all_to_all(pieces, SEQ, 0, 0, tiled=True)  10.3 us
    all_to_all x1, blocking collectives, per_device(): lax.all_to_all(jnp.stack([to_first, to_second]), 'core', 0, 0, tiled=True)  10.3 us
    all_to_all x1, blocking collectives, per_device(): sums = lax.all_to_all(sums, 'x', 0, 0, tiled=True)  10.1 us
  transfers between devices with their start and end apart: 12, of which 6 were waited for; matrix products, arithmetic and copies ran while one was open for 2% of the time, Pallas kernels for 5%

profile of v2, /device:TPU:1, one launch (start us, length us, event | category | flops | bytes accessed | tf_op | source)
XLA Modules:
  0.0 170.1 jit_solution(12446172022846859553)
XLA Ops:
  8.2 10.3 %all_to_all.35 = bf16[2,12,256]{2,1,0:T(8,128)(2,1)S(1)} all-to-all(bf16[2,12,256]{2,1,0:T(8,128)(2,1)S(1)} %pad_maximum_fusion), channel_id=1, replica_groups=mesh['dp'=8,'x'=4,'z'=8,'core'=2] {'core'}, dimensions={0} | all-to-all | bytes 24576 | tf_op jit(solution)/shard_map/all_to_all | solution.py:340
  19.4 11.2 %all-to-all-start.1 = ((bf16[64,24,256]{2,1,0:T(8,128)(2,1)}), bf16[64,24,256]{2,1,0:T(8,128)(2,1)}, u32[]{:S(2)}, u32[]{:S(2)}) async-start(bf16[64,24,256]{2,1,0:T(8,128)(2,1)} %broadcast_in_dim.11), calls=%async_computation.1 | async-start | bytes 1572864 | tf_op jit(solution)/shard_map/all_to_all | solution.py:33
  30.7 2.3 %shard_map.55 = (bf16[136,1536]{1,0:T(8,128)(2,1)S(1)}, bf16[136,1536]{1,0:T(8,128)(2,1)}, bf16[136,1536]{1,0:T(8,128)(2,1)}, bf16[136,1536]{1,0:T(8,128)(2,1)}) custom-call(s32[2]{0:T(128)S(1)} %pad_add_fusion.place_ref, bf16[136,6144]{1,0:T(8,128)(2,1)S(1)} %bitcast.32), custom_call_target="tpu_custom_call" | custom-call | bytes 3342336 | tf_op jit(solution)/shard_map/pallas_call | solution.py:81
  33.0 3.1 %collective-permute-start = (bf16[136,1536]{1,0:T(8,128)(2,1)}, bf16[136,1536]{1,0:T(8,128)(2,1)S(1)}, u32[]{:S(2)}, u32[]{:S(2)}) collective-permute-start(bf16[136,1536]{1,0:T(8,128)(2,1)} %get-tuple-element.27), channel_id=1, source_target_pairs={{0,16},{16,32},{32,48},{48,0},{1,17},{17,33},{33,49},{49,1},{2,18}... | collective-permute-start | bytes 1253384 | tf_op jit(solution)/shard_map/ppermute | solution.py:347
  36.1 4.4 %collective-permute-start.1 = (bf16[136,1536]{1,0:T(8,128)(2,1)}, bf16[136,1536]{1,0:T(8,128)(2,1)}, u32[]{:S(2)}, u32[]{:S(2)}) collective-permute-start(bf16[136,1536]{1,0:T(8,128)(2,1)} %get-tuple-element.28), channel_id=1, source_target_pairs={{0,32},{16,48},{32,0},{48,16},{1,33},{17,49},{33,1},{49,17},{2,34}... | collective-permute-start | bytes 1253384 | tf_op jit(solution)/shard_map/ppermute | solution.py:347
  40.5 3.1 %collective-permute-start.2 = (bf16[136,1536]{1,0:T(8,128)(2,1)}, bf16[136,1536]{1,0:T(8,128)(2,1)}, u32[]{:S(2)}, u32[]{:S(2)}) collective-permute-start(bf16[136,1536]{1,0:T(8,128)(2,1)} %get-tuple-element.29), channel_id=1, source_target_pairs={{0,48},{16,0},{32,16},{48,32},{1,49},{17,1},{33,17},{49,33},{2,50}... | collective-permute-start | bytes 1253384 | tf_op jit(solution)/shard_map/ppermute | solution.py:347
  43.5 8.5 %all-to-all-done.1 = bf16[64,24,256]{2,1,0:T(8,128)(2,1)} async-done(((bf16[64,24,256]{2,1,0:T(8,128)(2,1)}), bf16[64,24,256]{2,1,0:T(8,128)(2,1)}, u32[]{:S(2)}, u32[]{:S(2)}) %all-to-all-start.1) | async-done | bytes 786464 | tf_op jit(solution)/shard_map/all_to_all | solution.py:33
  52.0 1.9 %fusion.4 = (bf16[1536,128]{1,0:T(8,128)(2,1)S(1)}, bf16[1536,128]{1,0:T(8,128)(2,1)}) fusion(bf16[1536,256]{1,0:T(8,128)(2,1)} %bitcast.9), kind=kLoop, calls=%fused_computation.15 | loop fusion | bytes 1572864 | tf_op jit(solution)/shard_map/slice | solution.py:342
  53.9 4.8 %collective-permute-start.3 = (bf16[1536,128]{1,0:T(8,128)(2,1)S(1)}, bf16[1536,128]{1,0:T(8,128)(2,1)S(1)}, u32[]{:S(2)}, u32[]{:S(2)}) collective-permute-start(bf16[1536,128]{1,0:T(8,128)(2,1)S(1)} %get-tuple-element.45.mine_ref), channel_id=1, source_target_pairs={{0,1},{1,0},{2,3},{3,2},{4,5},{5,4},{6,7},{7,6},{8,9},{9,8},{10,11... | collective-permute-start | bytes 1179656 | tf_op jit(solution)/shard_map/ppermute | solution.py:43
  60.1 1.8 %shard_map.56 = bf16[4,136,256]{2,1,0:T(8,128)(2,1)S(1)} custom-call(s32[2]{0:T(128)S(1)} %pad_add_fusion.place_ref, bf16[136,1536]{1,0:T(8,128)(2,1)S(1)} %get-tuple-element.26.t0, bf16[136,1536]{1,0:T(8,128)(2,1)S(1)} %collective-permute-done.t1, bf16[136,1536]{1,0:T(8,128)(2,1)} %collective-permute-done.1.t2, ...), custom_call_target="tpu_custom_call" | custom-call | flops 427819008 | bytes 2457600 | tf_op jit(solution)/shard_map/pallas_call | solution.py:112
  61.9 10.1 %all_to_all.36.parts_ref = bf16[4,136,256]{2,1,0:T(8,128)(2,1)S(1)} all-to-all(bf16[4,136,256]{2,1,0:T(8,128)(2,1)S(1)} %shard_map.56), channel_id=1, replica_groups=mesh['dp'=8,'x'=4,'z'=8,'core'=2] {'x'}, dimensions={0} | all-to-all | bytes 557056 | tf_op jit(solution)/shard_map/all_to_all | solution.py:352
  72.8 17.3 %all_to_all.37 = bf16[64,2,128]{2,1,0:T(2,128)(2,1)S(1)} all-to-all(bf16[64,2,128]{2,1,0:T(2,128)(2,1)S(1)} %bitcast.43), channel_id=1, replica_groups=mesh['dp'=8,'x'=4,'z'=8,'core'=2] {'x','z','core'}, dimensions={0} | all-to-all | bytes 65536 | tf_op jit(solution)/shard_map/all_to_all | solution.py:317
  90.1 3.7 %all-gather.5.cloned.1.call-done = bf16[6144,128]{1,0:T(8,128)(2,1)} async-done(((bf16[1536,128]{1,0:T(8,128)(2,1)}), bf16[6144,128]{1,0:T(8,128)(2,1)}) %all-gather.5.cloned.1.call-update) | async-done | bytes 1572880 | tf_op jit(solution)/shard_map/all_gather | solution.py:359
  93.9 2.6 %collective-permute-start.4 = (bf16[4,8,192,128]{3,2,1,0:T(8,128)(2,1)}, bf16[4,8,192,128]{3,2,1,0:T(8,128)(2,1)S(1)}, u32[]{:S(2)}, u32[]{:S(2)}) collective-permute-start(bf16[4,8,192,128]{3,2,1,0:T(8,128)(2,1)} %bitcast.34), channel_id=1, source_target_pairs={{0,1},{1,0},{2,3},{3,2},{4,5},{5,4},{6,7},{7,6},{8,9},{9,8},{10,11... | collective-permute-start | bytes 4718600 | tf_op jit(solution)/shard_map/ppermute | solution.py:43
  97.2 9.3 %all-to-all-start.4 = ((bf16[64,2,128]{2,1,0:T(2,128)(2,1)}), bf16[64,2,128]{2,1,0:T(2,128)(2,1)S(1)}, u32[]{:S(2)}, u32[]{:S(2)}) async-start(bf16[64,2,128]{2,1,0:T(2,128)(2,1)} %reshape.41), calls=%async_computation.4 | async-start | bytes 65536 | tf_op jit(solution)/shard_map/all_to_all | solution.py:327
  109.1 1.4 copy-done.4
  110.5 1.5 copy-done.7
  112.1 3.4 %shard_map.58 = (bf16[136,128]{1,0:T(8,128)(2,1)S(1)}, f32[136,128]{1,0:T(8,128)S(1)}) custom-call(s32[2]{0:T(128)S(1)} %pad_add_fusion.place_ref, bf16[136,6144]{1,0:T(8,128)(2,1)S(1)} %bitcast.33, bf16[136,6144]{1,0:T(8,128)(2,1)S(1)} %bitcast.37, bf16[4,8,192,128]{3,2,1,0:T(8,128)(2,1)S(1)} %bitcast.35, bf16[4,8,192,128]{3,2,1,0:T(8,128)(2,1)S(1)} %copy-done.4), custom_call_target="tpu_custom_call" | custom-call | flops 427819008 | bytes 6488064 | tf_op jit(solution)/shard_map/pallas_call | solution.py:178
  116.8 10.3 %all-to-all-start.5 = ((bf16[64,2,128]{2,1,0:T(2,128)(2,1)}), bf16[64,2,128]{2,1,0:T(2,128)(2,1)S(1)}, u32[]{:S(2)}, u32[]{:S(2)}) async-start(bf16[64,2,128]{2,1,0:T(2,128)(2,1)} %bitcast.14), calls=%async_computation.5 | async-start | bytes 65536 | tf_op jit(solution)/shard_map/all_to_all | solution.py:317
  128.1 8.3 %all-to-all-done.5 = bf16[64,2,128]{2,1,0:T(2,128)(2,1)S(1)} async-done(((bf16[64,2,128]{2,1,0:T(2,128)(2,1)}), bf16[64,2,128]{2,1,0:T(2,128)(2,1)S(1)}, u32[]{:S(2)}, u32[]{:S(2)}) %all-to-all-start.5) | async-done | bytes 32800 | tf_op jit(solution)/shard_map/all_to_all | solution.py:317
  136.4 2.6 %collective-permute-start.5 = (bf16[4,8,192,128]{3,2,1,0:T(8,128)(2,1)}, bf16[4,8,192,128]{3,2,1,0:T(8,128)(2,1)S(1)}, u32[]{:S(2)}, u32[]{:S(2)}) collective-permute-start(bf16[4,8,192,128]{3,2,1,0:T(8,128)(2,1)} %bitcast.38), channel_id=1, source_target_pairs={{0,1},{1,0},{2,3},{3,2},{4,5},{5,4},{6,7},{7,6},{8,9},{9,8},{10,11... | collective-permute-start | bytes 4718600 | tf_op jit(solution)/shard_map/ppermute | solution.py:43
  139.7 4.2 %all-to-all-start.6 = ((bf16[64,2,128]{2,1,0:T(2,128)(2,1)}), bf16[64,2,128]{2,1,0:T(2,128)(2,1)S(1)}, u32[]{:S(2)}, u32[]{:S(2)}) async-start(bf16[64,2,128]{2,1,0:T(2,128)(2,1)} %reshape.46), calls=%async_computation.6 | async-start | bytes 65536 | tf_op jit(solution)/shard_map/all_to_all | solution.py:327
  145.6 7.6 %all-to-all-done.6 = bf16[64,2,128]{2,1,0:T(2,128)(2,1)S(1)} async-done(((bf16[64,2,128]{2,1,0:T(2,128)(2,1)}), bf16[64,2,128]{2,1,0:T(2,128)(2,1)S(1)}, u32[]{:S(2)}, u32[]{:S(2)}) %all-to-all-start.6) | async-done | bytes 32800 | tf_op jit(solution)/shard_map/all_to_all | solution.py:327
  157.8 5.5 %shard_map.62 = bf16[136,6144]{1,0:T(8,128)(2,1)} custom-call(s32[2]{0:T(128)S(1)} %pad_add_fusion.place_ref, f32[136,128]{1,0:T(8,128)S(1)} %get-tuple-element.41.dq, f32[136,128]{1,0:T(8,128)S(1)} %copy-done.10, f32[136,128]{1,0:T(8,128)S(1)} %copy-done.12, bf16[136,128]{1,0:T(8,128)(2,1)S(1)} %get-tuple-element.35.k_ref, ...), custom_call_target="tpu_custom_call" | custom-call | flops 641728512 | bytes 6389760 | tf_op jit(solution)/shard_map/pallas_call | solution.py:298
  (55 shorter events, 17.4 us)
Async XLA Ops:
  6.5 24.1 %copy-start = (bf16[1,136,6144]{2,1,0:T(8,128)(2,1)S(1)}, bf16[1,136,6144]{2,1,0:T(8,128)(2,1)}, u32[]{:S(2)}) copy-start(bf16[1,136,6144]{2,1,0:T(8,128)(2,1)} %param.5) | copy-start | bytes 5013508
  19.4 32.6 %all-to-all-start.1 = ((bf16[64,24,256]{2,1,0:T(8,128)(2,1)}), bf16[64,24,256]{2,1,0:T(8,128)(2,1)}, u32[]{:S(2)}, u32[]{:S(2)}) async-start(bf16[64,24,256]{2,1,0:T(8,128)(2,1)} %broadcast_in_dim.11), calls=%async_computation.1 | async-start | bytes 1572864 | tf_op jit(solution)/shard_map/all_to_all | solution.py:33
  30.5 63.3 %all-gather.5.cloned.1.call-start = ((), (), s32[]{:S(2)}) async-start(), calls=%async_computation.7 | async-start | bytes 1966080 | tf_op jit(solution)/shard_map/all_gather | solution.py:359
  33.0 25.7 %collective-permute-start = (bf16[136,1536]{1,0:T(8,128)(2,1)}, bf16[136,1536]{1,0:T(8,128)(2,1)S(1)}, u32[]{:S(2)}, u32[]{:S(2)}) collective-permute-start(bf16[136,1536]{1,0:T(8,128)(2,1)} %get-tuple-element.27), channel_id=1, source_target_pairs={{0,16},{16,32},{32,48},{48,0},{1,17},{17,33},{33,49},{49,1},{2,18}... | collective-permute-start | bytes 1253384 | tf_op jit(solution)/shard_map/ppermute | solution.py:347
  36.1 22.6 %collective-permute-start.1 = (bf16[136,1536]{1,0:T(8,128)(2,1)}, bf16[136,1536]{1,0:T(8,128)(2,1)}, u32[]{:S(2)}, u32[]{:S(2)}) collective-permute-start(bf16[136,1536]{1,0:T(8,128)(2,1)} %get-tuple-element.28), channel_id=1, source_target_pairs={{0,32},{16,48},{32,0},{48,16},{1,33},{17,49},{33,1},{49,17},{2,34}... | collective-permute-start | bytes 1253384 | tf_op jit(solution)/shard_map/ppermute | solution.py:347
  40.5 18.3 %collective-permute-start.2 = (bf16[136,1536]{1,0:T(8,128)(2,1)}, bf16[136,1536]{1,0:T(8,128)(2,1)}, u32[]{:S(2)}, u32[]{:S(2)}) collective-permute-start(bf16[136,1536]{1,0:T(8,128)(2,1)} %get-tuple-element.29), channel_id=1, source_target_pairs={{0,48},{16,0},{32,16},{48,32},{1,49},{17,1},{33,17},{49,33},{2,50}... | collective-permute-start | bytes 1253384 | tf_op jit(solution)/shard_map/ppermute | solution.py:347
  53.9 18.1 %copy-start.6 = (bf16[1536,128]{1,0:T(8,128)(2,1)}, bf16[1536,128]{1,0:T(8,128)(2,1)S(1)}, u32[]{:S(2)}) copy-start(bf16[1536,128]{1,0:T(8,128)(2,1)S(1)} %get-tuple-element.45.mine_ref) | copy-start | bytes 1179652
  53.9 6.2 %collective-permute-start.3 = (bf16[1536,128]{1,0:T(8,128)(2,1)S(1)}, bf16[1536,128]{1,0:T(8,128)(2,1)S(1)}, u32[]{:S(2)}, u32[]{:S(2)}) collective-permute-start(bf16[1536,128]{1,0:T(8,128)(2,1)S(1)} %get-tuple-element.45.mine_ref), channel_id=1, source_target_pairs={{0,1},{1,0},{2,3},{3,2},{4,5},{5,4},{6,7},{7,6},{8,9},{9,8},{10,11... | collective-permute-start | bytes 1179656 | tf_op jit(solution)/shard_map/ppermute | solution.py:43
  61.9 66.2 %all-gather.7.cloned.1.call-start = ((), (), s32[]{:S(2)}) async-start(), calls=%async_computation.8 | async-start | bytes 1966080 | tf_op jit(solution)/shard_map/all_gather | solution.py:359
  93.9 12.6 %collective-permute-start.4 = (bf16[4,8,192,128]{3,2,1,0:T(8,128)(2,1)}, bf16[4,8,192,128]{3,2,1,0:T(8,128)(2,1)S(1)}, u32[]{:S(2)}, u32[]{:S(2)}) collective-permute-start(bf16[4,8,192,128]{3,2,1,0:T(8,128)(2,1)} %bitcast.34), channel_id=1, source_target_pairs={{0,1},{1,0},{2,3},{3,2},{4,5},{5,4},{6,7},{7,6},{8,9},{9,8},{10,11... | collective-permute-start | bytes 4718600 | tf_op jit(solution)/shard_map/ppermute | solution.py:43
  97.2 18.6 %all-to-all-start.4 = ((bf16[64,2,128]{2,1,0:T(2,128)(2,1)}), bf16[64,2,128]{2,1,0:T(2,128)(2,1)S(1)}, u32[]{:S(2)}, u32[]{:S(2)}) async-start(bf16[64,2,128]{2,1,0:T(2,128)(2,1)} %reshape.41), calls=%async_computation.4 | async-start | bytes 65536 | tf_op jit(solution)/shard_map/all_to_all | solution.py:327
  106.5 1.1 copy-start.3
  107.7 1.4 copy-start.1
  109.1 1.4 copy-start.4
  110.5 1.5 copy-start.7
  112.1 3.8 %copy-start.13 = (f32[128]{0:T(128)S(1)}, f32[128]{0:T(128)}, u32[]{:S(2)}) copy-start(f32[128]{0:T(128)} %param.8) | copy-start | bytes 1540
  112.1 41.1 %copy-start.2 = (bf16[6144,128]{1,0:T(8,128)(2,1)S(1)}, bf16[6144,128]{1,0:T(8,128)(2,1)}, u32[]{:S(2)}) copy-start(bf16[6144,128]{1,0:T(8,128)(2,1)} %all-gather.5.cloned.1.call-done) | copy-start | bytes 4718596
  116.8 19.6 %all-to-all-start.5 = ((bf16[64,2,128]{2,1,0:T(2,128)(2,1)}), bf16[64,2,128]{2,1,0:T(2,128)(2,1)S(1)}, u32[]{:S(2)}, u32[]{:S(2)}) async-start(bf16[64,2,128]{2,1,0:T(2,128)(2,1)} %bitcast.14), calls=%async_computation.5 | async-start | bytes 65536 | tf_op jit(solution)/shard_map/all_to_all | solution.py:317
  136.4 16.8 %collective-permute-start.5 = (bf16[4,8,192,128]{3,2,1,0:T(8,128)(2,1)}, bf16[4,8,192,128]{3,2,1,0:T(8,128)(2,1)S(1)}, u32[]{:S(2)}, u32[]{:S(2)}) collective-permute-start(bf16[4,8,192,128]{3,2,1,0:T(8,128)(2,1)} %bitcast.38), channel_id=1, source_target_pairs={{0,1},{1,0},{2,3},{3,2},{4,5},{5,4},{6,7},{7,6},{8,9},{9,8},{10,11... | collective-permute-start | bytes 4718600 | tf_op jit(solution)/shard_map/ppermute | solution.py:43
  139.7 13.4 %all-to-all-start.6 = ((bf16[64,2,128]{2,1,0:T(2,128)(2,1)}), bf16[64,2,128]{2,1,0:T(2,128)(2,1)S(1)}, u32[]{:S(2)}, u32[]{:S(2)}) async-start(bf16[64,2,128]{2,1,0:T(2,128)(2,1)} %reshape.46), calls=%async_computation.6 | async-start | bytes 65536 | tf_op jit(solution)/shard_map/all_to_all | solution.py:327
  153.2 1.4 copy-start.5
  154.6 1.4 copy-start.8
  156.0 0.9 copy-start.10
  156.9 0.9 copy-start.12
  (2 other events, 1.3 us)
Sparse Core Ops, SparseCore 0:
  62.0 31.8 all-gather.4
  96.0 32.0 all-gather.6

commit v3 on v1

v3 whole, which is shorter than its diff:
```python
import functools

import jax
import jax.numpy as jnp
from jax import lax
from jax.experimental import pallas as pl
from jax.experimental.pallas import tpu as pltpu
from jax.sharding import Mesh
from jax.sharding import PartitionSpec as P

SEQ = ("x", "z", "core")
DP_SEQ = ("dp", "x", "z", "core")
ROWS = ("dp", "z")
BF16 = jnp.bfloat16
F32 = jnp.float32
LIMIT = 16 * 1024 * 1024
LONG = 30_000_000_000
SMEM = pl.BlockSpec(memory_space=pltpu.SMEM)
VMEM = pl.BlockSpec(memory_space=pltpu.VMEM)


def contract(left, right, left_dim, right_dim):
    return lax.dot_general(
        left, right, (((left_dim,), (right_dim,)), ((), ())), preferred_element_type=F32
    )


def cost(flops, moved):
    return pl.CostEstimate(flops=flops, bytes_accessed=moved, transcendentals=0)


def after(value, *events):
    return lax.optimization_barrier((value, *events))[0]


def core_swap(block):
    return lax.ppermute(block, "core", [(0, 1), (1, 0)])


def put_rows(parts, place_ref, blocks, out_ref):
    rows = blocks[0].shape[0] // parts
    for k, ref in enumerate(blocks):
        source = lax.rem(place_ref[0] - k + 4, 4)
        for p in range(parts):
            at = pl.multiple_of((p * 4 + source) * rows, 64)
            out_ref[pl.ds(at, rows), :] = ref[p * rows : (p + 1) * rows, :]


def project_kernel(parts, place_ref, *refs):
    tokens, blocks, (weight_ref, own_ref, send_ref) = refs[:-7], refs[-7:-3], refs[-3:]
    put_rows(parts, place_ref, blocks, weight_ref)

    def products(own, far):
        own_ref[...] = contract(own[...], weight_ref[...], 1, 0).astype(own_ref.dtype)
        send_ref[...] = contract(far[...], weight_ref[...], 1, 0).astype(send_ref.dtype)

    if len(tokens) == 2:
        products(*tokens)
    else:
        pl.when(place_ref[1] == 0)(lambda: products(*tokens[:2]))
        pl.when(place_ref[1] != 0)(lambda: products(*tokens[2:]))


def project(place, tokens, blocks, parts, dtype):
    count, depth = tokens[0].shape
    row = jax.ShapeDtypeStruct((count, 128), dtype)
    return pl.pallas_call(
        functools.partial(project_kernel, parts),
        out_shape=[jax.ShapeDtypeStruct((depth, 128), BF16), row, row],
        in_specs=[SMEM] + [VMEM] * (len(tokens) + 4),
        out_specs=[VMEM] * 3,
        compiler_params=pltpu.CompilerParams(vmem_limit_bytes=LIMIT),
        cost_estimate=cost(LONG, 4 * count * depth + 4 * depth * 128),
    )(place, *tokens, *blocks)


def state_kernel(place_ref, own_ref, recv_ref, key_ref, value_ref, state_ref):
    own, recv = own_ref[...], recv_ref[...]
    first = place_ref[1] == 0
    keys, values = jnp.where(first, own, recv), jnp.where(first, recv, own)
    key_ref[...] = keys
    value_ref[...] = values
    state_ref[...] = contract(keys, values, 0, 0).astype(BF16)


def keys_values_state(place, own, recv):
    row = jax.ShapeDtypeStruct(own.shape, BF16)
    return pl.pallas_call(
        state_kernel,
        out_shape=[row, row, jax.ShapeDtypeStruct((128, 128), BF16)],
        in_specs=[SMEM] + [VMEM] * 2,
        out_specs=[VMEM] * 3,
        compiler_params=pltpu.CompilerParams(vmem_limit_bytes=LIMIT),
        cost_estimate=cost(2 * own.size * 128, 8 * own.size),
    )(place, own, recv)


def gate_kernel(in_ref, out_ref):
    out_ref[...] = in_ref[...]


def gate(value):
    return pl.pallas_call(
        gate_kernel,
        out_shape=jax.ShapeDtypeStruct(value.shape, value.dtype),
        in_specs=[VMEM],
        out_specs=VMEM,
        compiler_params=pltpu.CompilerParams(vmem_limit_bytes=LIMIT),
        cost_estimate=cost(LONG, 4 * value.size),
    )(value)


def causal_of(count):
    rows = lax.broadcasted_iota(jnp.int32, (count, count), 0)
    return rows >= lax.broadcasted_iota(jnp.int32, (count, count), 1)


def grad_kernel(
    place_ref, near_ref, far_ref, k_ref, v_ref, prior_ref, gain_ref,
    q_ref, scores_ref, attn_ref, state_ref,
):
    first = place_ref[1] == 0
    near, far = near_ref[...], far_ref[...]
    queries = jnp.where(first, near, far).astype(BF16)
    head_grad = jnp.where(first, far, near)
    q_ref[...] = queries
    scores = contract(queries, k_ref[...], 1, 1)
    scores = jnp.where(causal_of(scores.shape[0]), scores, 0.0).astype(BF16)
    scores_ref[...] = scores
    attended = contract(scores, v_ref[...], 1, 0) + contract(queries, prior_ref[...], 1, 0)
    inv_rms = lax.rsqrt(jnp.mean(attended * attended, axis=-1, keepdims=True) + 1e-06)
    scaled = gain_ref[...] * head_grad
    mean = jnp.mean(attended * scaled, axis=-1, keepdims=True)
    attn_grad = inv_rms * scaled - attended * (inv_rms * inv_rms * inv_rms) * mean
    attn_grad = attn_grad.astype(BF16)
    attn_ref[...] = attn_grad
    state_ref[...] = contract(queries, attn_grad, 0, 0).astype(BF16)


def attention_grad(place, near, far, keys, values, prior, gain):
    count = keys.shape[0]
    row = jax.ShapeDtypeStruct((count, 128), BF16)
    return pl.pallas_call(
        grad_kernel,
        out_shape=[
            row,
            jax.ShapeDtypeStruct((count, count), BF16),
            row,
            jax.ShapeDtypeStruct((128, 128), BF16),
        ],
        in_specs=[SMEM] + [VMEM] * 6,
        out_specs=[VMEM] * 4,
        compiler_params=pltpu.CompilerParams(vmem_limit_bytes=LIMIT),
        cost_estimate=cost(LONG, 16 * count * 128),
    )(place, near, far, keys, values, prior, gain)


def inner_kernel(
    place_ref, q_ref, k_ref, v_ref, scores_ref, attn_ref, prior_ref, near_ref, far_ref,
    base_ref, dk_ref, dv_ref, dq,
):
    @pl.when(pl.program_id(0) == 0)
    def _():
        attn_grad = attn_ref[...]
        prob = contract(attn_grad, v_ref[...], 1, 1)
        prob = jnp.where(causal_of(prob.shape[0]), prob, 0.0).astype(BF16)
        query_grad = contract(prob, k_ref[...], 1, 0) + contract(attn_grad, prior_ref[...], 1, 1)
        dq[...] = query_grad.astype(BF16)
        dk_ref[...] = contract(prob, q_ref[...], 0, 0)
        dv_ref[...] = contract(scores_ref[...], attn_grad, 0, 0)

    weight = jnp.where(place_ref[1] == 0, near_ref[...], far_ref[...])
    base_ref[...] = contract(dq[...], weight, 1, 1)


def inner_grads(place, queries, keys, values, scores, attn_grad, prior, near, far):
    count, depth, steps = queries.shape[0], near.shape[0], 4
    row = pl.BlockSpec((count, 128), lambda i: (0, 0))
    square = pl.BlockSpec((128, 128), lambda i: (0, 0))
    inner = pl.BlockSpec((count, count), lambda i: (0, 0))
    weight = pl.BlockSpec((depth // steps, 128), lambda i: (i, 0))
    return pl.pallas_call(
        inner_kernel,
        grid=(steps,),
        out_shape=[
            jax.ShapeDtypeStruct((count, depth), F32),
            jax.ShapeDtypeStruct((count, 128), F32),
            jax.ShapeDtypeStruct((count, 128), F32),
        ],
        in_specs=[SMEM, row, row, row, inner, row, square, weight, weight],
        out_specs=[pl.BlockSpec((count, depth // steps), lambda i: (0, i)), row, row],
        scratch_shapes=[pltpu.VMEM((count, 128), BF16)],
        compiler_params=pltpu.CompilerParams(vmem_limit_bytes=LIMIT),
        cost_estimate=cost(2 * count * depth * 128, 4 * count * depth + 4 * depth * 128),
    )(place, queries, keys, values, scores, attn_grad, prior, near, far)


def output_kernel(place_ref, base, dk, dv, k_ref, v_ref, later, near_ref, far_ref, out_ref, joined):
    @pl.when(pl.program_id(0) == 0)
    def _():
        first = place_ref[1] == 0
        key_grad = (dk[...] + contract(v_ref[...], later[...], 1, 1)).astype(BF16)
        value_grad = (dv[...] + contract(k_ref[...], later[...], 1, 0)).astype(BF16)
        joined[:, :128] = jnp.where(first, key_grad, value_grad)
        joined[:, 128:] = jnp.where(first, value_grad, key_grad)

    weight = jnp.concatenate([near_ref[...], far_ref[...]], axis=1)
    total = base[...] + contract(joined[...], weight, 1, 1)
    out_ref[...] = total.astype(BF16)


def output(place, base, dk, dv, keys, values, later, near, far):
    count, depth = base.shape
    steps = 4
    row = pl.BlockSpec((count, 128), lambda i: (0, 0))
    square = pl.BlockSpec((128, 128), lambda i: (0, 0))
    wide = pl.BlockSpec((count, depth // steps), lambda i: (0, i))
    weight = pl.BlockSpec((depth // steps, 128), lambda i: (i, 0))
    return pl.pallas_call(
        output_kernel,
        grid=(steps,),
        out_shape=jax.ShapeDtypeStruct((count, depth), BF16),
        in_specs=[SMEM, wide, row, row, row, row, square, weight, weight],
        out_specs=wide,
        scratch_shapes=[pltpu.VMEM((count, 256), BF16)],
        compiler_params=pltpu.CompilerParams(vmem_limit_bytes=LIMIT),
        cost_estimate=cost(4 * count * depth * 128, 4 * depth * 128 + 6 * count * depth),
    )(place, base, dk, dv, keys, values, later, near, far)


def sums_kernel(reverse, in_ref, out_ref):
    each = in_ref.shape[0] // 64
    to = lax.broadcasted_iota(jnp.int32, (128, 128), 0)
    frm = lax.broadcasted_iota(jnp.int32, (128, 128), 1)
    others = (frm // each > to // each) if reverse else (frm // each < to // each)
    mask = jnp.where(others & (frm % each == to % each), 1.0, 0.0).astype(BF16)
    out_ref[...] = contract(mask, in_ref[...], 1, 0).astype(BF16)


def sums_of(pieces, reverse):
    return pl.pallas_call(
        functools.partial(sums_kernel, reverse),
        out_shape=jax.ShapeDtypeStruct(pieces.shape, BF16),
        in_specs=[VMEM],
        out_specs=VMEM,
        compiler_params=pltpu.CompilerParams(vmem_limit_bytes=LIMIT),
        cost_estimate=cost(LONG, 4 * pieces.size),
    )(pieces)


def exchange(state):
    peers, head = lax.axis_size(SEQ), state.shape[1]
    pieces = state.reshape(peers, -1, head)
    return lax.all_to_all(pieces, SEQ, 0, 0, tiled=True).reshape(state.shape)


def per_device(inputs, w_project, w_output, norm_gain, out_grad):
    tokens = inputs[0]
    grads_in = out_grad[0]
    head = w_output.shape[1]
    dps, zs, xs = lax.axis_size("dp"), lax.axis_size("z"), lax.axis_size("x")
    place = jnp.stack([lax.axis_index("x"), lax.axis_index("core")]).astype(jnp.int32)
    on_first = lax.axis_index("core") == 0

    rows = jnp.concatenate([w_project.reshape(-1, 3 * head), w_output], axis=1)
    rows = lax.all_gather(rows, "core", axis=0, tiled=True)
    kv_rows = jnp.where(on_first, rows[:, head : 2 * head], rows[:, 2 * head : 3 * head])
    qo_rows = jnp.where(on_first, rows[:, :head], rows[:, 3 * head :])

    def over_planes(block):
        copies = jnp.broadcast_to(block[None], (dps * zs, *block.shape))
        return lax.all_to_all(copies, ROWS, 0, 0, tiled=True).reshape(-1, head)

    def over_x(block):
        shifts = {k: lax.ppermute(block, "x", [(i, (i + k) % xs) for i in range(xs)]) for k in (2, 1, 3)}
        return [block, shifts[1], shifts[2], shifts[3]]

    tokens_far, grads_far = core_swap(tokens), core_swap(grads_in)
    kv_plane = over_planes(kv_rows)
    qo_plane = over_planes(after(qo_rows, kv_plane))
    kv_near, own, send = project(place, (tokens, tokens_far), over_x(kv_plane), dps, BF16)
    own, qo_plane = lax.optimization_barrier((own, qo_plane))
    keys, values, local_state = keys_values_state(place, own, core_swap(send))

    qo = over_x(after(qo_plane, local_state))
    prior_state = gate(exchange(sums_of(exchange(local_state), False)))
    qo_near, own, send = project(
        place, (tokens, tokens_far, grads_in, grads_far), qo, dps, F32
    )
    recv = after(core_swap(send), prior_state)
    queries, scores, attn_grad, local_grad = attention_grad(
        place, own, recv, keys, values, prior_state, norm_gain.reshape(1, head)
    )
    kv_far = core_swap(kv_near)
    grad_pieces = exchange(local_grad)
    qo_far = core_swap(qo_near)
    base, *grads = inner_grads(
        place, queries, keys, values, scores, attn_grad, prior_state, qo_near, qo_far
    )
    later_state = exchange(sums_of(grad_pieces, True))
    result = output(place, base, *grads, keys, values, later_state, kv_near, kv_far)
    return result[None]


def solution(mesh):
    split = Mesh(mesh.devices.reshape(mesh.shape["dp"], 4, 8, 2), DP_SEQ)
    in_specs = (P("dp", SEQ, None), P(DP_SEQ, None, None), P(DP_SEQ, None), P(), P("dp", SEQ, None))
    out_specs = P("dp", SEQ, None)
    return jax.shard_map(
        per_device, mesh=split, in_specs=in_specs, out_specs=out_specs, check_vma=False
    )
```

time: 197 us -> 164 us (0.83)
  blocking collectives: 77.4 us -> 27.6 us
  starting transfers between devices: 39.9 us -> 82.9 us
  matrix products: 27.6 us -> 0 us
  waiting for transfers between devices: 40.3 us -> 16.3 us
  Pallas kernels: 0 us -> 18.2 us
  local copies, waits for them, and re-layouts: 6.08 us -> 16.9 us
  other arithmetic: 4.56 us -> 0.78 us
    all_to_all x4 -> x1, blocking collectives: 77.4 us -> 25.8 us  [over_planes(): return lax.all_to_all(copies, ROWS, 0, 0, tiled=True).reshape(-1, head)]
    all_to_all x5, waiting for transfers between devices: 39.9 us -> 4.96 us  [the longest x4 4.96 us: exchange(): return lax.all_to_all(pieces, SEQ, 0, 0, tiled=True).reshape(state.shape)]
    dot_general x18 -> x0, matrix products: 27.6 us -> none  [contract(): lax.dot_general(left, right, (((left_dim,), (right_dim,)), ((), ())), pre...]
    ppermute x0 -> x6, starting transfers between devices: none -> 21.2 us  [over_x(): lax.ppermute(block, 'x', [(i, (i + k) % xs) for i in range(xs)])]
    pallas_call x0 -> x9, Pallas kernels: none -> 18.2 us  [the longest x2 6.26 us: project(): pl.pallas_call(functools.partial(project_kernel, parts), out_shape=[jax.S...]
    unnamed x11 -> x45, local copies, waits for them, and re-layouts: 0.68 us -> 16.1 us
    all_to_all x5, starting transfers between devices: 25.4 us -> 38.6 us  [the longest x4 32.1 us: exchange(): return lax.all_to_all(pieces, SEQ, 0, 0, tiled=True).reshape(state.shape)]
    ppermute x0 -> x6, waiting for transfers between devices: none -> 9.71 us  [over_x(): lax.ppermute(block, 'x', [(i, (i + k) % xs) for i in range(xs)])]
  transfers between devices with their start and end apart: 7 -> 17, of which waited for: 6 -> 7; matrix products, arithmetic and copies ran while one was open for 5% -> 1% of each run, Pallas kernels for 0% -> 6%
where the time goes in v3:
time: 164 us; the launch traced here: 163 us
  starting transfers between devices  82.9 us (51%)
  blocking collectives  27.6 us (17%)
  Pallas kernels  18.2 us (11%)
  local copies, waits for them, and re-layouts  16.9 us (10%)
  waiting for transfers between devices  16.3 us (10%)
    all_to_all x4, starting transfers between devices, exchange(): return lax.all_to_all(pieces, SEQ, 0, 0, tiled=True).reshape(state.shape)  32.1 us
    all_to_all x1, blocking collectives, over_planes(): return lax.all_to_all(copies, ROWS, 0, 0, tiled=True).reshape(-1, head)  25.8 us
    ppermute x6, starting transfers between devices, core_swap(): return lax.ppermute(block, 'core', [(0, 1), (1, 0)])  23.1 us
    ppermute x6, starting transfers between devices, over_x(): lax.ppermute(block, 'x', [(i, (i + k) % xs) for i in range(xs)])  21.2 us
    unnamed x45, local copies, waits for them, and re-layouts  16.1 us
    ppermute x6, waiting for transfers between devices, over_x(): lax.ppermute(block, 'x', [(i, (i + k) % xs) for i in range(xs)])  9.71 us
    all_to_all x1, starting transfers between devices, over_planes(): return lax.all_to_all(copies, ROWS, 0, 0, tiled=True).reshape(-1, head)  6.43 us
    pallas_call x2, Pallas kernels, project(): pl.pallas_call(functools.partial(project_kernel, parts), out_shape=[jax.S...  6.26 us
  transfers between devices with their start and end apart: 17, of which 7 were waited for; matrix products, arithmetic and copies ran while one was open for 1% of the time, Pallas kernels for 6%

profile of v3, /device:TPU:1, one launch (start us, length us, event | category | flops | bytes accessed | tf_op | source)
XLA Modules:
  0.0 163.1 jit_solution(13567353275958693527)
XLA Ops:
  0.0 8.8 %collective-permute-start = (bf16[136,6144]{1,0:T(8,128)(2,1)}, bf16[136,6144]{1,0:T(8,128)(2,1)}, u32[]{:S(2)}, u32[]{:S(2)}) collective-permute-start(bf16[136,6144]{1,0:T(8,128)(2,1)} %bitcast.33), channel_id=1, source_target_pairs={{0,1},{1,0},{2,3},{3,2},{4,5},{5,4},{6,7},{7,6},{8,9},{9,8},{10,11... | collective-permute-start | bytes 5013512 | tf_op jit(solution)/shard_map/ppermute | solution.py:37
  12.1 25.8 %all_to_all.30 = bf16[64,24,128]{2,1,0:T(8,128)(2,1)S(1)} all-to-all(bf16[64,24,128]{2,1,0:T(8,128)(2,1)S(1)} %broadcast_in_dim.6), channel_id=1, replica_groups=mesh['dp'=8,'x'=4,'z'=8,'core'=2] {'dp','z'}, dimensions={0} | all-to-all | bytes 786432 | tf_op jit(solution)/shard_map/all_to_all | solution.py:272
  37.9 3.1 %collective-permute-start.2 = (bf16[1536,128]{1,0:T(8,128)(2,1)S(1)}, bf16[1536,128]{1,0:T(8,128)(2,1)S(1)}, u32[]{:S(2)}, u32[]{:S(2)}) collective-permute-start(bf16[1536,128]{1,0:T(8,128)(2,1)S(1)} %bitcast.25), channel_id=1, source_target_pairs={{0,16},{16,32},{32,48},{48,0},{1,17},{17,33},{33,49},{49,1},{2,18}... | collective-permute-start | bytes 1179656 | tf_op jit(solution)/shard_map/ppermute | solution.py:275
  41.0 4.4 %collective-permute-start.3 = (bf16[1536,128]{1,0:T(8,128)(2,1)S(1)}, bf16[1536,128]{1,0:T(8,128)(2,1)S(1)}, u32[]{:S(2)}, u32[]{:S(2)}) collective-permute-start(bf16[1536,128]{1,0:T(8,128)(2,1)S(1)} %bitcast.26), channel_id=1, source_target_pairs={{0,32},{16,48},{32,0},{48,16},{1,33},{17,49},{33,1},{49,17},{2,34}... | collective-permute-start | bytes 1179656 | tf_op jit(solution)/shard_map/ppermute | solution.py:275
  45.4 3.1 %collective-permute-start.4 = (bf16[1536,128]{1,0:T(8,128)(2,1)S(1)}, bf16[1536,128]{1,0:T(8,128)(2,1)S(1)}, u32[]{:S(2)}, u32[]{:S(2)}) collective-permute-start(bf16[1536,128]{1,0:T(8,128)(2,1)S(1)} %bitcast.27), channel_id=1, source_target_pairs={{0,48},{16,0},{32,16},{48,32},{1,49},{17,1},{33,17},{49,33},{2,50}... | collective-permute-start | bytes 1179656 | tf_op jit(solution)/shard_map/ppermute | solution.py:275
  49.4 6.4 %all-to-all-start.1 = ((bf16[64,24,128]{2,1,0:T(8,128)(2,1)}), bf16[64,24,128]{2,1,0:T(8,128)(2,1)S(1)}, u32[]{:S(2)}, u32[]{:S(2)}) async-start(bf16[64,24,128]{2,1,0:T(8,128)(2,1)} %broadcast_in_dim.7), calls=%async_computation.1 | async-start | bytes 786432 | tf_op jit(solution)/shard_map/all_to_all | solution.py:272
  55.8 2.6 %collective-permute-done.3.refs_4_ = bf16[1536,128]{1,0:T(8,128)(2,1)S(1)} collective-permute-done((bf16[1536,128]{1,0:T(8,128)(2,1)S(1)}, bf16[1536,128]{1,0:T(8,128)(2,1)S(1)}, u32[]{:S(2)}, u32[]{:S(2)}) %collective-permute-start.3) | collective-permute-done | bytes 393248 | tf_op jit(solution)/shard_map/ppermute | solution.py:275
  58.4 2.4 %collective-permute-done.4.refs_5_ = bf16[1536,128]{1,0:T(8,128)(2,1)S(1)} collective-permute-done((bf16[1536,128]{1,0:T(8,128)(2,1)S(1)}, bf16[1536,128]{1,0:T(8,128)(2,1)S(1)}, u32[]{:S(2)}, u32[]{:S(2)}) %collective-permute-start.4) | collective-permute-done | bytes 393248 | tf_op jit(solution)/shard_map/ppermute | solution.py:275
  62.2 3.1 %shard_map.55 = (bf16[6144,128]{1,0:T(8,128)(2,1)}, bf16[136,128]{1,0:T(8,128)(2,1)S(1)}, bf16[136,128]{1,0:T(8,128)(2,1)S(1)}) custom-call(s32[2]{0:T(128)S(1)} %pad_add_fusion.place_ref, bf16[136,6144]{1,0:T(8,128)(2,1)S(1)} %bitcast.34, bf16[136,6144]{1,0:T(8,128)(2,1)} %collective-permute-done.refs_1_, bf16[1536,128]{1,0:T(8,128)(2,1)S(1)} %bitcast.28, ...), custom_call_target="tpu_custom_call" | custom-call | flops 30000001024 | bytes 6488064 | tf_op jit(solution)/shard_map/pallas_call | solution.py:67
  65.3 4.6 %collective-permute-start.5 = (bf16[136,128]{1,0:T(8,128)(2,1)S(1)}, bf16[136,128]{1,0:T(8,128)(2,1)S(1)}, u32[]{:S(2)}, u32[]{:S(2)}) collective-permute-start(bf16[136,128]{1,0:T(8,128)(2,1)S(1)} %get-tuple-element.30), channel_id=1, source_target_pairs={{0,1},{1,0},{2,3},{3,2},{4,5},{5,4},{6,7},{7,6},{8,9},{9,8},{10,11... | collective-permute-start | bytes 104456 | tf_op jit(solution)/shard_map/ppermute | solution.py:37
  72.1 8.1 %all-to-all-start.2 = ((bf16[64,2,128]{2,1,0:T(2,128)(2,1)}), bf16[64,2,128]{2,1,0:T(2,128)(2,1)S(1)}, u32[]{:S(2)}, u32[]{:S(2)}) async-start(bf16[64,2,128]{2,1,0:T(2,128)(2,1)} %bitcast.7), calls=%async_computation.2 | async-start | bytes 65536 | tf_op jit(solution)/shard_map/all_to_all | solution.py:254
  80.2 2.4 %collective-permute-start.1 = (bf16[136,6144]{1,0:T(8,128)(2,1)}, bf16[136,6144]{1,0:T(8,128)(2,1)}, u32[]{:S(2)}, u32[]{:S(2)}) collective-permute-start(bf16[136,6144]{1,0:T(8,128)(2,1)} %bitcast.36), channel_id=1, source_target_pairs={{0,1},{1,0},{2,3},{3,2},{4,5},{5,4},{6,7},{7,6},{8,9},{9,8},{10,11... | collective-permute-start | bytes 5013512 | tf_op jit(solution)/shard_map/ppermute | solution.py:37
  82.6 3.2 %collective-permute-start.6 = (bf16[1536,128]{1,0:T(8,128)(2,1)S(1)}, bf16[1536,128]{1,0:T(8,128)(2,1)S(1)}, u32[]{:S(2)}, u32[]{:S(2)}) collective-permute-start(bf16[1536,128]{1,0:T(8,128)(2,1)S(1)} %bitcast.21), channel_id=1, source_target_pairs={{0,16},{16,32},{32,48},{48,0},{1,17},{17,33},{33,49},{49,1},{2,18}... | collective-permute-start | bytes 1179656 | tf_op jit(solution)/shard_map/ppermute | solution.py:275
  85.8 4.5 %collective-permute-start.7 = (bf16[1536,128]{1,0:T(8,128)(2,1)S(1)}, bf16[1536,128]{1,0:T(8,128)(2,1)S(1)}, u32[]{:S(2)}, u32[]{:S(2)}) collective-permute-start(bf16[1536,128]{1,0:T(8,128)(2,1)S(1)} %bitcast.22), channel_id=1, source_target_pairs={{0,32},{16,48},{32,0},{48,16},{1,33},{17,49},{33,1},{49,17},{2,34}... | collective-permute-start | bytes 1179656 | tf_op jit(solution)/shard_map/ppermute | solution.py:275
  90.3 3.0 %collective-permute-start.8 = (bf16[1536,128]{1,0:T(8,128)(2,1)S(1)}, bf16[1536,128]{1,0:T(8,128)(2,1)S(1)}, u32[]{:S(2)}, u32[]{:S(2)}) collective-permute-start(bf16[1536,128]{1,0:T(8,128)(2,1)S(1)} %bitcast.23), channel_id=1, source_target_pairs={{0,48},{16,0},{32,16},{48,32},{1,49},{17,1},{33,17},{49,33},{2,50}... | collective-permute-start | bytes 1179656 | tf_op jit(solution)/shard_map/ppermute | solution.py:275
  94.1 8.4 %all-to-all-start.3 = ((bf16[64,2,128]{2,1,0:T(2,128)(2,1)}), bf16[64,2,128]{2,1,0:T(2,128)(2,1)S(1)}, u32[]{:S(2)}, u32[]{:S(2)}) async-start(bf16[64,2,128]{2,1,0:T(2,128)(2,1)} %bitcast.9), calls=%async_computation.3 | async-start | bytes 65536 | tf_op jit(solution)/shard_map/all_to_all | solution.py:254
  102.5 3.5 %collective-permute-done.7.refs_6_ = bf16[1536,128]{1,0:T(8,128)(2,1)S(1)} collective-permute-done((bf16[1536,128]{1,0:T(8,128)(2,1)S(1)}, bf16[1536,128]{1,0:T(8,128)(2,1)S(1)}, u32[]{:S(2)}, u32[]{:S(2)}) %collective-permute-start.7) | collective-permute-done | bytes 393248 | tf_op jit(solution)/shard_map/ppermute | solution.py:275
  110.1 3.2 %shard_map.57 = (bf16[6144,128]{1,0:T(8,128)(2,1)S(1)}, f32[136,128]{1,0:T(8,128)S(1)}, f32[136,128]{1,0:T(8,128)S(1)}) custom-call(s32[2]{0:T(128)S(1)} %pad_add_fusion.place_ref, bf16[136,6144]{1,0:T(8,128)(2,1)S(1)} %bitcast.35, bf16[136,6144]{1,0:T(8,128)(2,1)} %collective-permute-done.refs_1_, bf16[136,6144]{1,0:T(8,128)(2,1)S(1)} %bitcast.37, ...), custom_call_target="tpu_custom_call" | custom-call | flops 30000001024 | bytes 6488064 | tf_op jit(solution)/shard_map/pallas_call | solution.py:67
  113.9 3.1 %collective-permute-start.9 = (f32[136,128]{1,0:T(8,128)S(1)}, f32[136,128]{1,0:T(8,128)S(1)}, u32[]{:S(2)}, u32[]{:S(2)}) collective-permute-start(f32[136,128]{1,0:T(8,128)S(1)} %get-tuple-element.34), channel_id=1, source_target_pairs={{0,1},{1,0},{2,3},{3,2},{4,5},{5,4},{6,7},{7,6},{8,9},{9,8},{10,11... | collective-permute-start | bytes 208904 | tf_op jit(solution)/shard_map/ppermute | solution.py:37
  120.2 10.3 %all-to-all-start.4 = ((bf16[64,2,128]{2,1,0:T(2,128)(2,1)}), bf16[64,2,128]{2,1,0:T(2,128)(2,1)S(1)}, u32[]{:S(2)}, u32[]{:S(2)}) async-start(bf16[64,2,128]{2,1,0:T(2,128)(2,1)} %bitcast.12), calls=%async_computation.4 | async-start | bytes 65536 | tf_op jit(solution)/shard_map/all_to_all | solution.py:254
  134.9 4.9 %all-to-all-done.4 = bf16[64,2,128]{2,1,0:T(2,128)(2,1)S(1)} async-done(((bf16[64,2,128]{2,1,0:T(2,128)(2,1)}), bf16[64,2,128]{2,1,0:T(2,128)(2,1)S(1)}, u32[]{:S(2)}, u32[]{:S(2)}) %all-to-all-start.4) | async-done | bytes 32800 | tf_op jit(solution)/shard_map/all_to_all | solution.py:254
  140.6 5.4 %all-to-all-start.5 = ((bf16[64,2,128]{2,1,0:T(2,128)(2,1)}), bf16[64,2,128]{2,1,0:T(2,128)(2,1)S(1)}, u32[]{:S(2)}, u32[]{:S(2)}) async-start(bf16[64,2,128]{2,1,0:T(2,128)(2,1)} %bitcast.14), calls=%async_computation.5 | async-start | bytes 65536 | tf_op jit(solution)/shard_map/all_to_all | solution.py:254
  152.1 2.4 %shard_map.61 = (f32[136,6144]{1,0:T(8,128)S(1)}, f32[136,128]{1,0:T(8,128)S(1)}, f32[136,128]{1,0:T(8,128)S(1)}) custom-call(s32[2]{0:T(128)S(1)} %copy-done.13, bf16[136,128]{1,0:T(8,128)(2,1)S(1)} %get-tuple-element.38.q_ref, bf16[136,128]{1,0:T(8,128)(2,1)S(1)} %get-tuple-element.36.k_ref, bf16[136,128]{1,0:T(8,128)(2,1)S(1)} %get-tuple-element.37.v_ref, ...), custom_call_target="tpu_custom_call" | custom-call | flops 213909504 | bytes 6488064 | tf_op jit(solution)/shard_map/pallas_call | solution.py:182
  158.2 4.9 %shard_map.63 = bf16[136,6144]{1,0:T(8,128)(2,1)} custom-call(s32[2]{0:T(128)S(1)} %copy-done.14, f32[136,6144]{1,0:T(8,128)S(1)} %get-tuple-element.42.base, f32[136,128]{1,0:T(8,128)S(1)} %copy-done.5, f32[136,128]{1,0:T(8,128)S(1)} %copy-done.7, bf16[136,128]{1,0:T(8,128)(2,1)S(1)} %get-tuple-element.36.k_ref, ...), custom_call_target="tpu_custom_call" | custom-call | flops 427819008 | bytes 8159232 | tf_op jit(solution)/shard_map/pallas_call | solution.py:219
  (71 shorter events, 31.4 us)
Async XLA Ops:
  0.0 60.8 %collective-permute-start = (bf16[136,6144]{1,0:T(8,128)(2,1)}, bf16[136,6144]{1,0:T(8,128)(2,1)}, u32[]{:S(2)}, u32[]{:S(2)}) collective-permute-start(bf16[136,6144]{1,0:T(8,128)(2,1)} %bitcast.33), channel_id=1, source_target_pairs={{0,1},{1,0},{2,3},{3,2},{4,5},{5,4},{6,7},{7,6},{8,9},{9,8},{10,11... | collective-permute-start | bytes 5013512 | tf_op jit(solution)/shard_map/ppermute | solution.py:37
  37.9 17.9 %collective-permute-start.2 = (bf16[1536,128]{1,0:T(8,128)(2,1)S(1)}, bf16[1536,128]{1,0:T(8,128)(2,1)S(1)}, u32[]{:S(2)}, u32[]{:S(2)}) collective-permute-start(bf16[1536,128]{1,0:T(8,128)(2,1)S(1)} %bitcast.25), channel_id=1, source_target_pairs={{0,16},{16,32},{32,48},{48,0},{1,17},{17,33},{33,49},{49,1},{2,18}... | collective-permute-start | bytes 1179656 | tf_op jit(solution)/shard_map/ppermute | solution.py:275
  41.0 17.4 %collective-permute-start.3 = (bf16[1536,128]{1,0:T(8,128)(2,1)S(1)}, bf16[1536,128]{1,0:T(8,128)(2,1)S(1)}, u32[]{:S(2)}, u32[]{:S(2)}) collective-permute-start(bf16[1536,128]{1,0:T(8,128)(2,1)S(1)} %bitcast.26), channel_id=1, source_target_pairs={{0,32},{16,48},{32,0},{48,16},{1,33},{17,49},{33,1},{49,17},{2,34}... | collective-permute-start | bytes 1179656 | tf_op jit(solution)/shard_map/ppermute | solution.py:275
  45.4 15.4 %collective-permute-start.4 = (bf16[1536,128]{1,0:T(8,128)(2,1)S(1)}, bf16[1536,128]{1,0:T(8,128)(2,1)S(1)}, u32[]{:S(2)}, u32[]{:S(2)}) collective-permute-start(bf16[1536,128]{1,0:T(8,128)(2,1)S(1)} %bitcast.27), channel_id=1, source_target_pairs={{0,48},{16,0},{32,16},{48,32},{1,49},{17,1},{33,17},{49,33},{2,50}... | collective-permute-start | bytes 1179656 | tf_op jit(solution)/shard_map/ppermute | solution.py:275
  48.6 69.3 %copy-start.12 = (s32[2]{0:T(128)}, s32[2]{0:T(128)S(1)}, u32[]{:S(2)}) copy-start(s32[2]{0:T(128)S(1)} %pad_add_fusion.place_ref) | copy-start | bytes 28
  49.4 20.6 %all-to-all-start.1 = ((bf16[64,24,128]{2,1,0:T(8,128)(2,1)}), bf16[64,24,128]{2,1,0:T(8,128)(2,1)S(1)}, u32[]{:S(2)}, u32[]{:S(2)}) async-start(bf16[64,24,128]{2,1,0:T(8,128)(2,1)} %broadcast_in_dim.7), calls=%async_computation.1 | async-start | bytes 786432 | tf_op jit(solution)/shard_map/all_to_all | solution.py:272
  60.8 1.4 copy-start.15
  65.3 5.4 %collective-permute-start.5 = (bf16[136,128]{1,0:T(8,128)(2,1)S(1)}, bf16[136,128]{1,0:T(8,128)(2,1)S(1)}, u32[]{:S(2)}, u32[]{:S(2)}) collective-permute-start(bf16[136,128]{1,0:T(8,128)(2,1)S(1)} %get-tuple-element.30), channel_id=1, source_target_pairs={{0,1},{1,0},{2,3},{3,2},{4,5},{5,4},{6,7},{7,6},{8,9},{9,8},{10,11... | collective-permute-start | bytes 104456 | tf_op jit(solution)/shard_map/ppermute | solution.py:37
  72.1 21.2 %all-to-all-start.2 = ((bf16[64,2,128]{2,1,0:T(2,128)(2,1)}), bf16[64,2,128]{2,1,0:T(2,128)(2,1)S(1)}, u32[]{:S(2)}, u32[]{:S(2)}) async-start(bf16[64,2,128]{2,1,0:T(2,128)(2,1)} %bitcast.7), calls=%async_computation.2 | async-start | bytes 65536 | tf_op jit(solution)/shard_map/all_to_all | solution.py:254
  80.2 22.2 %collective-permute-start.1 = (bf16[136,6144]{1,0:T(8,128)(2,1)}, bf16[136,6144]{1,0:T(8,128)(2,1)}, u32[]{:S(2)}, u32[]{:S(2)}) collective-permute-start(bf16[136,6144]{1,0:T(8,128)(2,1)} %bitcast.36), channel_id=1, source_target_pairs={{0,1},{1,0},{2,3},{3,2},{4,5},{5,4},{6,7},{7,6},{8,9},{9,8},{10,11... | collective-permute-start | bytes 5013512 | tf_op jit(solution)/shard_map/ppermute | solution.py:37
  82.6 19.9 %collective-permute-start.6 = (bf16[1536,128]{1,0:T(8,128)(2,1)S(1)}, bf16[1536,128]{1,0:T(8,128)(2,1)S(1)}, u32[]{:S(2)}, u32[]{:S(2)}) collective-permute-start(bf16[1536,128]{1,0:T(8,128)(2,1)S(1)} %bitcast.21), channel_id=1, source_target_pairs={{0,16},{16,32},{32,48},{48,0},{1,17},{17,33},{33,49},{49,1},{2,18}... | collective-permute-start | bytes 1179656 | tf_op jit(solution)/shard_map/ppermute | solution.py:275
  85.8 20.1 %collective-permute-start.7 = (bf16[1536,128]{1,0:T(8,128)(2,1)S(1)}, bf16[1536,128]{1,0:T(8,128)(2,1)S(1)}, u32[]{:S(2)}, u32[]{:S(2)}) collective-permute-start(bf16[1536,128]{1,0:T(8,128)(2,1)S(1)} %bitcast.22), channel_id=1, source_target_pairs={{0,32},{16,48},{32,0},{48,16},{1,33},{17,49},{33,1},{49,17},{2,34}... | collective-permute-start | bytes 1179656 | tf_op jit(solution)/shard_map/ppermute | solution.py:275
  90.3 16.9 %collective-permute-start.8 = (bf16[1536,128]{1,0:T(8,128)(2,1)S(1)}, bf16[1536,128]{1,0:T(8,128)(2,1)S(1)}, u32[]{:S(2)}, u32[]{:S(2)}) collective-permute-start(bf16[1536,128]{1,0:T(8,128)(2,1)S(1)} %bitcast.23), channel_id=1, source_target_pairs={{0,48},{16,0},{32,16},{48,32},{1,49},{17,1},{33,17},{49,33},{2,50}... | collective-permute-start | bytes 1179656 | tf_op jit(solution)/shard_map/ppermute | solution.py:275
  94.1 22.9 %all-to-all-start.3 = ((bf16[64,2,128]{2,1,0:T(2,128)(2,1)}), bf16[64,2,128]{2,1,0:T(2,128)(2,1)S(1)}, u32[]{:S(2)}, u32[]{:S(2)}) async-start(bf16[64,2,128]{2,1,0:T(2,128)(2,1)} %bitcast.9), calls=%async_computation.3 | async-start | bytes 65536 | tf_op jit(solution)/shard_map/all_to_all | solution.py:254
  107.2 1.4 copy-start.16
  108.6 1.4 copy-start.17
  113.9 19.0 %copy-start = (bf16[6144,128]{1,0:T(8,128)(2,1)}, bf16[6144,128]{1,0:T(8,128)(2,1)S(1)}, u32[]{:S(2)}) copy-start(bf16[6144,128]{1,0:T(8,128)(2,1)S(1)} %get-tuple-element.41.near_ref) | copy-start | bytes 4718596
  113.9 4.0 %collective-permute-start.9 = (f32[136,128]{1,0:T(8,128)S(1)}, f32[136,128]{1,0:T(8,128)S(1)}, u32[]{:S(2)}, u32[]{:S(2)}) collective-permute-start(f32[136,128]{1,0:T(8,128)S(1)} %get-tuple-element.34), channel_id=1, source_target_pairs={{0,1},{1,0},{2,3},{3,2},{4,5},{5,4},{6,7},{7,6},{8,9},{9,8},{10,11... | collective-permute-start | bytes 208904 | tf_op jit(solution)/shard_map/ppermute | solution.py:37
  117.0 2.6 %copy-start.10 = (bf16[128,128]{1,0:T(8,128)(2,1)}, bf16[128,128]{1,0:T(8,128)(2,1)S(1)}, u32[]{:S(2)}) copy-start(bf16[128,128]{1,0:T(8,128)(2,1)S(1)} %shard_map.59.prior_ref) | copy-start | bytes 98308
  120.2 19.6 %all-to-all-start.4 = ((bf16[64,2,128]{2,1,0:T(2,128)(2,1)}), bf16[64,2,128]{2,1,0:T(2,128)(2,1)S(1)}, u32[]{:S(2)}, u32[]{:S(2)}) async-start(bf16[64,2,128]{2,1,0:T(2,128)(2,1)} %bitcast.12), calls=%async_computation.4 | async-start | bytes 65536 | tf_op jit(solution)/shard_map/all_to_all | solution.py:254
  130.5 25.3 %collective-permute-start.11 = (bf16[6144,128]{1,0:T(8,128)(2,1)}, bf16[6144,128]{1,0:T(8,128)(2,1)}, u32[]{:S(2)}, u32[]{:S(2)}) collective-permute-start(bf16[6144,128]{1,0:T(8,128)(2,1)} %get-tuple-element.46.near_ref), channel_id=1, source_target_pairs={{0,1},{1,0},{2,3},{3,2},{4,5},{5,4},{6,7},{7,6},{8,9},{9,8},{10,11... | collective-permute-start | bytes 4718600 | tf_op jit(solution)/shard_map/ppermute | solution.py:37
  132.9 13.1 %collective-permute-start.10 = (bf16[6144,128]{1,0:T(8,128)(2,1)S(1)}, bf16[6144,128]{1,0:T(8,128)(2,1)S(1)}, u32[]{:S(2)}, u32[]{:S(2)}) collective-permute-start(bf16[6144,128]{1,0:T(8,128)(2,1)S(1)} %get-tuple-element.41.near_ref), channel_id=1, source_target_pairs={{0,1},{1,0},{2,3},{3,2},{4,5},{5,4},{6,7},{7,6},{8,9},{9,8},{10,11... | collective-permute-start | bytes 4718600 | tf_op jit(solution)/shard_map/ppermute | solution.py:37
  140.6 15.2 %all-to-all-start.5 = ((bf16[64,2,128]{2,1,0:T(2,128)(2,1)}), bf16[64,2,128]{2,1,0:T(2,128)(2,1)S(1)}, u32[]{:S(2)}, u32[]{:S(2)}) async-start(bf16[64,2,128]{2,1,0:T(2,128)(2,1)} %bitcast.14), calls=%async_computation.5 | async-start | bytes 65536 | tf_op jit(solution)/shard_map/all_to_all | solution.py:254
  147.1 1.4 copy-start.1
  (14 other events, 11.4 us)

commit v4 on v3

v4 whole, which is shorter than its diff:
```python
import functools

import jax
import jax.numpy as jnp
from jax import lax
from jax.experimental import pallas as pl
from jax.experimental.pallas import tpu as pltpu
from jax.sharding import Mesh
from jax.sharding import PartitionSpec as P

SEQ = ("x", "z", "core")
DP_SEQ = ("dp", "x", "z", "core")
ROWS = ("dp", "z")
BF16 = jnp.bfloat16
F32 = jnp.float32
LIMIT = 16 * 1024 * 1024
LONG = 30_000_000_000
SMEM = pl.BlockSpec(memory_space=pltpu.SMEM)
VMEM = pl.BlockSpec(memory_space=pltpu.VMEM)


def contract(left, right, left_dim, right_dim):
    return lax.dot_general(
        left, right, (((left_dim,), (right_dim,)), ((), ())), preferred_element_type=F32
    )


def cost(flops, moved):
    return pl.CostEstimate(flops=flops, bytes_accessed=moved, transcendentals=0)


def after(value, *events):
    return lax.optimization_barrier((value, *events))[0]


def core_swap(block):
    return lax.ppermute(block, "core", [(0, 1), (1, 0)])


def in_hbm(*values):
    return [pltpu.with_memory_space_constraint(v, pltpu.HBM) for v in values]


def in_vmem(*values):
    return [pltpu.with_memory_space_constraint(v, pltpu.VMEM) for v in values]


def project_kernel(shifts, steps, place_ref, *refs):
    tokens, blocks, (weight_ref, own_ref, send_ref, owns, sends) = refs[:-9], refs[-9:-5], refs[-5:]
    step = pl.program_id(0)
    depth = tokens[0].shape[1]
    rows = depth // 8

    @pl.when(step == 0)
    def _():
        owns[...] = jnp.zeros_like(owns)
        sends[...] = jnp.zeros_like(sends)

    for k, ref in zip(shifts, blocks):
        source = lax.rem(place_ref[0] - k + 4, 4)
        for p in range(2):
            at = pl.multiple_of(step * depth + (p * 4 + source) * rows, 64)
            weight_ref[pl.ds(at, rows), :] = ref[p * rows : (p + 1) * rows, :]

    weight = weight_ref[pl.ds(pl.multiple_of(step * depth, 128), depth), :]

    def products(own, far):
        owns[...] += contract(own[...], weight, 1, 0)
        sends[...] += contract(far[...], weight, 1, 0)

    if len(tokens) == 2:
        products(*tokens)
    else:
        pl.when(place_ref[1] == 0)(lambda: products(*tokens[:2]))
        pl.when(place_ref[1] != 0)(lambda: products(*tokens[2:]))

    @pl.when(step == steps - 1)
    def _():
        own_ref[...] = owns[...].astype(own_ref.dtype)
        send_ref[...] = sends[...].astype(send_ref.dtype)


def project(place, tokens, blocks, dtype):
    count, depth = tokens[0].shape
    steps = 4
    wide = (count, depth // steps)
    if len(tokens) == 2:
        pairs = [pl.BlockSpec(wide, lambda i, s: (0, i))] * 2
    else:
        pairs = [pl.BlockSpec(wide, lambda i, s: (0, i * (1 - s[1])))] * 2
        pairs += [pl.BlockSpec(wide, lambda i, s: (0, i * s[1]))] * 2
    weight = pl.BlockSpec((depth // 4 // steps, 128), lambda i, s: (i, 0))
    return pl.pallas_call(
        functools.partial(project_kernel, tuple(blocks), steps),
        out_shape=[pltpu.VMEM((depth, 128), BF16), *[pltpu.VMEM((count, 128), dtype)] * 2],
        grid_spec=pltpu.PrefetchScalarGridSpec(
            num_scalar_prefetch=1,
            grid=(steps,),
            in_specs=pairs + [weight] * 4,
            out_specs=[VMEM] * 3,
            scratch_shapes=[pltpu.VMEM((count, 128), F32)] * 2,
        ),
        compiler_params=pltpu.CompilerParams(vmem_limit_bytes=LIMIT),
        cost_estimate=cost(LONG, 4 * count * depth + 4 * depth * 128),
    )(place, *in_hbm(*tokens), *blocks.values())


def state_kernel(place_ref, own_ref, recv_ref, key_ref, value_ref, state_ref):
    own, recv = own_ref[...], recv_ref[...]
    first = place_ref[1] == 0
    keys, values = jnp.where(first, own, recv), jnp.where(first, recv, own)
    key_ref[...] = keys
    value_ref[...] = values
    state_ref[...] = contract(keys, values, 0, 0).astype(BF16)


def keys_values_state(place, own, recv):
    row = pltpu.VMEM(own.shape, BF16)
    return pl.pallas_call(
        state_kernel,
        out_shape=[row, row, jax.ShapeDtypeStruct((128, 128), BF16)],
        in_specs=[SMEM] + [VMEM] * 2,
        out_specs=[VMEM] * 3,
        compiler_params=pltpu.CompilerParams(vmem_limit_bytes=LIMIT),
        cost_estimate=cost(2 * own.size * 128, 8 * own.size),
    )(place, *in_vmem(own), recv)


def gate_kernel(in_ref, out_ref):
    out_ref[...] = in_ref[...]


def gate(value):
    return pl.pallas_call(
        gate_kernel,
        out_shape=pltpu.VMEM(value.shape, value.dtype),
        in_specs=[VMEM],
        out_specs=VMEM,
        compiler_params=pltpu.CompilerParams(vmem_limit_bytes=LIMIT),
        cost_estimate=cost(LONG, 4 * value.size),
    )(value)


def causal_of(count):
    rows = lax.broadcasted_iota(jnp.int32, (count, count), 0)
    return rows >= lax.broadcasted_iota(jnp.int32, (count, count), 1)


def grad_kernel(
    place_ref, near_ref, far_ref, k_ref, v_ref, prior_ref, gain_ref,
    q_ref, attn_ref, state_ref,
):
    first = place_ref[1] == 0
    near, far = near_ref[...], far_ref[...]
    queries = jnp.where(first, near, far).astype(BF16)
    head_grad = jnp.where(first, far, near)
    q_ref[...] = queries
    scores = contract(queries, k_ref[...], 1, 1)
    scores = jnp.where(causal_of(scores.shape[0]), scores, 0.0).astype(BF16)
    attended = contract(scores, v_ref[...], 1, 0) + contract(queries, prior_ref[...], 1, 0)
    inv_rms = lax.rsqrt(jnp.mean(attended * attended, axis=-1, keepdims=True) + 1e-06)
    scaled = gain_ref[...] * head_grad
    mean = jnp.mean(attended * scaled, axis=-1, keepdims=True)
    attn_grad = inv_rms * scaled - attended * (inv_rms * inv_rms * inv_rms) * mean
    attn_grad = attn_grad.astype(BF16)
    attn_ref[...] = attn_grad
    state_ref[...] = contract(queries, attn_grad, 0, 0).astype(BF16)


def attention_grad(place, near, far, keys, values, prior, gain):
    count = keys.shape[0]
    row = pltpu.VMEM((count, 128), BF16)
    return pl.pallas_call(
        grad_kernel,
        out_shape=[
            row,
            row,
            jax.ShapeDtypeStruct((128, 128), BF16),
        ],
        in_specs=[SMEM] + [VMEM] * 6,
        out_specs=[VMEM] * 3,
        compiler_params=pltpu.CompilerParams(vmem_limit_bytes=LIMIT),
        cost_estimate=cost(LONG, 16 * count * 128),
    )(place, *in_vmem(near), far, *in_vmem(keys, values, prior), gain)


def inner_kernel(
    place_ref, q_ref, k_ref, v_ref, attn_ref, prior_ref, near_ref, far_ref,
    base_ref, dk_ref, dv_ref,
):
    attn_grad = attn_ref[...]
    scores = contract(q_ref[...], k_ref[...], 1, 1)
    scores = jnp.where(causal_of(scores.shape[0]), scores, 0.0).astype(BF16)
    prob = contract(attn_grad, v_ref[...], 1, 1)
    prob = jnp.where(causal_of(prob.shape[0]), prob, 0.0).astype(BF16)
    query_grad = contract(prob, k_ref[...], 1, 0) + contract(attn_grad, prior_ref[...], 1, 1)
    query_grad = query_grad.astype(BF16)
    dk_ref[...] = contract(prob, q_ref[...], 0, 0)
    dv_ref[...] = contract(scores, attn_grad, 0, 0)
    part = near_ref.shape[0] // 4
    for i in range(4):
        at = slice(i * part, (i + 1) * part)
        weight = jnp.where(place_ref[1] == 0, near_ref[at, :], far_ref[at, :])
        base_ref[:, at] = contract(query_grad, weight, 1, 1)


def inner_grads(place, queries, keys, values, attn_grad, prior, near, far):
    count, depth = queries.shape[0], near.shape[0]
    return pl.pallas_call(
        inner_kernel,
        out_shape=[
            pltpu.VMEM((count, depth), F32),
            pltpu.VMEM((count, 128), F32),
            pltpu.VMEM((count, 128), F32),
        ],
        in_specs=[SMEM] + [VMEM] * 7,
        out_specs=[VMEM] * 3,
        compiler_params=pltpu.CompilerParams(vmem_limit_bytes=LIMIT),
        cost_estimate=cost(LONG, 4 * count * depth + 4 * depth * 128),
    )(place, *in_vmem(queries, keys, values, attn_grad, prior, near), far)


def output_kernel(place_ref, base, dk, dv, k_ref, v_ref, later, near_ref, far_ref, out_ref, joined):
    @pl.when(pl.program_id(0) == 0)
    def _():
        first = place_ref[1] == 0
        key_grad = (dk[...] + contract(v_ref[...], later[...], 1, 1)).astype(BF16)
        value_grad = (dv[...] + contract(k_ref[...], later[...], 1, 0)).astype(BF16)
        joined[:, :128] = jnp.where(first, key_grad, value_grad)
        joined[:, 128:] = jnp.where(first, value_grad, key_grad)

    part = out_ref.shape[1]
    at = pl.ds(pl.multiple_of(pl.program_id(0) * part, 128), part)
    weight = jnp.concatenate([near_ref[at, :], far_ref[at, :]], axis=1)
    total = base[:, at] + contract(joined[...], weight, 1, 1)
    out_ref[...] = total.astype(BF16)


def output(place, base, dk, dv, keys, values, later, near, far):
    count, depth = base.shape
    steps = 4
    return pl.pallas_call(
        output_kernel,
        grid=(steps,),
        out_shape=jax.ShapeDtypeStruct((count, depth), BF16),
        in_specs=[SMEM] + [VMEM] * 8,
        out_specs=pl.BlockSpec((count, depth // steps), lambda i: (0, i)),
        scratch_shapes=[pltpu.VMEM((count, 256), BF16)],
        compiler_params=pltpu.CompilerParams(vmem_limit_bytes=LIMIT),
        cost_estimate=cost(4 * count * depth * 128, 4 * depth * 128 + 6 * count * depth),
    )(place, *in_vmem(base, dk, dv, keys, values), later, *in_vmem(near), far)


def sums_kernel(reverse, in_ref, out_ref):
    each = in_ref.shape[0] // 64
    to = lax.broadcasted_iota(jnp.int32, (128, 128), 0)
    frm = lax.broadcasted_iota(jnp.int32, (128, 128), 1)
    others = (frm // each > to // each) if reverse else (frm // each < to // each)
    mask = jnp.where(others & (frm % each == to % each), 1.0, 0.0).astype(BF16)
    out_ref[...] = contract(mask, in_ref[...], 1, 0).astype(BF16)


def sums_of(pieces, reverse):
    return pl.pallas_call(
        functools.partial(sums_kernel, reverse),
        out_shape=jax.ShapeDtypeStruct(pieces.shape, BF16),
        in_specs=[VMEM],
        out_specs=VMEM,
        compiler_params=pltpu.CompilerParams(vmem_limit_bytes=LIMIT),
        cost_estimate=cost(LONG, 4 * pieces.size),
    )(pieces)


def exchange(state):
    peers, head = lax.axis_size(SEQ), state.shape[1]
    pieces = state.reshape(peers, -1, head)
    return lax.all_to_all(pieces, SEQ, 0, 0, tiled=True).reshape(state.shape)


def per_device(inputs, w_project, w_output, norm_gain, out_grad):
    tokens = inputs[0]
    grads_in = out_grad[0]
    head = w_output.shape[1]
    dps, zs, xs = lax.axis_size("dp"), lax.axis_size("z"), lax.axis_size("x")
    place = jnp.stack([lax.axis_index("x"), lax.axis_index("core")]).astype(jnp.int32)
    on_first = lax.axis_index("core") == 0

    rows = jnp.concatenate([w_project.reshape(-1, 3 * head), w_output], axis=1)
    rows = lax.all_gather(rows, "core", axis=0, tiled=True)
    kv_rows = jnp.where(on_first, rows[:, head : 2 * head], rows[:, 2 * head : 3 * head])
    qo_rows = jnp.where(on_first, rows[:, :head], rows[:, 3 * head :])

    def copied(block):
        return jnp.broadcast_to(block[None], (dps * zs, *block.shape))

    def over_planes(copies):
        return lax.all_to_all(copies, ROWS, 0, 0, tiled=True).reshape(-1, head)

    def over_x(block):
        shifts = {k: lax.ppermute(block, "x", [(i, (i + k) % xs) for i in range(xs)]) for k in (2, 1, 3)}
        return {1: shifts[1], 3: shifts[3], 2: shifts[2], 0: block}

    kv_copies = copied(kv_rows)
    tokens_far = core_swap(after(tokens, kv_copies))
    grads_far = core_swap(after(grads_in, kv_copies))
    kv_plane = over_planes(kv_copies)
    qo_plane = over_planes(copied(gate(after(qo_rows, kv_plane))))
    tokens_far = after(tokens_far, grads_far)
    kv_near, own, send = project(place, (tokens, tokens_far), over_x(kv_plane), BF16)
    own, qo_plane = lax.optimization_barrier((own, qo_plane))
    keys, values, local_state = keys_values_state(place, own, core_swap(send))

    qo = over_x(after(qo_plane, local_state))
    prior_state = gate(exchange(sums_of(exchange(local_state), False)))
    qo_near, own, send = project(
        place, (tokens, tokens_far, grads_in, grads_far), qo, F32
    )
    recv = after(core_swap(send), prior_state)
    queries, attn_grad, local_grad = attention_grad(
        place, own, recv, keys, values, prior_state, norm_gain.reshape(1, head)
    )
    kv_far = core_swap(kv_near)
    grad_pieces = exchange(local_grad)
    qo_far = core_swap(qo_near)
    base, *grads = inner_grads(
        place, queries, keys, values, attn_grad, prior_state, qo_near, qo_far
    )
    later_state = exchange(sums_of(grad_pieces, True))
    result = output(place, base, *grads, keys, values, later_state, kv_near, kv_far)
    return result[None]


def solution(mesh):
    split = Mesh(mesh.devices.reshape(mesh.shape["dp"], 4, 8, 2), DP_SEQ)
    in_specs = (P("dp", SEQ, None), P(DP_SEQ, None, None), P(DP_SEQ, None), P(), P("dp", SEQ, None))
    out_specs = P("dp", SEQ, None)
    return jax.shard_map(
        per_device, mesh=split, in_specs=in_specs, out_specs=out_specs, check_vma=False
    )
```

time: 164 us -> 154 us (0.939)
  blocking collectives: 27.6 us -> 8.36 us
  local copies, waits for them, and re-layouts: 16.9 us -> 7.57 us
  waiting for transfers between devices: 16.3 us -> 25.6 us
  starting transfers between devices: 82.9 us -> 88.3 us
  Pallas kernels: 18.2 us -> 21.8 us
    all_to_all x1 -> x0, blocking collectives: 25.8 us -> none  [over_planes(): return lax.all_to_all(copies, ROWS, 0, 0, tiled=True).reshape(-1, head)]
    all_to_all x1 -> x2, starting transfers between devices: 6.43 us -> 17.4 us  [over_planes(): return lax.all_to_all(copies, ROWS, 0, 0, tiled=True).reshape(-1, head)]
    all_to_all x1 -> x2, waiting for transfers between devices: 0.01 us -> 10.5 us  [over_planes(): return lax.all_to_all(copies, ROWS, 0, 0, tiled=True).reshape(-1, head)]
    unnamed x45 -> x27, local copies, waits for them, and re-layouts: 16.1 us -> 5.97 us
    ppermute x6, starting transfers between devices: 23.1 us -> 16 us  [core_swap(): return lax.ppermute(block, 'core', [(0, 1), (1, 0)])]
    all_gather x1, blocking collectives: 1.82 us -> 8.36 us  [per_device(): rows = lax.all_gather(rows, 'core', axis=0, tiled=True)]
    pallas_call x5 -> x6, Pallas kernels: 10.4 us -> 14.1 us  [the longest x2 10.1 us: project(): pl.pallas_call(functools.partial(project_kernel, tuple(blocks), steps), o...]
    ppermute x6, waiting for transfers between devices: 9.71 us -> 6.02 us  [over_x(): lax.ppermute(block, 'x', [(i, (i + k) % xs) for i in range(xs)])]
  transfers between devices with their start and end apart: 17 -> 18, of which waited for: 7 -> 9; matrix products, arithmetic and copies ran while one was open for 1% -> 1% of each run, Pallas kernels for 6% -> 9%
where the time goes in v4:
time: 154 us; the launch traced here: 153 us
  starting transfers between devices  88.3 us (57%)
  waiting for transfers between devices  25.6 us (17%)
  Pallas kernels  21.8 us (14%)
  blocking collectives  8.36 us (5%)
  local copies, waits for them, and re-layouts  7.57 us (5%)
    all_to_all x4, starting transfers between devices, exchange(): return lax.all_to_all(pieces, SEQ, 0, 0, tiled=True).reshape(state.shape)  34.7 us
    ppermute x6, starting transfers between devices, over_x(): lax.ppermute(block, 'x', [(i, (i + k) % xs) for i in range(xs)])  20.1 us
    all_to_all x2, starting transfers between devices, over_planes(): return lax.all_to_all(copies, ROWS, 0, 0, tiled=True).reshape(-1, head)  17.4 us
    ppermute x6, starting transfers between devices, core_swap(): return lax.ppermute(block, 'core', [(0, 1), (1, 0)])  16 us
    all_to_all x2, waiting for transfers between devices, over_planes(): return lax.all_to_all(copies, ROWS, 0, 0, tiled=True).reshape(-1, head)  10.5 us
    pallas_call x2, Pallas kernels, project(): pl.pallas_call(functools.partial(project_kernel, tuple(blocks), steps), o...  10.1 us
    all_gather x1, blocking collectives, per_device(): rows = lax.all_gather(rows, 'core', axis=0, tiled=True)  8.36 us
    all_to_all x4, waiting for transfers between devices, exchange(): return lax.all_to_all(pieces, SEQ, 0, 0, tiled=True).reshape(state.shape)  7.42 us
  transfers between devices with their start and end apart: 18, of which 9 were waited for; matrix products, arithmetic and copies ran while one was open for 1% of the time, Pallas kernels for 9%

profile of v4, /device:TPU:1, one launch (start us, length us, event | category | flops | bytes accessed | tf_op | source)
XLA Modules:
  0.0 152.7 jit_solution(14847513067086327237)
XLA Ops:
  1.4 8.4 %all-gather = bf16[2,12,512]{2,1,0:T(8,128)(2,1)S(1)} all-gather(bf16[1,12,512]{2,1,0:T(8,128)(2,1)S(1)} %maximum_bitcast_fusion), channel_id=1, replica_groups=mesh['dp'=8,'x'=4,'z'=8,'core'=2] {'core'}, dimensions={0}, use_global_device_ids=true | all-gather | bytes 36864 | tf_op jit(solution)/shard_map/all_gather | solution.py:289
  10.6 10.9 %all-to-all-start = ((bf16[64,24,128]{2,1,0:T(8,128)(2,1)}), bf16[64,24,128]{2,1,0:T(8,128)(2,1)S(1)}, u32[]{:S(2)}, u32[]{:S(2)}) async-start(bf16[64,24,128]{2,1,0:T(8,128)(2,1)} %broadcast_in_dim.6), calls=%async_computation | async-start | bytes 786432 | tf_op jit(solution)/shard_map/all_to_all | solution.py:297
  21.6 2.5 %collective-permute-start = (bf16[136,6144]{1,0:T(8,128)(2,1)}, bf16[136,6144]{1,0:T(8,128)(2,1)}, u32[]{:S(2)}, u32[]{:S(2)}) collective-permute-start(bf16[136,6144]{1,0:T(8,128)(2,1)} %bitcast.36), channel_id=1, source_target_pairs={{0,1},{1,0},{2,3},{3,2},{4,5},{5,4},{6,7},{7,6},{8,9},{9,8},{10,11... | collective-permute-start | bytes 5013512 | tf_op jit(solution)/shard_map/ppermute | solution.py:37
  26.1 10.5 %all-to-all-done = bf16[64,24,128]{2,1,0:T(8,128)(2,1)S(1)} async-done(((bf16[64,24,128]{2,1,0:T(8,128)(2,1)}), bf16[64,24,128]{2,1,0:T(8,128)(2,1)S(1)}, u32[]{:S(2)}, u32[]{:S(2)}) %all-to-all-start) | async-done | bytes 393248 | tf_op jit(solution)/shard_map/all_to_all | solution.py:297
  36.6 4.6 %collective-permute-start.4 = (bf16[1536,128]{1,0:T(8,128)(2,1)S(1)}, bf16[1536,128]{1,0:T(8,128)(2,1)S(1)}, u32[]{:S(2)}, u32[]{:S(2)}) collective-permute-start(bf16[1536,128]{1,0:T(8,128)(2,1)S(1)} %bitcast.25), channel_id=1, source_target_pairs={{0,32},{16,48},{32,0},{48,16},{1,33},{17,49},{33,1},{49,17},{2,34}... | collective-permute-start | bytes 1179656 | tf_op jit(solution)/shard_map/ppermute | solution.py:300
  41.2 2.8 %collective-permute-start.3 = (bf16[1536,128]{1,0:T(8,128)(2,1)S(1)}, bf16[1536,128]{1,0:T(8,128)(2,1)S(1)}, u32[]{:S(2)}, u32[]{:S(2)}) collective-permute-start(bf16[1536,128]{1,0:T(8,128)(2,1)S(1)} %bitcast.26), channel_id=1, source_target_pairs={{0,48},{16,0},{32,16},{48,32},{1,49},{17,1},{33,17},{49,33},{2,50}... | collective-permute-start | bytes 1179656 | tf_op jit(solution)/shard_map/ppermute | solution.py:300
  44.0 2.5 %collective-permute-start.2 = (bf16[1536,128]{1,0:T(8,128)(2,1)S(1)}, bf16[1536,128]{1,0:T(8,128)(2,1)S(1)}, u32[]{:S(2)}, u32[]{:S(2)}) collective-permute-start(bf16[1536,128]{1,0:T(8,128)(2,1)S(1)} %bitcast.27), channel_id=1, source_target_pairs={{0,16},{16,32},{32,48},{48,0},{1,17},{17,33},{33,49},{49,1},{2,18}... | collective-permute-start | bytes 1179656 | tf_op jit(solution)/shard_map/ppermute | solution.py:300
  47.3 6.5 %all-to-all-start.1 = ((bf16[64,24,128]{2,1,0:T(8,128)(2,1)}), bf16[64,24,128]{2,1,0:T(8,128)(2,1)S(1)}, u32[]{:S(2)}, u32[]{:S(2)}) async-start(bf16[64,24,128]{2,1,0:T(8,128)(2,1)} %broadcast_in_dim.7), calls=%async_computation.1 | async-start | bytes 786432 | tf_op jit(solution)/shard_map/all_to_all | solution.py:297
  53.9 4.1 %collective-permute-done.3.refs_3_ = bf16[1536,128]{1,0:T(8,128)(2,1)S(1)} collective-permute-done((bf16[1536,128]{1,0:T(8,128)(2,1)S(1)}, bf16[1536,128]{1,0:T(8,128)(2,1)S(1)}, u32[]{:S(2)}, u32[]{:S(2)}) %collective-permute-start.3) | collective-permute-done | bytes 393248 | tf_op jit(solution)/shard_map/ppermute | solution.py:300
  58.2 5.3 %shard_map.55 = (bf16[6144,128]{1,0:T(8,128)(2,1)}, bf16[136,128]{1,0:T(8,128)(2,1)S(1)}, bf16[136,128]{1,0:T(8,128)(2,1)S(1)}) custom-call(s32[2]{0:T(128)S(1)} %pad_add_fusion.place_ref, bf16[136,6144]{1,0:T(8,128)(2,1)} %bitcast.37, bf16[136,6144]{1,0:T(8,128)(2,1)} %collective-permute-done.refs_1_, bf16[1536,128]{1,0:T(8,128)(2,1)S(1)} %collective-permute-done.2.refs_2_, ...), custom_call_target="tpu_custom_call" | custom-call | flops 30000001024 | bytes 6488064 | tf_op jit(solution)/shard_map/pallas_call | solution.py:93
  63.6 4.2 %collective-permute-start.5 = (bf16[136,128]{1,0:T(8,128)(2,1)S(1)}, bf16[136,128]{1,0:T(8,128)(2,1)S(1)}, u32[]{:S(2)}, u32[]{:S(2)}) collective-permute-start(bf16[136,128]{1,0:T(8,128)(2,1)S(1)} %get-tuple-element.35), channel_id=1, source_target_pairs={{0,1},{1,0},{2,3},{3,2},{4,5},{5,4},{6,7},{7,6},{8,9},{9,8},{10,11... | collective-permute-start | bytes 104456 | tf_op jit(solution)/shard_map/ppermute | solution.py:37
  70.1 9.1 %all-to-all-start.2 = ((bf16[64,2,128]{2,1,0:T(2,128)(2,1)}), bf16[64,2,128]{2,1,0:T(2,128)(2,1)S(1)}, u32[]{:S(2)}, u32[]{:S(2)}) async-start(bf16[64,2,128]{2,1,0:T(2,128)(2,1)} %bitcast.7), calls=%async_computation.2 | async-start | bytes 65536 | tf_op jit(solution)/shard_map/all_to_all | solution.py:277
  79.1 4.9 %collective-permute-start.8 = (bf16[1536,128]{1,0:T(8,128)(2,1)S(1)}, bf16[1536,128]{1,0:T(8,128)(2,1)S(1)}, u32[]{:S(2)}, u32[]{:S(2)}) collective-permute-start(bf16[1536,128]{1,0:T(8,128)(2,1)S(1)} %bitcast.21), channel_id=1, source_target_pairs={{0,32},{16,48},{32,0},{48,16},{1,33},{17,49},{33,1},{49,17},{2,34}... | collective-permute-start | bytes 1179656 | tf_op jit(solution)/shard_map/ppermute | solution.py:300
  84.1 2.7 %collective-permute-start.7 = (bf16[1536,128]{1,0:T(8,128)(2,1)S(1)}, bf16[1536,128]{1,0:T(8,128)(2,1)S(1)}, u32[]{:S(2)}, u32[]{:S(2)}) collective-permute-start(bf16[1536,128]{1,0:T(8,128)(2,1)S(1)} %bitcast.22), channel_id=1, source_target_pairs={{0,48},{16,0},{32,16},{48,32},{1,49},{17,1},{33,17},{49,33},{2,50}... | collective-permute-start | bytes 1179656 | tf_op jit(solution)/shard_map/ppermute | solution.py:300
  86.8 2.6 %collective-permute-start.6 = (bf16[1536,128]{1,0:T(8,128)(2,1)S(1)}, bf16[1536,128]{1,0:T(8,128)(2,1)S(1)}, u32[]{:S(2)}, u32[]{:S(2)}) collective-permute-start(bf16[1536,128]{1,0:T(8,128)(2,1)S(1)} %bitcast.23), channel_id=1, source_target_pairs={{0,16},{16,32},{32,48},{48,0},{1,17},{17,33},{33,49},{49,1},{2,18}... | collective-permute-start | bytes 1179656 | tf_op jit(solution)/shard_map/ppermute | solution.py:300
  90.1 10.2 %all-to-all-start.3 = ((bf16[64,2,128]{2,1,0:T(2,128)(2,1)}), bf16[64,2,128]{2,1,0:T(2,128)(2,1)S(1)}, u32[]{:S(2)}, u32[]{:S(2)}) async-start(bf16[64,2,128]{2,1,0:T(2,128)(2,1)} %bitcast.9), calls=%async_computation.3 | async-start | bytes 65536 | tf_op jit(solution)/shard_map/all_to_all | solution.py:277
  101.9 4.7 %shard_map.58 = (bf16[6144,128]{1,0:T(8,128)(2,1)S(1)}, f32[136,128]{1,0:T(8,128)S(1)}, f32[136,128]{1,0:T(8,128)S(1)}) custom-call(s32[2]{0:T(128)S(1)} %pad_add_fusion.place_ref, bf16[136,6144]{1,0:T(8,128)(2,1)} %bitcast.38, bf16[136,6144]{1,0:T(8,128)(2,1)} %collective-permute-done.refs_1_, bf16[136,6144]{1,0:T(8,128)(2,1)} %bitcast.40, ...), custom_call_target="tpu_custom_call" | custom-call | flops 30000001024 | bytes 6488064 | tf_op jit(solution)/shard_map/pallas_call | solution.py:93
  106.7 3.0 %collective-permute-start.9 = (f32[136,128]{1,0:T(8,128)S(1)}, f32[136,128]{1,0:T(8,128)S(1)}, u32[]{:S(2)}, u32[]{:S(2)}) collective-permute-start(f32[136,128]{1,0:T(8,128)S(1)} %get-tuple-element.39), channel_id=1, source_target_pairs={{0,1},{1,0},{2,3},{3,2},{4,5},{5,4},{6,7},{7,6},{8,9},{9,8},{10,11... | collective-permute-start | bytes 208904 | tf_op jit(solution)/shard_map/ppermute | solution.py:37
  112.2 10.1 %all-to-all-start.4 = ((bf16[64,2,128]{2,1,0:T(2,128)(2,1)}), bf16[64,2,128]{2,1,0:T(2,128)(2,1)S(1)}, u32[]{:S(2)}, u32[]{:S(2)}) async-start(bf16[64,2,128]{2,1,0:T(2,128)(2,1)} %bitcast.12), calls=%async_computation.4 | async-start | bytes 65536 | tf_op jit(solution)/shard_map/all_to_all | solution.py:277
  122.4 2.4 %collective-permute-start.11 = (bf16[6144,128]{1,0:T(8,128)(2,1)}, bf16[6144,128]{1,0:T(8,128)(2,1)}, u32[]{:S(2)}, u32[]{:S(2)}) collective-permute-start(bf16[6144,128]{1,0:T(8,128)(2,1)} %get-tuple-element.50.near_ref), channel_id=1, source_target_pairs={{0,1},{1,0},{2,3},{3,2},{4,5},{5,4},{6,7},{7,6},{8,9},{9,8},{10,11... | collective-permute-start | bytes 4718600 | tf_op jit(solution)/shard_map/ppermute | solution.py:37
  126.7 4.9 %all-to-all-done.4 = bf16[64,2,128]{2,1,0:T(2,128)(2,1)S(1)} async-done(((bf16[64,2,128]{2,1,0:T(2,128)(2,1)}), bf16[64,2,128]{2,1,0:T(2,128)(2,1)S(1)}, u32[]{:S(2)}, u32[]{:S(2)}) %all-to-all-start.4) | async-done | bytes 32800 | tf_op jit(solution)/shard_map/all_to_all | solution.py:277
  132.4 5.4 %all-to-all-start.5 = ((bf16[64,2,128]{2,1,0:T(2,128)(2,1)}), bf16[64,2,128]{2,1,0:T(2,128)(2,1)S(1)}, u32[]{:S(2)}, u32[]{:S(2)}) async-start(bf16[64,2,128]{2,1,0:T(2,128)(2,1)} %bitcast.14), calls=%async_computation.5 | async-start | bytes 65536 | tf_op jit(solution)/shard_map/all_to_all | solution.py:277
  144.6 2.5 %all-to-all-done.5 = bf16[64,2,128]{2,1,0:T(2,128)(2,1)S(1)} async-done(((bf16[64,2,128]{2,1,0:T(2,128)(2,1)}), bf16[64,2,128]{2,1,0:T(2,128)(2,1)S(1)}, u32[]{:S(2)}, u32[]{:S(2)}) %all-to-all-start.5) | async-done | bytes 32800 | tf_op jit(solution)/shard_map/all_to_all | solution.py:277
  147.9 4.8 %shard_map.64 = bf16[136,6144]{1,0:T(8,128)(2,1)} custom-call(s32[2]{0:T(128)S(1)} %pad_add_fusion.place_ref, f32[136,6144]{1,0:T(8,128)S(1)} %get-tuple-element.46.base, f32[136,128]{1,0:T(8,128)S(1)} %get-tuple-element.47.dk, f32[136,128]{1,0:T(8,128)S(1)} %get-tuple-element.48.dv, bf16[136,128]{1,0:T(8,128)(2,1)S(1)} %get-tuple-element.41.k_ref, ...), custom_call_target="tpu_custom_call" | custom-call | flops 427819008 | bytes 8159232 | tf_op jit(solution)/shard_map/pallas_call | solution.py:242
  (55 shorter events, 22.8 us)
Async XLA Ops:
  10.6 25.9 %all-to-all-start = ((bf16[64,24,128]{2,1,0:T(8,128)(2,1)}), bf16[64,24,128]{2,1,0:T(8,128)(2,1)S(1)}, u32[]{:S(2)}, u32[]{:S(2)}) async-start(bf16[64,24,128]{2,1,0:T(8,128)(2,1)} %broadcast_in_dim.6), calls=%async_computation | async-start | bytes 786432 | tf_op jit(solution)/shard_map/all_to_all | solution.py:297
  21.6 32.3 %collective-permute-start = (bf16[136,6144]{1,0:T(8,128)(2,1)}, bf16[136,6144]{1,0:T(8,128)(2,1)}, u32[]{:S(2)}, u32[]{:S(2)}) collective-permute-start(bf16[136,6144]{1,0:T(8,128)(2,1)} %bitcast.36), channel_id=1, source_target_pairs={{0,1},{1,0},{2,3},{3,2},{4,5},{5,4},{6,7},{7,6},{8,9},{9,8},{10,11... | collective-permute-start | bytes 5013512 | tf_op jit(solution)/shard_map/ppermute | solution.py:37
  24.1 29.7 %collective-permute-start.1 = (bf16[136,6144]{1,0:T(8,128)(2,1)}, bf16[136,6144]{1,0:T(8,128)(2,1)}, u32[]{:S(2)}, u32[]{:S(2)}) collective-permute-start(bf16[136,6144]{1,0:T(8,128)(2,1)} %bitcast.39), channel_id=1, source_target_pairs={{0,1},{1,0},{2,3},{3,2},{4,5},{5,4},{6,7},{7,6},{8,9},{9,8},{10,11... | collective-permute-start | bytes 5013512 | tf_op jit(solution)/shard_map/ppermute | solution.py:37
  36.6 17.3 %collective-permute-start.4 = (bf16[1536,128]{1,0:T(8,128)(2,1)S(1)}, bf16[1536,128]{1,0:T(8,128)(2,1)S(1)}, u32[]{:S(2)}, u32[]{:S(2)}) collective-permute-start(bf16[1536,128]{1,0:T(8,128)(2,1)S(1)} %bitcast.25), channel_id=1, source_target_pairs={{0,32},{16,48},{32,0},{48,16},{1,33},{17,49},{33,1},{49,17},{2,34}... | collective-permute-start | bytes 1179656 | tf_op jit(solution)/shard_map/ppermute | solution.py:300
  41.2 16.7 %collective-permute-start.3 = (bf16[1536,128]{1,0:T(8,128)(2,1)S(1)}, bf16[1536,128]{1,0:T(8,128)(2,1)S(1)}, u32[]{:S(2)}, u32[]{:S(2)}) collective-permute-start(bf16[1536,128]{1,0:T(8,128)(2,1)S(1)} %bitcast.26), channel_id=1, source_target_pairs={{0,48},{16,0},{32,16},{48,32},{1,49},{17,1},{33,17},{49,33},{2,50}... | collective-permute-start | bytes 1179656 | tf_op jit(solution)/shard_map/ppermute | solution.py:300
  44.0 14.3 %collective-permute-start.2 = (bf16[1536,128]{1,0:T(8,128)(2,1)S(1)}, bf16[1536,128]{1,0:T(8,128)(2,1)S(1)}, u32[]{:S(2)}, u32[]{:S(2)}) collective-permute-start(bf16[1536,128]{1,0:T(8,128)(2,1)S(1)} %bitcast.27), channel_id=1, source_target_pairs={{0,16},{16,32},{32,48},{48,0},{1,17},{17,33},{33,49},{49,1},{2,18}... | collective-permute-start | bytes 1179656 | tf_op jit(solution)/shard_map/ppermute | solution.py:300
  47.3 20.5 %all-to-all-start.1 = ((bf16[64,24,128]{2,1,0:T(8,128)(2,1)}), bf16[64,24,128]{2,1,0:T(8,128)(2,1)S(1)}, u32[]{:S(2)}, u32[]{:S(2)}) async-start(bf16[64,24,128]{2,1,0:T(8,128)(2,1)} %broadcast_in_dim.7), calls=%async_computation.1 | async-start | bytes 786432 | tf_op jit(solution)/shard_map/all_to_all | solution.py:297
  63.6 5.1 %collective-permute-start.5 = (bf16[136,128]{1,0:T(8,128)(2,1)S(1)}, bf16[136,128]{1,0:T(8,128)(2,1)S(1)}, u32[]{:S(2)}, u32[]{:S(2)}) collective-permute-start(bf16[136,128]{1,0:T(8,128)(2,1)S(1)} %get-tuple-element.35), channel_id=1, source_target_pairs={{0,1},{1,0},{2,3},{3,2},{4,5},{5,4},{6,7},{7,6},{8,9},{9,8},{10,11... | collective-permute-start | bytes 104456 | tf_op jit(solution)/shard_map/ppermute | solution.py:37
  70.1 40.5 %copy-start = (bf16[136,128]{1,0:T(8,128)(2,1)}, bf16[136,128]{1,0:T(8,128)(2,1)S(1)}, u32[]{:S(2)}) copy-start(bf16[136,128]{1,0:T(8,128)(2,1)S(1)} %get-tuple-element.42.v_ref) | copy-start | bytes 104452
  70.1 19.3 %all-to-all-start.2 = ((bf16[64,2,128]{2,1,0:T(2,128)(2,1)}), bf16[64,2,128]{2,1,0:T(2,128)(2,1)S(1)}, u32[]{:S(2)}, u32[]{:S(2)}) async-start(bf16[64,2,128]{2,1,0:T(2,128)(2,1)} %bitcast.7), calls=%async_computation.2 | async-start | bytes 65536 | tf_op jit(solution)/shard_map/all_to_all | solution.py:277
  79.1 21.1 %collective-permute-start.8 = (bf16[1536,128]{1,0:T(8,128)(2,1)S(1)}, bf16[1536,128]{1,0:T(8,128)(2,1)S(1)}, u32[]{:S(2)}, u32[]{:S(2)}) collective-permute-start(bf16[1536,128]{1,0:T(8,128)(2,1)S(1)} %bitcast.21), channel_id=1, source_target_pairs={{0,32},{16,48},{32,0},{48,16},{1,33},{17,49},{33,1},{49,17},{2,34}... | collective-permute-start | bytes 1179656 | tf_op jit(solution)/shard_map/ppermute | solution.py:300
  84.1 17.8 %collective-permute-start.7 = (bf16[1536,128]{1,0:T(8,128)(2,1)S(1)}, bf16[1536,128]{1,0:T(8,128)(2,1)S(1)}, u32[]{:S(2)}, u32[]{:S(2)}) collective-permute-start(bf16[1536,128]{1,0:T(8,128)(2,1)S(1)} %bitcast.22), channel_id=1, source_target_pairs={{0,48},{16,0},{32,16},{48,32},{1,49},{17,1},{33,17},{49,33},{2,50}... | collective-permute-start | bytes 1179656 | tf_op jit(solution)/shard_map/ppermute | solution.py:300
  86.8 15.2 %collective-permute-start.6 = (bf16[1536,128]{1,0:T(8,128)(2,1)S(1)}, bf16[1536,128]{1,0:T(8,128)(2,1)S(1)}, u32[]{:S(2)}, u32[]{:S(2)}) collective-permute-start(bf16[1536,128]{1,0:T(8,128)(2,1)S(1)} %bitcast.23), channel_id=1, source_target_pairs={{0,16},{16,32},{32,48},{48,0},{1,17},{17,33},{33,49},{49,1},{2,18}... | collective-permute-start | bytes 1179656 | tf_op jit(solution)/shard_map/ppermute | solution.py:300
  90.1 19.6 %all-to-all-start.3 = ((bf16[64,2,128]{2,1,0:T(2,128)(2,1)}), bf16[64,2,128]{2,1,0:T(2,128)(2,1)S(1)}, u32[]{:S(2)}, u32[]{:S(2)}) async-start(bf16[64,2,128]{2,1,0:T(2,128)(2,1)} %bitcast.9), calls=%async_computation.3 | async-start | bytes 65536 | tf_op jit(solution)/shard_map/all_to_all | solution.py:277
  106.7 18.1 %copy-start.3 = (bf16[6144,128]{1,0:T(8,128)(2,1)}, bf16[6144,128]{1,0:T(8,128)(2,1)S(1)}, u32[]{:S(2)}) copy-start(bf16[6144,128]{1,0:T(8,128)(2,1)S(1)} %get-tuple-element.45.near_ref) | copy-start | bytes 4718596
  106.7 3.9 %collective-permute-start.9 = (f32[136,128]{1,0:T(8,128)S(1)}, f32[136,128]{1,0:T(8,128)S(1)}, u32[]{:S(2)}, u32[]{:S(2)}) collective-permute-start(f32[136,128]{1,0:T(8,128)S(1)} %get-tuple-element.39), channel_id=1, source_target_pairs={{0,1},{1,0},{2,3},{3,2},{4,5},{5,4},{6,7},{7,6},{8,9},{9,8},{10,11... | collective-permute-start | bytes 208904 | tf_op jit(solution)/shard_map/ppermute | solution.py:37
  109.7 2.5 %copy-start.10 = (bf16[128,128]{1,0:T(8,128)(2,1)}, bf16[128,128]{1,0:T(8,128)(2,1)S(1)}, u32[]{:S(2)}) copy-start(bf16[128,128]{1,0:T(8,128)(2,1)S(1)} %shard_map.60.prior_ref) | copy-start | bytes 98308
  112.2 20.2 %copy-start.6 = (bf16[136,128]{1,0:T(8,128)(2,1)}, bf16[136,128]{1,0:T(8,128)(2,1)S(1)}, u32[]{:S(2)}) copy-start(bf16[136,128]{1,0:T(8,128)(2,1)S(1)} %get-tuple-element.43.q_ref) | copy-start | bytes 104452
  112.2 20.2 %copy-start.8 = (bf16[136,128]{1,0:T(8,128)(2,1)}, bf16[136,128]{1,0:T(8,128)(2,1)S(1)}, u32[]{:S(2)}) copy-start(bf16[136,128]{1,0:T(8,128)(2,1)S(1)} %get-tuple-element.44.attn_ref) | copy-start | bytes 104452
  112.2 19.4 %all-to-all-start.4 = ((bf16[64,2,128]{2,1,0:T(2,128)(2,1)}), bf16[64,2,128]{2,1,0:T(2,128)(2,1)S(1)}, u32[]{:S(2)}, u32[]{:S(2)}) async-start(bf16[64,2,128]{2,1,0:T(2,128)(2,1)} %bitcast.12), calls=%async_computation.4 | async-start | bytes 65536 | tf_op jit(solution)/shard_map/all_to_all | solution.py:277
  122.4 24.7 %collective-permute-start.11 = (bf16[6144,128]{1,0:T(8,128)(2,1)}, bf16[6144,128]{1,0:T(8,128)(2,1)}, u32[]{:S(2)}, u32[]{:S(2)}) collective-permute-start(bf16[6144,128]{1,0:T(8,128)(2,1)} %get-tuple-element.50.near_ref), channel_id=1, source_target_pairs={{0,1},{1,0},{2,3},{3,2},{4,5},{5,4},{6,7},{7,6},{8,9},{9,8},{10,11... | collective-permute-start | bytes 4718600 | tf_op jit(solution)/shard_map/ppermute | solution.py:37
  124.8 13.1 %collective-permute-start.10 = (bf16[6144,128]{1,0:T(8,128)(2,1)S(1)}, bf16[6144,128]{1,0:T(8,128)(2,1)}, u32[]{:S(2)}, u32[]{:S(2)}) collective-permute-start(bf16[6144,128]{1,0:T(8,128)(2,1)S(1)} %get-tuple-element.45.near_ref), channel_id=1, source_target_pairs={{0,1},{1,0},{2,3},{3,2},{4,5},{5,4},{6,7},{7,6},{8,9},{9,8},{10,11... | collective-permute-start | bytes 4718600 | tf_op jit(solution)/shard_map/ppermute | solution.py:37
  132.4 14.7 %all-to-all-start.5 = ((bf16[64,2,128]{2,1,0:T(2,128)(2,1)}), bf16[64,2,128]{2,1,0:T(2,128)(2,1)S(1)}, u32[]{:S(2)}, u32[]{:S(2)}) async-start(bf16[64,2,128]{2,1,0:T(2,128)(2,1)} %bitcast.14), calls=%async_computation.5 | async-start | bytes 65536 | tf_op jit(solution)/shard_map/all_to_all | solution.py:277
  138.6 1.4 copy-start.4
  (6 other events, 4.7 us)

commit v5 on v3

v5 whole, which is shorter than its diff:
```python
import functools

import jax
import jax.numpy as jnp
from jax import lax
from jax.experimental import pallas as pl
from jax.experimental.pallas import tpu as pltpu
from jax.sharding import Mesh
from jax.sharding import PartitionSpec as P

SEQ = ("x", "z", "core")
DP_SEQ = ("dp", "x", "z", "core")
ROWS = ("dp", "z")
BF16 = jnp.bfloat16
F32 = jnp.float32
LIMIT = 16 * 1024 * 1024
LONG = 30_000_000_000
SMEM = pl.BlockSpec(memory_space=pltpu.SMEM)
VMEM = pl.BlockSpec(memory_space=pltpu.VMEM)


def contract(left, right, left_dim, right_dim):
    return lax.dot_general(
        left, right, (((left_dim,), (right_dim,)), ((), ())), preferred_element_type=F32
    )


def cost(flops, moved):
    return pl.CostEstimate(flops=flops, bytes_accessed=moved, transcendentals=0)


def after(value, *events):
    return lax.optimization_barrier((value, *events))[0]


def core_swap(block):
    return lax.ppermute(block, "core", [(0, 1), (1, 0)])


def in_hbm(*values):
    return [pltpu.with_memory_space_constraint(v, pltpu.HBM) for v in values]


def project_kernel(shifts, place_ref, *refs):
    tokens, blocks, outs, scratch = refs[:-11], refs[-11:-7], refs[-7:-4], refs[-4:]
    weight_ref, own_ref, send_ref = outs
    own_held, far_held, own_sem, far_sem = scratch
    rows = weight_ref.shape[0] // 32

    def products(own, far):
        own_copy = pltpu.make_async_copy(own, own_held, own_sem)
        far_copy = pltpu.make_async_copy(far, far_held, far_sem)
        own_copy.start()
        far_copy.start()
        for k, ref in zip(shifts, blocks):
            source = lax.rem(place_ref[0] - k + 4, 4)
            for p in range(8):
                at = pl.multiple_of((p * 4 + source) * rows, 64)
                weight_ref[pl.ds(at, rows), :] = ref[p * rows : (p + 1) * rows, :]
        own_copy.wait()
        own_ref[...] = contract(own_held[...], weight_ref[...], 1, 0).astype(own_ref.dtype)
        far_copy.wait()
        send_ref[...] = contract(far_held[...], weight_ref[...], 1, 0).astype(send_ref.dtype)

    if len(tokens) == 2:
        products(*tokens)
    else:
        pl.when(place_ref[1] == 0)(lambda: products(*tokens[:2]))
        pl.when(place_ref[1] != 0)(lambda: products(*tokens[2:]))


def project(place, tokens, blocks, dtype):
    count, depth = tokens[0].shape
    row = jax.ShapeDtypeStruct((count, 128), dtype)
    return pl.pallas_call(
        functools.partial(project_kernel, tuple(blocks)),
        out_shape=[jax.ShapeDtypeStruct((depth, 128), BF16), row, row],
        in_specs=[SMEM] + [pl.BlockSpec(memory_space=pl.ANY)] * len(tokens) + [VMEM] * 4,
        out_specs=[VMEM] * 3,
        scratch_shapes=[pltpu.VMEM((count, depth), BF16)] * 2 + [pltpu.SemaphoreType.DMA] * 2,
        compiler_params=pltpu.CompilerParams(vmem_limit_bytes=LIMIT),
        cost_estimate=cost(LONG, 4 * count * depth + 4 * depth * 128),
    )(place, *in_hbm(*tokens), *blocks.values())


def state_kernel(place_ref, own_ref, recv_ref, key_ref, value_ref, state_ref):
    own, recv = own_ref[...], recv_ref[...]
    first = place_ref[1] == 0
    keys, values = jnp.where(first, own, recv), jnp.where(first, recv, own)
    key_ref[...] = keys
    value_ref[...] = values
    state_ref[...] = contract(keys, values, 0, 0).astype(BF16)


def keys_values_state(place, own, recv):
    row = jax.ShapeDtypeStruct(own.shape, BF16)
    return pl.pallas_call(
        state_kernel,
        out_shape=[row, row, jax.ShapeDtypeStruct((128, 128), BF16)],
        in_specs=[SMEM] + [VMEM] * 2,
        out_specs=[VMEM] * 3,
        compiler_params=pltpu.CompilerParams(vmem_limit_bytes=LIMIT),
        cost_estimate=cost(2 * own.size * 128, 8 * own.size),
    )(place, own, recv)


def gate_kernel(in_ref, out_ref):
    out_ref[...] = in_ref[...]


def gate(value):
    return pl.pallas_call(
        gate_kernel,
        out_shape=jax.ShapeDtypeStruct(value.shape, value.dtype),
        in_specs=[VMEM],
        out_specs=VMEM,
        compiler_params=pltpu.CompilerParams(vmem_limit_bytes=LIMIT),
        cost_estimate=cost(LONG, 4 * value.size),
    )(value)


def causal_of(count):
    rows = lax.broadcasted_iota(jnp.int32, (count, count), 0)
    return rows >= lax.broadcasted_iota(jnp.int32, (count, count), 1)


def grad_kernel(
    place_ref, near_ref, far_ref, k_ref, v_ref, prior_ref, gain_ref,
    q_ref, attn_ref, state_ref,
):
    first = place_ref[1] == 0
    near, far = near_ref[...], far_ref[...]
    queries = jnp.where(first, near, far).astype(BF16)
    head_grad = jnp.where(first, far, near)
    q_ref[...] = queries
    scores = contract(queries, k_ref[...], 1, 1)
    scores = jnp.where(causal_of(scores.shape[0]), scores, 0.0).astype(BF16)
    attended = contract(scores, v_ref[...], 1, 0) + contract(queries, prior_ref[...], 1, 0)
    inv_rms = lax.rsqrt(jnp.mean(attended * attended, axis=-1, keepdims=True) + 1e-06)
    scaled = gain_ref[...] * head_grad
    mean = jnp.mean(attended * scaled, axis=-1, keepdims=True)
    attn_grad = inv_rms * scaled - attended * (inv_rms * inv_rms * inv_rms) * mean
    attn_grad = attn_grad.astype(BF16)
    attn_ref[...] = attn_grad
    state_ref[...] = contract(queries, attn_grad, 0, 0).astype(BF16)


def attention_grad(place, near, far, keys, values, prior, gain):
    count = keys.shape[0]
    row = jax.ShapeDtypeStruct((count, 128), BF16)
    return pl.pallas_call(
        grad_kernel,
        out_shape=[
            row,
            row,
            jax.ShapeDtypeStruct((128, 128), BF16),
        ],
        in_specs=[SMEM] + [VMEM] * 6,
        out_specs=[VMEM] * 3,
        compiler_params=pltpu.CompilerParams(vmem_limit_bytes=LIMIT),
        cost_estimate=cost(LONG, 16 * count * 128),
    )(place, near, far, keys, values, prior, gain)


def inner_kernel(place_ref, *refs):
    rows_any, (near_any, far_any), outs, scratch = refs[:5], refs[5:7], refs[7:10], refs[10:]
    base_ref, dk_ref, dv_ref = outs
    q_ref, k_ref, v_ref, attn_ref, prior_ref, weight_ref, row_sems, weight_sem = scratch

    def body(weight_any):
        weight_copy = pltpu.make_async_copy(weight_any, weight_ref, weight_sem)
        copies = [
            pltpu.make_async_copy(source, target, row_sems.at[i])
            for i, (source, target) in enumerate(zip(rows_any, scratch[:5]))
        ]
        for copy in copies:
            copy.start()
        weight_copy.start()
        for copy in copies:
            copy.wait()
        attn_grad = attn_ref[...]
        causal = causal_of(attn_grad.shape[0])
        scores = contract(q_ref[...], k_ref[...], 1, 1)
        scores = jnp.where(causal, scores, 0.0).astype(BF16)
        prob = contract(attn_grad, v_ref[...], 1, 1)
        prob = jnp.where(causal, prob, 0.0).astype(BF16)
        query_grad = contract(prob, k_ref[...], 1, 0) + contract(attn_grad, prior_ref[...], 1, 1)
        query_grad = query_grad.astype(BF16)
        dk_ref[...] = contract(prob, q_ref[...], 0, 0)
        dv_ref[...] = contract(scores, attn_grad, 0, 0)
        weight_copy.wait()
        part = weight_ref.shape[0] // 4
        for i in range(4):
            at = slice(i * part, (i + 1) * part)
            base_ref[:, at] = contract(query_grad, weight_ref[at, :], 1, 1)

    pl.when(place_ref[1] == 0)(lambda: body(near_any))
    pl.when(place_ref[1] != 0)(lambda: body(far_any))


def inner_grads(place, queries, keys, values, attn_grad, prior, near, far):
    count, depth = queries.shape[0], near.shape[0]
    row = pltpu.VMEM((count, 128), BF16)
    return pl.pallas_call(
        inner_kernel,
        out_shape=[
            jax.ShapeDtypeStruct((count, depth), F32),
            jax.ShapeDtypeStruct((count, 128), F32),
            jax.ShapeDtypeStruct((count, 128), F32),
        ],
        in_specs=[SMEM] + [pl.BlockSpec(memory_space=pl.ANY)] * 7,
        out_specs=[VMEM] * 3,
        scratch_shapes=[
            *[row] * 4,
            pltpu.VMEM((128, 128), BF16),
            pltpu.VMEM((depth, 128), BF16),
            pltpu.SemaphoreType.DMA((5,)),
            pltpu.SemaphoreType.DMA,
        ],
        compiler_params=pltpu.CompilerParams(vmem_limit_bytes=LIMIT),
        cost_estimate=cost(LONG, 4 * count * depth + 4 * depth * 128),
    )(place, *in_hbm(queries, keys, values, attn_grad, prior, near, far))


def output_kernel(
    place_ref, base, dk, dv, k_any, v_any, later, near_any, far_any, out_any,
    k_ref, v_ref, near_ref, far_ref, out_ref, row_sems, weight_sems, out_sems,
):
    steps, _, part = out_ref.shape
    rows = [
        pltpu.make_async_copy(k_any, k_ref, row_sems.at[0]),
        pltpu.make_async_copy(v_any, v_ref, row_sems.at[1]),
    ]
    weights = []
    for i in range(steps):
        at = pl.ds(i * part, part)
        for n, (source, target) in enumerate(((near_any, near_ref), (far_any, far_ref))):
            weights.append(
                pltpu.make_async_copy(source.at[at], target.at[at], weight_sems.at[2 * i + n])
            )
    for copy in rows + weights:
        copy.start()
    for copy in rows:
        copy.wait()
    first = place_ref[1] == 0
    key_grad = (dk[...] + contract(v_ref[...], later[...], 1, 1)).astype(BF16)
    value_grad = (dv[...] + contract(k_ref[...], later[...], 1, 0)).astype(BF16)
    near_grad = jnp.where(first, key_grad, value_grad)
    far_grad = jnp.where(first, value_grad, key_grad)
    joined = jnp.concatenate([near_grad, far_grad], axis=1)
    outs = []
    for i in range(steps):
        weights[2 * i].wait()
        weights[2 * i + 1].wait()
        at = slice(i * part, (i + 1) * part)
        weight = jnp.concatenate([near_ref[at, :], far_ref[at, :]], axis=1)
        out_ref[i] = (base[:, at] + contract(joined, weight, 1, 1)).astype(BF16)
        copy = pltpu.make_async_copy(
            out_ref.at[i], out_any.at[:, pl.ds(i * part, part)], out_sems.at[i]
        )
        copy.start()
        outs.append(copy)
    for copy in outs:
        copy.wait()


def output(place, base, dk, dv, keys, values, later, near, far):
    count, depth = base.shape
    steps = 4
    anywhere = pl.BlockSpec(memory_space=pl.ANY)
    return pl.pallas_call(
        output_kernel,
        out_shape=jax.ShapeDtypeStruct((count, depth), BF16),
        in_specs=[SMEM] + [VMEM] * 3 + [anywhere] * 2 + [VMEM] + [anywhere] * 2,
        out_specs=anywhere,
        scratch_shapes=[
            pltpu.VMEM((count, 128), BF16),
            pltpu.VMEM((count, 128), BF16),
            pltpu.VMEM((depth, 128), BF16),
            pltpu.VMEM((depth, 128), BF16),
            pltpu.VMEM((steps, count, depth // steps), BF16),
            pltpu.SemaphoreType.DMA((2,)),
            pltpu.SemaphoreType.DMA((2 * steps,)),
            pltpu.SemaphoreType.DMA((steps,)),
        ],
        compiler_params=pltpu.CompilerParams(vmem_limit_bytes=LIMIT),
        cost_estimate=cost(4 * count * depth * 128, 4 * depth * 128 + 6 * count * depth),
    )(place, base, dk, dv, *in_hbm(keys, values), later, *in_hbm(near, far))


def sums_kernel(reverse, in_ref, out_ref):
    each = in_ref.shape[0] // 64
    to = lax.broadcasted_iota(jnp.int32, (128, 128), 0)
    frm = lax.broadcasted_iota(jnp.int32, (128, 128), 1)
    others = (frm // each > to // each) if reverse else (frm // each < to // each)
    mask = jnp.where(others & (frm % each == to % each), 1.0, 0.0).astype(BF16)
    out_ref[...] = contract(mask, in_ref[...], 1, 0).astype(BF16)


def sums_of(pieces, reverse):
    return pl.pallas_call(
        functools.partial(sums_kernel, reverse),
        out_shape=jax.ShapeDtypeStruct(pieces.shape, BF16),
        in_specs=[VMEM],
        out_specs=VMEM,
        compiler_params=pltpu.CompilerParams(vmem_limit_bytes=LIMIT),
        cost_estimate=cost(LONG, 4 * pieces.size),
    )(pieces)


def exchange(state):
    peers, head = lax.axis_size(SEQ), state.shape[1]
    pieces = state.reshape(peers, -1, head)
    return lax.all_to_all(pieces, SEQ, 0, 0, tiled=True).reshape(state.shape)


def per_device(inputs, w_project, w_output, norm_gain, out_grad):
    tokens = inputs[0]
    grads_in = out_grad[0]
    head = w_output.shape[1]
    dps, zs, xs = lax.axis_size("dp"), lax.axis_size("z"), lax.axis_size("x")
    place = jnp.stack([lax.axis_index("x"), lax.axis_index("core")]).astype(jnp.int32)
    on_first = lax.axis_index("core") == 0

    rows = jnp.concatenate([w_project.reshape(-1, 3 * head), w_output], axis=1)
    rows = lax.all_gather(rows, "core", axis=0, tiled=True)
    kv_rows = jnp.where(on_first, rows[:, head : 2 * head], rows[:, 2 * head : 3 * head])
    qo_rows = jnp.where(on_first, rows[:, :head], rows[:, 3 * head :])

    def copied(block):
        return jnp.broadcast_to(block[None], (dps * zs, *block.shape))

    def over_planes(copies):
        return lax.all_to_all(copies, ROWS, 0, 0, tiled=True).reshape(-1, head)

    def over_x(block):
        shifts = {k: lax.ppermute(block, "x", [(i, (i + k) % xs) for i in range(xs)]) for k in (2, 1, 3)}
        return {1: shifts[1], 3: shifts[3], 2: shifts[2], 0: block}

    kv_copies = copied(kv_rows)
    tokens_far = core_swap(after(tokens, kv_copies))
    grads_far = core_swap(after(grads_in, kv_copies))
    kv_plane = over_planes(kv_copies)
    qo_plane = over_planes(copied(gate(after(qo_rows, kv_plane))))
    tokens_far = after(tokens_far, grads_far)
    kv_near, own, send = project(place, (tokens, tokens_far), over_x(kv_plane), BF16)
    own, qo_plane = lax.optimization_barrier((own, qo_plane))
    keys, values, local_state = keys_values_state(place, own, core_swap(send))

    qo = over_x(after(qo_plane, local_state))
    prior_state = gate(exchange(sums_of(exchange(local_state), False)))
    qo_near, own, send = project(
        place, (tokens, tokens_far, grads_in, grads_far), qo, F32
    )
    recv = after(core_swap(send), prior_state)
    queries, attn_grad, local_grad = attention_grad(
        place, own, recv, keys, values, prior_state, norm_gain.reshape(1, head)
    )
    kv_far = core_swap(kv_near)
    grad_pieces = exchange(local_grad)
    qo_far = core_swap(qo_near)
    base, *grads = inner_grads(
        place, queries, keys, values, attn_grad, prior_state, qo_near, qo_far
    )
    later_state = exchange(sums_of(grad_pieces, True))
    result = output(place, base, *grads, keys, values, later_state, kv_near, kv_far)
    return result[None]


def solution(mesh):
    split = Mesh(mesh.devices.reshape(mesh.shape["dp"], 4, 8, 2), DP_SEQ)
    in_specs = (P("dp", SEQ, None), P(DP_SEQ, None, None), P(DP_SEQ, None), P(), P("dp", SEQ, None))
    out_specs = P("dp", SEQ, None)
    return jax.shard_map(
        per_device, mesh=split, in_specs=in_specs, out_specs=out_specs, check_vma=False
    )
```

time: 164 us -> 152 us (0.927)
  blocking collectives: 27.6 us -> 8.36 us
  local copies, waits for them, and re-layouts: 16.9 us -> 2.97 us
  waiting for transfers between devices: 16.3 us -> 30.2 us
  starting transfers between devices: 82.9 us -> 88.5 us
    all_to_all x1 -> x0, blocking collectives: 25.8 us -> none  [over_planes(): return lax.all_to_all(copies, ROWS, 0, 0, tiled=True).reshape(-1, head)]
    unnamed x45 -> x17, local copies, waits for them, and re-layouts: 16.1 us -> 1.37 us
    all_to_all x1 -> x2, waiting for transfers between devices: 0.01 us -> 11.6 us  [over_planes(): return lax.all_to_all(copies, ROWS, 0, 0, tiled=True).reshape(-1, head)]
    all_to_all x1 -> x2, starting transfers between devices: 6.43 us -> 17.4 us  [over_planes(): return lax.all_to_all(copies, ROWS, 0, 0, tiled=True).reshape(-1, head)]
    all_to_all x4, waiting for transfers between devices: 4.96 us -> 12.6 us  [exchange(): return lax.all_to_all(pieces, SEQ, 0, 0, tiled=True).reshape(state.shape)]
    ppermute x6, starting transfers between devices: 23.1 us -> 16 us  [core_swap(): return lax.ppermute(block, 'core', [(0, 1), (1, 0)])]
    all_gather x1, blocking collectives: 1.82 us -> 8.36 us  [per_device(): rows = lax.all_gather(rows, 'core', axis=0, tiled=True)]
    ppermute x6, waiting for transfers between devices: 9.71 us -> 6.01 us  [over_x(): lax.ppermute(block, 'x', [(i, (i + k) % xs) for i in range(xs)])]
  transfers between devices with their start and end apart: 17 -> 18, of which waited for: 7 -> 9; matrix products, arithmetic and copies ran while one was open for 1% -> 1% of each run, Pallas kernels for 6% -> 8%
where the time goes in v5:
time: 152 us; the launch traced here: 151 us
  starting transfers between devices  88.5 us (58%)
  waiting for transfers between devices  30.2 us (20%)
  Pallas kernels  19.4 us (13%)
  blocking collectives  8.36 us (6%)
  local copies, waits for them, and re-layouts  2.97 us (2%)
    all_to_all x4, starting transfers between devices, exchange(): return lax.all_to_all(pieces, SEQ, 0, 0, tiled=True).reshape(state.shape)  34.9 us
    ppermute x6, starting transfers between devices, over_x(): lax.ppermute(block, 'x', [(i, (i + k) % xs) for i in range(xs)])  20.1 us
    all_to_all x2, starting transfers between devices, over_planes(): return lax.all_to_all(copies, ROWS, 0, 0, tiled=True).reshape(-1, head)  17.4 us
    ppermute x6, starting transfers between devices, core_swap(): return lax.ppermute(block, 'core', [(0, 1), (1, 0)])  16 us
    all_to_all x4, waiting for transfers between devices, exchange(): return lax.all_to_all(pieces, SEQ, 0, 0, tiled=True).reshape(state.shape)  12.6 us
    all_to_all x2, waiting for transfers between devices, over_planes(): return lax.all_to_all(copies, ROWS, 0, 0, tiled=True).reshape(-1, head)  11.6 us
    all_gather x1, blocking collectives, per_device(): rows = lax.all_gather(rows, 'core', axis=0, tiled=True)  8.36 us
    pallas_call x2, Pallas kernels, project(): pl.pallas_call(functools.partial(project_kernel, tuple(blocks)), out_shap...  7.05 us
  transfers between devices with their start and end apart: 18, of which 9 were waited for; matrix products, arithmetic and copies ran while one was open for 1% of the time, Pallas kernels for 8%

profile of v5, /device:TPU:1, one launch (start us, length us, event | category | flops | bytes accessed | tf_op | source)
XLA Modules:
  0.0 150.7 jit_solution(15767869006922860888)
XLA Ops:
  1.4 8.4 %all-gather = bf16[2,12,512]{2,1,0:T(8,128)(2,1)S(1)} all-gather(bf16[1,12,512]{2,1,0:T(8,128)(2,1)S(1)} %maximum_bitcast_fusion), channel_id=1, replica_groups=mesh['dp'=8,'x'=4,'z'=8,'core'=2] {'core'}, dimensions={0}, use_global_device_ids=true | all-gather | bytes 36864 | tf_op jit(solution)/shard_map/all_gather | solution.py:326
  10.6 10.9 %all-to-all-start = ((bf16[64,24,128]{2,1,0:T(8,128)(2,1)}), bf16[64,24,128]{2,1,0:T(8,128)(2,1)S(1)}, u32[]{:S(2)}, u32[]{:S(2)}) async-start(bf16[64,24,128]{2,1,0:T(8,128)(2,1)} %broadcast_in_dim.6), calls=%async_computation | async-start | bytes 786432 | tf_op jit(solution)/shard_map/all_to_all | solution.py:334
  21.6 2.5 %collective-permute-start = (bf16[136,6144]{1,0:T(8,128)(2,1)}, bf16[136,6144]{1,0:T(8,128)(2,1)}, u32[]{:S(2)}, u32[]{:S(2)}) collective-permute-start(bf16[136,6144]{1,0:T(8,128)(2,1)} %bitcast.36), channel_id=1, source_target_pairs={{0,1},{1,0},{2,3},{3,2},{4,5},{5,4},{6,7},{7,6},{8,9},{9,8},{10,11... | collective-permute-start | bytes 5013512 | tf_op jit(solution)/shard_map/ppermute | solution.py:37
  26.1 10.5 %all-to-all-done = bf16[64,24,128]{2,1,0:T(8,128)(2,1)S(1)} async-done(((bf16[64,24,128]{2,1,0:T(8,128)(2,1)}), bf16[64,24,128]{2,1,0:T(8,128)(2,1)S(1)}, u32[]{:S(2)}, u32[]{:S(2)}) %all-to-all-start) | async-done | bytes 393248 | tf_op jit(solution)/shard_map/all_to_all | solution.py:334
  36.6 4.6 %collective-permute-start.4 = (bf16[1536,128]{1,0:T(8,128)(2,1)S(1)}, bf16[1536,128]{1,0:T(8,128)(2,1)S(1)}, u32[]{:S(2)}, u32[]{:S(2)}) collective-permute-start(bf16[1536,128]{1,0:T(8,128)(2,1)S(1)} %bitcast.25), channel_id=1, source_target_pairs={{0,32},{16,48},{32,0},{48,16},{1,33},{17,49},{33,1},{49,17},{2,34}... | collective-permute-start | bytes 1179656 | tf_op jit(solution)/shard_map/ppermute | solution.py:337
  41.2 2.8 %collective-permute-start.3 = (bf16[1536,128]{1,0:T(8,128)(2,1)S(1)}, bf16[1536,128]{1,0:T(8,128)(2,1)S(1)}, u32[]{:S(2)}, u32[]{:S(2)}) collective-permute-start(bf16[1536,128]{1,0:T(8,128)(2,1)S(1)} %bitcast.26), channel_id=1, source_target_pairs={{0,48},{16,0},{32,16},{48,32},{1,49},{17,1},{33,17},{49,33},{2,50}... | collective-permute-start | bytes 1179656 | tf_op jit(solution)/shard_map/ppermute | solution.py:337
  44.0 2.5 %collective-permute-start.2 = (bf16[1536,128]{1,0:T(8,128)(2,1)S(1)}, bf16[1536,128]{1,0:T(8,128)(2,1)S(1)}, u32[]{:S(2)}, u32[]{:S(2)}) collective-permute-start(bf16[1536,128]{1,0:T(8,128)(2,1)S(1)} %bitcast.27), channel_id=1, source_target_pairs={{0,16},{16,32},{32,48},{48,0},{1,17},{17,33},{33,49},{49,1},{2,18}... | collective-permute-start | bytes 1179656 | tf_op jit(solution)/shard_map/ppermute | solution.py:337
  47.3 6.5 %all-to-all-start.1 = ((bf16[64,24,128]{2,1,0:T(8,128)(2,1)}), bf16[64,24,128]{2,1,0:T(8,128)(2,1)S(1)}, u32[]{:S(2)}, u32[]{:S(2)}) async-start(bf16[64,24,128]{2,1,0:T(8,128)(2,1)} %broadcast_in_dim.7), calls=%async_computation.1 | async-start | bytes 786432 | tf_op jit(solution)/shard_map/all_to_all | solution.py:334
  53.9 4.1 %collective-permute-done.3.refs_3_ = bf16[1536,128]{1,0:T(8,128)(2,1)S(1)} collective-permute-done((bf16[1536,128]{1,0:T(8,128)(2,1)S(1)}, bf16[1536,128]{1,0:T(8,128)(2,1)S(1)}, u32[]{:S(2)}, u32[]{:S(2)}) %collective-permute-start.3) | collective-permute-done | bytes 393248 | tf_op jit(solution)/shard_map/ppermute | solution.py:337
  58.2 3.8 %shard_map.55 = (bf16[6144,128]{1,0:T(8,128)(2,1)}, bf16[136,128]{1,0:T(8,128)(2,1)S(1)}, bf16[136,128]{1,0:T(8,128)(2,1)S(1)}) custom-call(s32[2]{0:T(128)S(1)} %pad_add_fusion.place_ref, bf16[136,6144]{1,0:T(8,128)(2,1)} %bitcast.37, bf16[136,6144]{1,0:T(8,128)(2,1)} %collective-permute-done.refs_1_, bf16[1536,128]{1,0:T(8,128)(2,1)S(1)} %collective-permute-done.2.refs_2_, ...), custom_call_target="tpu_custom_call" | custom-call | flops 30000001024 | bytes 6488064 | tf_op jit(solution)/shard_map/pallas_call | solution.py:75
  62.0 4.3 %collective-permute-start.5 = (bf16[136,128]{1,0:T(8,128)(2,1)S(1)}, bf16[136,128]{1,0:T(8,128)(2,1)S(1)}, u32[]{:S(2)}, u32[]{:S(2)}) collective-permute-start(bf16[136,128]{1,0:T(8,128)(2,1)S(1)} %get-tuple-element.35), channel_id=1, source_target_pairs={{0,1},{1,0},{2,3},{3,2},{4,5},{5,4},{6,7},{7,6},{8,9},{9,8},{10,11... | collective-permute-start | bytes 104456 | tf_op jit(solution)/shard_map/ppermute | solution.py:37
  68.8 10.4 %all-to-all-start.2 = ((bf16[64,2,128]{2,1,0:T(2,128)(2,1)}), bf16[64,2,128]{2,1,0:T(2,128)(2,1)S(1)}, u32[]{:S(2)}, u32[]{:S(2)}) async-start(bf16[64,2,128]{2,1,0:T(2,128)(2,1)} %bitcast.7), calls=%async_computation.2 | async-start | bytes 65536 | tf_op jit(solution)/shard_map/all_to_all | solution.py:314
  79.1 4.9 %collective-permute-start.8 = (bf16[1536,128]{1,0:T(8,128)(2,1)S(1)}, bf16[1536,128]{1,0:T(8,128)(2,1)S(1)}, u32[]{:S(2)}, u32[]{:S(2)}) collective-permute-start(bf16[1536,128]{1,0:T(8,128)(2,1)S(1)} %bitcast.21), channel_id=1, source_target_pairs={{0,32},{16,48},{32,0},{48,16},{1,33},{17,49},{33,1},{49,17},{2,34}... | collective-permute-start | bytes 1179656 | tf_op jit(solution)/shard_map/ppermute | solution.py:337
  84.1 2.7 %collective-permute-start.7 = (bf16[1536,128]{1,0:T(8,128)(2,1)S(1)}, bf16[1536,128]{1,0:T(8,128)(2,1)S(1)}, u32[]{:S(2)}, u32[]{:S(2)}) collective-permute-start(bf16[1536,128]{1,0:T(8,128)(2,1)S(1)} %bitcast.22), channel_id=1, source_target_pairs={{0,48},{16,0},{32,16},{48,32},{1,49},{17,1},{33,17},{49,33},{2,50}... | collective-permute-start | bytes 1179656 | tf_op jit(solution)/shard_map/ppermute | solution.py:337
  86.8 2.6 %collective-permute-start.6 = (bf16[1536,128]{1,0:T(8,128)(2,1)S(1)}, bf16[1536,128]{1,0:T(8,128)(2,1)S(1)}, u32[]{:S(2)}, u32[]{:S(2)}) collective-permute-start(bf16[1536,128]{1,0:T(8,128)(2,1)S(1)} %bitcast.23), channel_id=1, source_target_pairs={{0,16},{16,32},{32,48},{48,0},{1,17},{17,33},{33,49},{49,1},{2,18}... | collective-permute-start | bytes 1179656 | tf_op jit(solution)/shard_map/ppermute | solution.py:337
  90.1 10.2 %all-to-all-start.3 = ((bf16[64,2,128]{2,1,0:T(2,128)(2,1)}), bf16[64,2,128]{2,1,0:T(2,128)(2,1)S(1)}, u32[]{:S(2)}, u32[]{:S(2)}) async-start(bf16[64,2,128]{2,1,0:T(2,128)(2,1)} %bitcast.9), calls=%async_computation.3 | async-start | bytes 65536 | tf_op jit(solution)/shard_map/all_to_all | solution.py:314
  101.9 3.3 %shard_map.58 = (bf16[6144,128]{1,0:T(8,128)(2,1)S(1)}, f32[136,128]{1,0:T(8,128)S(1)}, f32[136,128]{1,0:T(8,128)S(1)}) custom-call(s32[2]{0:T(128)S(1)} %pad_add_fusion.place_ref, bf16[136,6144]{1,0:T(8,128)(2,1)} %bitcast.38, bf16[136,6144]{1,0:T(8,128)(2,1)} %collective-permute-done.refs_1_, bf16[136,6144]{1,0:T(8,128)(2,1)} %bitcast.40, ...), custom_call_target="tpu_custom_call" | custom-call | flops 30000001024 | bytes 6488064 | tf_op jit(solution)/shard_map/pallas_call | solution.py:75
  105.2 3.0 %collective-permute-start.9 = (f32[136,128]{1,0:T(8,128)S(1)}, f32[136,128]{1,0:T(8,128)S(1)}, u32[]{:S(2)}, u32[]{:S(2)}) collective-permute-start(f32[136,128]{1,0:T(8,128)S(1)} %get-tuple-element.39), channel_id=1, source_target_pairs={{0,1},{1,0},{2,3},{3,2},{4,5},{5,4},{6,7},{7,6},{8,9},{9,8},{10,11... | collective-permute-start | bytes 208904 | tf_op jit(solution)/shard_map/ppermute | solution.py:37
  111.9 9.0 %all-to-all-start.4 = ((bf16[64,2,128]{2,1,0:T(2,128)(2,1)}), bf16[64,2,128]{2,1,0:T(2,128)(2,1)S(1)}, u32[]{:S(2)}, u32[]{:S(2)}) async-start(bf16[64,2,128]{2,1,0:T(2,128)(2,1)} %bitcast.12), calls=%async_computation.4 | async-start | bytes 65536 | tf_op jit(solution)/shard_map/all_to_all | solution.py:314
  125.3 4.9 %all-to-all-done.4 = bf16[64,2,128]{2,1,0:T(2,128)(2,1)S(1)} async-done(((bf16[64,2,128]{2,1,0:T(2,128)(2,1)}), bf16[64,2,128]{2,1,0:T(2,128)(2,1)S(1)}, u32[]{:S(2)}, u32[]{:S(2)}) %all-to-all-start.4) | async-done | bytes 32800 | tf_op jit(solution)/shard_map/all_to_all | solution.py:314
  131.0 5.4 %all-to-all-start.5 = ((bf16[64,2,128]{2,1,0:T(2,128)(2,1)}), bf16[64,2,128]{2,1,0:T(2,128)(2,1)S(1)}, u32[]{:S(2)}, u32[]{:S(2)}) async-start(bf16[64,2,128]{2,1,0:T(2,128)(2,1)} %bitcast.14), calls=%async_computation.5 | async-start | bytes 65536 | tf_op jit(solution)/shard_map/all_to_all | solution.py:314
  136.4 2.9 %shard_map.62 = (f32[136,6144]{1,0:T(8,128)S(1)}, f32[136,128]{1,0:T(8,128)S(1)}, f32[136,128]{1,0:T(8,128)S(1)}) custom-call(s32[2]{0:T(128)S(1)} %pad_add_fusion.place_ref, bf16[136,128]{1,0:T(8,128)(2,1)} %copy-done.4, bf16[136,128]{1,0:T(8,128)(2,1)} %copy-done, bf16[136,128]{1,0:T(8,128)(2,1)} %copy-done.1, bf16[136,128]{1,0:T(8,128)(2,1)} %copy-done.5, ...), custom_call_target="tpu_custom_call" | custom-call | flops 30000001024 | bytes 6488064 | tf_op jit(solution)/shard_map/pallas_call | solution.py:204
  139.3 6.3 %all-to-all-done.5 = bf16[64,2,128]{2,1,0:T(2,128)(2,1)S(1)} async-done(((bf16[64,2,128]{2,1,0:T(2,128)(2,1)}), bf16[64,2,128]{2,1,0:T(2,128)(2,1)S(1)}, u32[]{:S(2)}, u32[]{:S(2)}) %all-to-all-start.5) | async-done | bytes 32800 | tf_op jit(solution)/shard_map/all_to_all | solution.py:314
  145.7 4.9 %shard_map.64 = bf16[136,6144]{1,0:T(8,128)(2,1)} custom-call(s32[2]{0:T(128)S(1)} %pad_add_fusion.place_ref, f32[136,6144]{1,0:T(8,128)S(1)} %get-tuple-element.46.base, f32[136,128]{1,0:T(8,128)S(1)} %get-tuple-element.47.dk, f32[136,128]{1,0:T(8,128)S(1)} %get-tuple-element.48.dv, bf16[136,128]{1,0:T(8,128)(2,1)} %copy-done, bf16[136,128]{1,0:T(8,128)(2,1)} %copy-done.1, ...), custom_call_target="tpu_custom_call" | custom-call | flops 427819008 | bytes 8159232 | tf_op jit(solution)/shard_map/pallas_call | solution.py:271
  (45 shorter events, 19.0 us)
Async XLA Ops:
  10.6 25.9 %all-to-all-start = ((bf16[64,24,128]{2,1,0:T(8,128)(2,1)}), bf16[64,24,128]{2,1,0:T(8,128)(2,1)S(1)}, u32[]{:S(2)}, u32[]{:S(2)}) async-start(bf16[64,24,128]{2,1,0:T(8,128)(2,1)} %broadcast_in_dim.6), calls=%async_computation | async-start | bytes 786432 | tf_op jit(solution)/shard_map/all_to_all | solution.py:334
  21.6 32.3 %collective-permute-start = (bf16[136,6144]{1,0:T(8,128)(2,1)}, bf16[136,6144]{1,0:T(8,128)(2,1)}, u32[]{:S(2)}, u32[]{:S(2)}) collective-permute-start(bf16[136,6144]{1,0:T(8,128)(2,1)} %bitcast.36), channel_id=1, source_target_pairs={{0,1},{1,0},{2,3},{3,2},{4,5},{5,4},{6,7},{7,6},{8,9},{9,8},{10,11... | collective-permute-start | bytes 5013512 | tf_op jit(solution)/shard_map/ppermute | solution.py:37
  24.1 29.7 %collective-permute-start.1 = (bf16[136,6144]{1,0:T(8,128)(2,1)}, bf16[136,6144]{1,0:T(8,128)(2,1)}, u32[]{:S(2)}, u32[]{:S(2)}) collective-permute-start(bf16[136,6144]{1,0:T(8,128)(2,1)} %bitcast.39), channel_id=1, source_target_pairs={{0,1},{1,0},{2,3},{3,2},{4,5},{5,4},{6,7},{7,6},{8,9},{9,8},{10,11... | collective-permute-start | bytes 5013512 | tf_op jit(solution)/shard_map/ppermute | solution.py:37
  36.6 17.3 %collective-permute-start.4 = (bf16[1536,128]{1,0:T(8,128)(2,1)S(1)}, bf16[1536,128]{1,0:T(8,128)(2,1)S(1)}, u32[]{:S(2)}, u32[]{:S(2)}) collective-permute-start(bf16[1536,128]{1,0:T(8,128)(2,1)S(1)} %bitcast.25), channel_id=1, source_target_pairs={{0,32},{16,48},{32,0},{48,16},{1,33},{17,49},{33,1},{49,17},{2,34}... | collective-permute-start | bytes 1179656 | tf_op jit(solution)/shard_map/ppermute | solution.py:337
  41.2 16.7 %collective-permute-start.3 = (bf16[1536,128]{1,0:T(8,128)(2,1)S(1)}, bf16[1536,128]{1,0:T(8,128)(2,1)S(1)}, u32[]{:S(2)}, u32[]{:S(2)}) collective-permute-start(bf16[1536,128]{1,0:T(8,128)(2,1)S(1)} %bitcast.26), channel_id=1, source_target_pairs={{0,48},{16,0},{32,16},{48,32},{1,49},{17,1},{33,17},{49,33},{2,50}... | collective-permute-start | bytes 1179656 | tf_op jit(solution)/shard_map/ppermute | solution.py:337
  44.0 14.3 %collective-permute-start.2 = (bf16[1536,128]{1,0:T(8,128)(2,1)S(1)}, bf16[1536,128]{1,0:T(8,128)(2,1)S(1)}, u32[]{:S(2)}, u32[]{:S(2)}) collective-permute-start(bf16[1536,128]{1,0:T(8,128)(2,1)S(1)} %bitcast.27), channel_id=1, source_target_pairs={{0,16},{16,32},{32,48},{48,0},{1,17},{17,33},{33,49},{49,1},{2,18}... | collective-permute-start | bytes 1179656 | tf_op jit(solution)/shard_map/ppermute | solution.py:337
  47.3 20.1 %all-to-all-start.1 = ((bf16[64,24,128]{2,1,0:T(8,128)(2,1)}), bf16[64,24,128]{2,1,0:T(8,128)(2,1)S(1)}, u32[]{:S(2)}, u32[]{:S(2)}) async-start(bf16[64,24,128]{2,1,0:T(8,128)(2,1)} %broadcast_in_dim.7), calls=%async_computation.1 | async-start | bytes 786432 | tf_op jit(solution)/shard_map/all_to_all | solution.py:334
  62.0 5.4 %collective-permute-start.5 = (bf16[136,128]{1,0:T(8,128)(2,1)S(1)}, bf16[136,128]{1,0:T(8,128)(2,1)S(1)}, u32[]{:S(2)}, u32[]{:S(2)}) collective-permute-start(bf16[136,128]{1,0:T(8,128)(2,1)S(1)} %get-tuple-element.35), channel_id=1, source_target_pairs={{0,1},{1,0},{2,3},{3,2},{4,5},{5,4},{6,7},{7,6},{8,9},{9,8},{10,11... | collective-permute-start | bytes 104456 | tf_op jit(solution)/shard_map/ppermute | solution.py:37
  68.8 40.8 %copy-start = (bf16[136,128]{1,0:T(8,128)(2,1)}, bf16[136,128]{1,0:T(8,128)(2,1)S(1)}, u32[]{:S(2)}) copy-start(bf16[136,128]{1,0:T(8,128)(2,1)S(1)} %get-tuple-element.41.k_ref.refs_1_.k_any) | copy-start | bytes 104452
  68.8 40.8 %copy-start.1 = (bf16[136,128]{1,0:T(8,128)(2,1)}, bf16[136,128]{1,0:T(8,128)(2,1)S(1)}, u32[]{:S(2)}) copy-start(bf16[136,128]{1,0:T(8,128)(2,1)S(1)} %get-tuple-element.42.v_ref.refs_2_.v_any) | copy-start | bytes 104452
  68.8 20.6 %all-to-all-start.2 = ((bf16[64,2,128]{2,1,0:T(2,128)(2,1)}), bf16[64,2,128]{2,1,0:T(2,128)(2,1)S(1)}, u32[]{:S(2)}, u32[]{:S(2)}) async-start(bf16[64,2,128]{2,1,0:T(2,128)(2,1)} %bitcast.7), calls=%async_computation.2 | async-start | bytes 65536 | tf_op jit(solution)/shard_map/all_to_all | solution.py:314
  79.1 21.2 %collective-permute-start.8 = (bf16[1536,128]{1,0:T(8,128)(2,1)S(1)}, bf16[1536,128]{1,0:T(8,128)(2,1)S(1)}, u32[]{:S(2)}, u32[]{:S(2)}) collective-permute-start(bf16[1536,128]{1,0:T(8,128)(2,1)S(1)} %bitcast.21), channel_id=1, source_target_pairs={{0,32},{16,48},{32,0},{48,16},{1,33},{17,49},{33,1},{49,17},{2,34}... | collective-permute-start | bytes 1179656 | tf_op jit(solution)/shard_map/ppermute | solution.py:337
  84.1 17.8 %collective-permute-start.7 = (bf16[1536,128]{1,0:T(8,128)(2,1)S(1)}, bf16[1536,128]{1,0:T(8,128)(2,1)S(1)}, u32[]{:S(2)}, u32[]{:S(2)}) collective-permute-start(bf16[1536,128]{1,0:T(8,128)(2,1)S(1)} %bitcast.22), channel_id=1, source_target_pairs={{0,48},{16,0},{32,16},{48,32},{1,49},{17,1},{33,17},{49,33},{2,50}... | collective-permute-start | bytes 1179656 | tf_op jit(solution)/shard_map/ppermute | solution.py:337
  86.8 15.2 %collective-permute-start.6 = (bf16[1536,128]{1,0:T(8,128)(2,1)S(1)}, bf16[1536,128]{1,0:T(8,128)(2,1)S(1)}, u32[]{:S(2)}, u32[]{:S(2)}) collective-permute-start(bf16[1536,128]{1,0:T(8,128)(2,1)S(1)} %bitcast.23), channel_id=1, source_target_pairs={{0,16},{16,32},{32,48},{48,0},{1,17},{17,33},{33,49},{49,1},{2,18}... | collective-permute-start | bytes 1179656 | tf_op jit(solution)/shard_map/ppermute | solution.py:337
  90.1 19.4 %all-to-all-start.3 = ((bf16[64,2,128]{2,1,0:T(2,128)(2,1)}), bf16[64,2,128]{2,1,0:T(2,128)(2,1)S(1)}, u32[]{:S(2)}, u32[]{:S(2)}) async-start(bf16[64,2,128]{2,1,0:T(2,128)(2,1)} %bitcast.9), calls=%async_computation.3 | async-start | bytes 65536 | tf_op jit(solution)/shard_map/all_to_all | solution.py:314
  105.2 18.1 %copy-start.2 = (bf16[6144,128]{1,0:T(8,128)(2,1)}, bf16[6144,128]{1,0:T(8,128)(2,1)S(1)}, u32[]{:S(2)}) copy-start(bf16[6144,128]{1,0:T(8,128)(2,1)S(1)} %get-tuple-element.45.refs_5_) | copy-start | bytes 4718596
  105.2 4.4 %collective-permute-start.9 = (f32[136,128]{1,0:T(8,128)S(1)}, f32[136,128]{1,0:T(8,128)S(1)}, u32[]{:S(2)}, u32[]{:S(2)}) collective-permute-start(f32[136,128]{1,0:T(8,128)S(1)} %get-tuple-element.39), channel_id=1, source_target_pairs={{0,1},{1,0},{2,3},{3,2},{4,5},{5,4},{6,7},{7,6},{8,9},{9,8},{10,11... | collective-permute-start | bytes 208904 | tf_op jit(solution)/shard_map/ppermute | solution.py:37
  109.6 2.3 %copy-start.6 = (bf16[128,128]{1,0:T(8,128)(2,1)}, bf16[128,128]{1,0:T(8,128)(2,1)S(1)}, u32[]{:S(2)}) copy-start(bf16[128,128]{1,0:T(8,128)(2,1)S(1)} %shard_map.60.prior_ref.refs_4_) | copy-start | bytes 98308
  111.9 19.1 %copy-start.4 = (bf16[136,128]{1,0:T(8,128)(2,1)}, bf16[136,128]{1,0:T(8,128)(2,1)S(1)}, u32[]{:S(2)}) copy-start(bf16[136,128]{1,0:T(8,128)(2,1)S(1)} %get-tuple-element.43.refs_0_) | copy-start | bytes 104452
  111.9 19.1 %copy-start.5 = (bf16[136,128]{1,0:T(8,128)(2,1)}, bf16[136,128]{1,0:T(8,128)(2,1)S(1)}, u32[]{:S(2)}) copy-start(bf16[136,128]{1,0:T(8,128)(2,1)S(1)} %get-tuple-element.44.refs_3_) | copy-start | bytes 104452
  111.9 18.3 %all-to-all-start.4 = ((bf16[64,2,128]{2,1,0:T(2,128)(2,1)}), bf16[64,2,128]{2,1,0:T(2,128)(2,1)S(1)}, u32[]{:S(2)}, u32[]{:S(2)}) async-start(bf16[64,2,128]{2,1,0:T(2,128)(2,1)} %bitcast.12), calls=%async_computation.4 | async-start | bytes 65536 | tf_op jit(solution)/shard_map/all_to_all | solution.py:314
  121.0 24.7 %collective-permute-start.11 = (bf16[6144,128]{1,0:T(8,128)(2,1)}, bf16[6144,128]{1,0:T(8,128)(2,1)}, u32[]{:S(2)}, u32[]{:S(2)}) collective-permute-start(bf16[6144,128]{1,0:T(8,128)(2,1)} %get-tuple-element.50.near_any), channel_id=1, source_target_pairs={{0,1},{1,0},{2,3},{3,2},{4,5},{5,4},{6,7},{7,6},{8,9},{9,8},{10,11... | collective-permute-start | bytes 4718600 | tf_op jit(solution)/shard_map/ppermute | solution.py:37
  123.3 13.1 %collective-permute-start.10 = (bf16[6144,128]{1,0:T(8,128)(2,1)S(1)}, bf16[6144,128]{1,0:T(8,128)(2,1)}, u32[]{:S(2)}, u32[]{:S(2)}) collective-permute-start(bf16[6144,128]{1,0:T(8,128)(2,1)S(1)} %get-tuple-element.45.refs_5_), channel_id=1, source_target_pairs={{0,1},{1,0},{2,3},{3,2},{4,5},{5,4},{6,7},{7,6},{8,9},{9,8},{10,11... | collective-permute-start | bytes 4718600 | tf_op jit(solution)/shard_map/ppermute | solution.py:37
  131.0 14.7 %all-to-all-start.5 = ((bf16[64,2,128]{2,1,0:T(2,128)(2,1)}), bf16[64,2,128]{2,1,0:T(2,128)(2,1)S(1)}, u32[]{:S(2)}, u32[]{:S(2)}) async-start(bf16[64,2,128]{2,1,0:T(2,128)(2,1)} %bitcast.14), calls=%async_computation.5 | async-start | bytes 65536 | tf_op jit(solution)/shard_map/all_to_all | solution.py:314
  (1 other events, 0.7 us)

commit v6 on v5

--- a/solution.py
+++ b/solution.py
@@ -44,23 +44,28 @@
 def project_kernel(shifts, place_ref, *refs):
     tokens, blocks, outs, scratch = refs[:-11], refs[-11:-7], refs[-7:-4], refs[-4:]
     weight_ref, own_ref, send_ref = outs
-    own_held, far_held, own_sem, far_sem = scratch
-    rows = weight_ref.shape[0] // 32
+    own_held, far_held, row_sems, block_sems = scratch
+    dps, xs, rows, head = weight_ref.shape
 
     def products(own, far):
-        own_copy = pltpu.make_async_copy(own, own_held, own_sem)
-        far_copy = pltpu.make_async_copy(far, far_held, far_sem)
-        own_copy.start()
-        far_copy.start()
-        for k, ref in zip(shifts, blocks):
-            source = lax.rem(place_ref[0] - k + 4, 4)
-            for p in range(8):
-                at = pl.multiple_of((p * 4 + source) * rows, 64)
-                weight_ref[pl.ds(at, rows), :] = ref[p * rows : (p + 1) * rows, :]
-        own_copy.wait()
-        own_ref[...] = contract(own_held[...], weight_ref[...], 1, 0).astype(own_ref.dtype)
-        far_copy.wait()
-        send_ref[...] = contract(far_held[...], weight_ref[...], 1, 0).astype(send_ref.dtype)
+        row_copies = [
+            pltpu.make_async_copy(own, own_held, row_sems.at[0]),
+            pltpu.make_async_copy(far, far_held, row_sems.at[1]),
+        ]
+        block_copies = []
+        for i, (k, ref) in enumerate(zip(shifts, blocks)):
+            source = lax.rem(place_ref[0] - k + xs, xs)
+            block_copies.append(
+                pltpu.make_async_copy(ref, weight_ref.at[:, source], block_sems.at[i])
+            )
+        for copy in block_copies + row_copies:
+            copy.start()
+        for copy in block_copies + row_copies[:1]:
+            copy.wait()
+        weight = weight_ref[...].reshape(dps * xs * rows, head)
+        own_ref[...] = contract(own_held[...], weight, 1, 0).astype(own_ref.dtype)
+        row_copies[1].wait()
+        send_ref[...] = contract(far_held[...], weight, 1, 0).astype(send_ref.dtype)
 
     if len(tokens) == 2:
         products(*tokens)
@@ -71,16 +76,20 @@
 
 def project(place, tokens, blocks, dtype):
     count, depth = tokens[0].shape
+    dps, xs = lax.axis_size("dp"), len(blocks)
+    rows = depth // (dps * xs)
     row = jax.ShapeDtypeStruct((count, 128), dtype)
-    return pl.pallas_call(
+    weight, own, send = pl.pallas_call(
         functools.partial(project_kernel, tuple(blocks)),
-        out_shape=[jax.ShapeDtypeStruct((depth, 128), BF16), row, row],
-        in_specs=[SMEM] + [pl.BlockSpec(memory_space=pl.ANY)] * len(tokens) + [VMEM] * 4,
+        out_shape=[jax.ShapeDtypeStruct((dps, xs, rows, 128), BF16), row, row],
+        in_specs=[SMEM] + [pl.BlockSpec(memory_space=pl.ANY)] * (len(tokens) + xs),
         out_specs=[VMEM] * 3,
-        scratch_shapes=[pltpu.VMEM((count, depth), BF16)] * 2 + [pltpu.SemaphoreType.DMA] * 2,
+        scratch_shapes=[pltpu.VMEM((count, depth), BF16)] * 2
+        + [pltpu.SemaphoreType.DMA((2,)), pltpu.SemaphoreType.DMA((xs,))],
         compiler_params=pltpu.CompilerParams(vmem_limit_bytes=LIMIT),
         cost_estimate=cost(LONG, 4 * count * depth + 4 * depth * 128),
-    )(place, *in_hbm(*tokens), *blocks.values())
+    )(place, *in_hbm(*tokens), *in_hbm(*[v.reshape(dps, rows, 128) for v in blocks.values()]))
+    return weight.reshape(depth, 128), own, send
 
 
 def state_kernel(place_ref, own_ref, recv_ref, key_ref, value_ref, state_ref):
@@ -337,26 +346,23 @@
         shifts = {k: lax.ppermute(block, "x", [(i, (i + k) % xs) for i in range(xs)]) for k in (2, 1, 3)}
         return {1: shifts[1], 3: shifts[3], 2: shifts[2], 0: block}
 
-    kv_copies = copied(kv_rows)
+    kv_copies, qo_copies = copied(kv_rows), copied(qo_rows)
     tokens_far = core_swap(after(tokens, kv_copies))
     grads_far = core_swap(after(grads_in, kv_copies))
-    kv_plane = over_planes(kv_copies)
-    qo_plane = over_planes(copied(gate(after(qo_rows, kv_plane))))
-    tokens_far = after(tokens_far, grads_far)
-    kv_near, own, send = project(place, (tokens, tokens_far), over_x(kv_plane), BF16)
-    own, qo_plane = lax.optimization_barrier((own, qo_plane))
+    kv_plane = gate(over_planes(kv_copies))
+    qo_plane = gate(over_planes(after(qo_copies, kv_plane, tokens_far, grads_far)))
+    kv, qo = over_x(kv_plane), over_x(qo_plane)
+    kv_near, own, send = project(place, (tokens, tokens_far), kv, BF16)
     keys, values, local_state = keys_values_state(place, own, core_swap(send))
 
-    qo = over_x(after(qo_plane, local_state))
-    prior_state = gate(exchange(sums_of(exchange(local_state), False)))
-    qo_near, own, send = project(
-        place, (tokens, tokens_far, grads_in, grads_far), qo, F32
+    pieces = exchange(local_state)
+    qo_near, own, send = project(place, (tokens, tokens_far, grads_in, grads_far), qo, F32)
+    prior_state = gate(exchange(sums_of(after(pieces, own), False)))
+    recv = after(core_swap(send), prior_state)
+    kv_far = core_swap(kv_near)
+    queries, attn_grad, local_grad = attention_grad(
+        place, own, recv, keys, after(values, kv_far), prior_state, norm_gain.reshape(1, head)
     )
-    recv = after(core_swap(send), prior_state)
-    queries, attn_grad, local_grad = attention_grad(
-        place, own, recv, keys, values, prior_state, norm_gain.reshape(1, head)
-    )
-    kv_far = core_swap(kv_near)
     grad_pieces = exchange(local_grad)
     qo_far = core_swap(qo_near)
     base, *grads = inner_grads(

time: 152 us -> 157 us (1.033)
  waiting for transfers between devices: 30.2 us -> 37.1 us
  starting transfers between devices: 88.5 us -> 82.8 us
  local copies, waits for them, and re-layouts: 2.97 us -> 5.87 us
    all_to_all x4, waiting for transfers between devices: 12.6 us -> 21.4 us  [exchange(): return lax.all_to_all(pieces, SEQ, 0, 0, tiled=True).reshape(state.shape)]
    all_to_all x4, starting transfers between devices: 34.9 us -> 26.3 us  [exchange(): return lax.all_to_all(pieces, SEQ, 0, 0, tiled=True).reshape(state.shape)]
    ppermute x6, waiting for transfers between devices: 6.01 us -> 0.02 us  [over_x(): lax.ppermute(block, 'x', [(i, (i + k) % xs) for i in range(xs)])]
    all_to_all x2, waiting for transfers between devices: 11.6 us -> 14.8 us  [over_planes(): return lax.all_to_all(copies, ROWS, 0, 0, tiled=True).reshape(-1, head)]
    ppermute x6, starting transfers between devices: 16 us -> 19.2 us  [core_swap(): return lax.ppermute(block, 'core', [(0, 1), (1, 0)])]
    unnamed x17 -> x35, local copies, waits for them, and re-layouts: 1.37 us -> 4.23 us
  transfers between devices with their start and end apart: 18 -> 18, of which waited for: 9 -> 7; matrix products, arithmetic and copies ran while one was open for 1% -> 0% of each run, Pallas kernels for 8% -> 9%
where the time goes in v6:
time: 157 us; the launch traced here: 156 us
  starting transfers between devices  82.8 us (53%)
  waiting for transfers between devices  37.1 us (24%)
  Pallas kernels  20.7 us (13%)
  blocking collectives  8.36 us (5%)
  local copies, waits for them, and re-layouts  5.87 us (4%)
    all_to_all x4, starting transfers between devices, exchange(): return lax.all_to_all(pieces, SEQ, 0, 0, tiled=True).reshape(state.shape)  26.3 us
    all_to_all x4, waiting for transfers between devices, exchange(): return lax.all_to_all(pieces, SEQ, 0, 0, tiled=True).reshape(state.shape)  21.4 us
    ppermute x6, starting transfers between devices, over_x(): lax.ppermute(block, 'x', [(i, (i + k) % xs) for i in range(xs)])  19.9 us
    ppermute x6, starting transfers between devices, core_swap(): return lax.ppermute(block, 'core', [(0, 1), (1, 0)])  19.2 us
    all_to_all x2, starting transfers between devices, over_planes(): return lax.all_to_all(copies, ROWS, 0, 0, tiled=True).reshape(-1, head)  17.4 us
    all_to_all x2, waiting for transfers between devices, over_planes(): return lax.all_to_all(copies, ROWS, 0, 0, tiled=True).reshape(-1, head)  14.8 us
    all_gather x1, blocking collectives, per_device(): rows = lax.all_gather(rows, 'core', axis=0, tiled=True)  8.36 us
    pallas_call x2, Pallas kernels, project(): pl.pallas_call(functools.partial(project_kernel, tuple(blocks)), out_shap...  8.35 us
  transfers between devices with their start and end apart: 18, of which 7 were waited for; matrix products, arithmetic and copies ran while one was open for 0% of the time, Pallas kernels for 9%

profile of v6, /device:TPU:1, one launch (start us, length us, event | category | flops | bytes accessed | tf_op | source)
XLA Modules:
  0.0 156.2 jit_solution(6445979255836480928)
XLA Ops:
  1.4 8.4 %all-gather = bf16[2,12,512]{2,1,0:T(8,128)(2,1)S(1)} all-gather(bf16[1,12,512]{2,1,0:T(8,128)(2,1)S(1)} %maximum_bitcast_fusion), channel_id=1, replica_groups=mesh['dp'=8,'x'=4,'z'=8,'core'=2] {'core'}, dimensions={0}, use_global_device_ids=true | all-gather | bytes 36864 | tf_op jit(solution)/shard_map/all_gather | solution.py:335
  10.6 10.9 %all-to-all-start = ((bf16[64,24,128]{2,1,0:T(8,128)(2,1)}), bf16[64,24,128]{2,1,0:T(8,128)(2,1)S(1)}, u32[]{:S(2)}, u32[]{:S(2)}) async-start(bf16[64,24,128]{2,1,0:T(8,128)(2,1)} %broadcast_in_dim.6), calls=%async_computation | async-start | bytes 786432 | tf_op jit(solution)/shard_map/all_to_all | solution.py:343
  21.6 2.5 %collective-permute-start = (bf16[136,6144]{1,0:T(8,128)(2,1)}, bf16[136,6144]{1,0:T(8,128)(2,1)}, u32[]{:S(2)}, u32[]{:S(2)}) collective-permute-start(bf16[136,6144]{1,0:T(8,128)(2,1)} %bitcast.46), channel_id=1, source_target_pairs={{0,1},{1,0},{2,3},{3,2},{4,5},{5,4},{6,7},{7,6},{8,9},{9,8},{10,11... | collective-permute-start | bytes 5013512 | tf_op jit(solution)/shard_map/ppermute | solution.py:37
  26.0 10.5 %all-to-all-done = bf16[64,24,128]{2,1,0:T(8,128)(2,1)S(1)} async-done(((bf16[64,24,128]{2,1,0:T(8,128)(2,1)}), bf16[64,24,128]{2,1,0:T(8,128)(2,1)S(1)}, u32[]{:S(2)}, u32[]{:S(2)}) %all-to-all-start) | async-done | bytes 393248 | tf_op jit(solution)/shard_map/all_to_all | solution.py:343
  37.5 6.5 %all-to-all-start.1 = ((bf16[64,24,128]{2,1,0:T(8,128)(2,1)}), bf16[64,24,128]{2,1,0:T(8,128)(2,1)S(1)}, u32[]{:S(2)}, u32[]{:S(2)}) async-start(bf16[64,24,128]{2,1,0:T(8,128)(2,1)} %broadcast_in_dim.7), calls=%async_computation.1 | async-start | bytes 786432 | tf_op jit(solution)/shard_map/all_to_all | solution.py:343
  44.1 4.6 %collective-permute-start.8 = (bf16[1536,128]{1,0:T(8,128)(2,1)S(1)}, bf16[1536,128]{1,0:T(8,128)(2,1)S(1)}, u32[]{:S(2)}, u32[]{:S(2)}) collective-permute-start(bf16[1536,128]{1,0:T(8,128)(2,1)S(1)} %shard_map.55), channel_id=1, source_target_pairs={{0,32},{16,48},{32,0},{48,16},{1,33},{17,49},{33,1},{49,17},{2,34}... | collective-permute-start | bytes 1179656 | tf_op jit(solution)/shard_map/ppermute | solution.py:346
  48.7 2.8 %collective-permute-start.7 = (bf16[1536,128]{1,0:T(8,128)(2,1)S(1)}, bf16[1536,128]{1,0:T(8,128)(2,1)S(1)}, u32[]{:S(2)}, u32[]{:S(2)}) collective-permute-start(bf16[1536,128]{1,0:T(8,128)(2,1)S(1)} %shard_map.55), channel_id=1, source_target_pairs={{0,48},{16,0},{32,16},{48,32},{1,49},{17,1},{33,17},{49,33},{2,50}... | collective-permute-start | bytes 1179656 | tf_op jit(solution)/shard_map/ppermute | solution.py:346
  54.0 4.3 %all-to-all-done.1 = bf16[64,24,128]{2,1,0:T(8,128)(2,1)S(1)} async-done(((bf16[64,24,128]{2,1,0:T(8,128)(2,1)}), bf16[64,24,128]{2,1,0:T(8,128)(2,1)S(1)}, u32[]{:S(2)}, u32[]{:S(2)}) %all-to-all-start.1) | async-done | bytes 393248 | tf_op jit(solution)/shard_map/all_to_all | solution.py:343
  58.4 4.7 %collective-permute-start.4 = (bf16[1536,128]{1,0:T(8,128)(2,1)S(1)}, bf16[1536,128]{1,0:T(8,128)(2,1)S(1)}, u32[]{:S(2)}, u32[]{:S(2)}) collective-permute-start(bf16[1536,128]{1,0:T(8,128)(2,1)S(1)} %shard_map.56), channel_id=1, source_target_pairs={{0,32},{16,48},{32,0},{48,16},{1,33},{17,49},{33,1},{49,17},{2,34}... | collective-permute-start | bytes 1179656 | tf_op jit(solution)/shard_map/ppermute | solution.py:346
  63.0 2.8 %collective-permute-start.3 = (bf16[1536,128]{1,0:T(8,128)(2,1)S(1)}, bf16[1536,128]{1,0:T(8,128)(2,1)S(1)}, u32[]{:S(2)}, u32[]{:S(2)}) collective-permute-start(bf16[1536,128]{1,0:T(8,128)(2,1)S(1)} %shard_map.56), channel_id=1, source_target_pairs={{0,48},{16,0},{32,16},{48,32},{1,49},{17,1},{33,17},{49,33},{2,50}... | collective-permute-start | bytes 1179656 | tf_op jit(solution)/shard_map/ppermute | solution.py:346
  65.8 2.5 %collective-permute-start.2 = (bf16[1536,128]{1,0:T(8,128)(2,1)S(1)}, bf16[1536,128]{1,0:T(8,128)(2,1)}, u32[]{:S(2)}, u32[]{:S(2)}) collective-permute-start(bf16[1536,128]{1,0:T(8,128)(2,1)S(1)} %shard_map.56), channel_id=1, source_target_pairs={{0,16},{16,32},{32,48},{48,0},{1,17},{17,33},{33,49},{49,1},{2,18}... | collective-permute-start | bytes 1179656 | tf_op jit(solution)/shard_map/ppermute | solution.py:346
  69.2 4.2 %shard_map.58 = (bf16[8,4,192,128]{3,2,1,0:T(8,128)(2,1)S(1)}, bf16[136,128]{1,0:T(8,128)(2,1)S(1)}, bf16[136,128]{1,0:T(8,128)(2,1)S(1)}) custom-call(s32[2]{0:T(128)S(1)} %pad_add_fusion.place_ref, bf16[136,6144]{1,0:T(8,128)(2,1)} %bitcast.47, bf16[136,6144]{1,0:T(8,128)(2,1)} %collective-permute-done.refs_1_, bf16[8,192,128]{2,1,0:T(8,128)(2,1)} %bitcast.55, ...), custom_call_target="tpu_custom_call" | custom-call | flops 30000001024 | bytes 6488064 | tf_op jit(solution)/shard_map/pallas_call | solution.py:82
  73.4 8.1 %collective-permute-start.9 = (bf16[136,128]{1,0:T(8,128)(2,1)S(1)}, bf16[136,128]{1,0:T(8,128)(2,1)S(1)}, u32[]{:S(2)}, u32[]{:S(2)}) collective-permute-start(bf16[136,128]{1,0:T(8,128)(2,1)S(1)} %get-tuple-element.32), channel_id=1, source_target_pairs={{0,1},{1,0},{2,3},{3,2},{4,5},{5,4},{6,7},{7,6},{8,9},{9,8},{10,11... | collective-permute-start | bytes 104456 | tf_op jit(solution)/shard_map/ppermute | solution.py:37
  83.7 9.5 %all-to-all-start.2 = ((bf16[64,2,128]{2,1,0:T(2,128)(2,1)}), bf16[64,2,128]{2,1,0:T(2,128)(2,1)S(1)}, u32[]{:S(2)}, u32[]{:S(2)}) async-start(bf16[64,2,128]{2,1,0:T(2,128)(2,1)} %bitcast.15), calls=%async_computation.2 | async-start | bytes 65536 | tf_op jit(solution)/shard_map/all_to_all | solution.py:323
  94.1 4.2 %shard_map.57 = (bf16[8,4,192,128]{3,2,1,0:T(8,128)(2,1)S(1)}, f32[136,128]{1,0:T(8,128)S(1)}, f32[136,128]{1,0:T(8,128)S(1)}) custom-call(s32[2]{0:T(128)S(1)} %pad_add_fusion.place_ref, bf16[136,6144]{1,0:T(8,128)(2,1)} %bitcast.48, bf16[136,6144]{1,0:T(8,128)(2,1)} %collective-permute-done.refs_1_, bf16[136,6144]{1,0:T(8,128)(2,1)} %bitcast.50, ...), custom_call_target="tpu_custom_call" | custom-call | flops 30000001024 | bytes 6488064 | tf_op jit(solution)/shard_map/pallas_call | solution.py:82
  98.3 4.2 %all-to-all-done.2 = bf16[64,2,128]{2,1,0:T(2,128)(2,1)S(1)} async-done(((bf16[64,2,128]{2,1,0:T(2,128)(2,1)}), bf16[64,2,128]{2,1,0:T(2,128)(2,1)S(1)}, u32[]{:S(2)}, u32[]{:S(2)}) %all-to-all-start.2) | async-done | bytes 32800 | tf_op jit(solution)/shard_map/all_to_all | solution.py:323
  103.3 6.3 %all-to-all-start.3 = ((bf16[64,2,128]{2,1,0:T(2,128)(2,1)}), bf16[64,2,128]{2,1,0:T(2,128)(2,1)S(1)}, u32[]{:S(2)}, u32[]{:S(2)}) async-start(bf16[64,2,128]{2,1,0:T(2,128)(2,1)} %bitcast.17), calls=%async_computation.3 | async-start | bytes 65536 | tf_op jit(solution)/shard_map/all_to_all | solution.py:323
  113.9 4.9 %all-to-all-done.3 = bf16[64,2,128]{2,1,0:T(2,128)(2,1)S(1)} async-done(((bf16[64,2,128]{2,1,0:T(2,128)(2,1)}), bf16[64,2,128]{2,1,0:T(2,128)(2,1)S(1)}, u32[]{:S(2)}, u32[]{:S(2)}) %all-to-all-start.3) | async-done | bytes 32800 | tf_op jit(solution)/shard_map/all_to_all | solution.py:323
  121.2 5.8 %all-to-all-start.4 = ((bf16[64,2,128]{2,1,0:T(2,128)(2,1)}), bf16[64,2,128]{2,1,0:T(2,128)(2,1)S(1)}, u32[]{:S(2)}, u32[]{:S(2)}) async-start(bf16[64,2,128]{2,1,0:T(2,128)(2,1)} %bitcast.22), calls=%async_computation.4 | async-start | bytes 65536 | tf_op jit(solution)/shard_map/all_to_all | solution.py:323
  129.4 6.9 %all-to-all-done.4 = bf16[64,2,128]{2,1,0:T(2,128)(2,1)S(1)} async-done(((bf16[64,2,128]{2,1,0:T(2,128)(2,1)}), bf16[64,2,128]{2,1,0:T(2,128)(2,1)S(1)}, u32[]{:S(2)}, u32[]{:S(2)}) %all-to-all-start.4) | async-done | bytes 32800 | tf_op jit(solution)/shard_map/all_to_all | solution.py:323
  137.1 4.7 %all-to-all-start.5 = ((bf16[64,2,128]{2,1,0:T(2,128)(2,1)}), bf16[64,2,128]{2,1,0:T(2,128)(2,1)S(1)}, u32[]{:S(2)}, u32[]{:S(2)}) async-start(bf16[64,2,128]{2,1,0:T(2,128)(2,1)} %bitcast.24), calls=%async_computation.5 | async-start | bytes 65536 | tf_op jit(solution)/shard_map/all_to_all | solution.py:323
  143.0 2.9 %shard_map.63 = (f32[136,6144]{1,0:T(8,128)S(1)}, f32[136,128]{1,0:T(8,128)S(1)}, f32[136,128]{1,0:T(8,128)S(1)}) custom-call(s32[2]{0:T(128)S(1)} %pad_add_fusion.place_ref, bf16[136,128]{1,0:T(8,128)(2,1)} %copy-done.7, bf16[136,128]{1,0:T(8,128)(2,1)} %copy-done.1, bf16[136,128]{1,0:T(8,128)(2,1)} %copy-done.2, bf16[136,128]{1,0:T(8,128)(2,1)} %copy-done.8, ...), custom_call_target="tpu_custom_call" | custom-call | flops 30000001024 | bytes 6488064 | tf_op jit(solution)/shard_map/pallas_call | solution.py:213
  145.9 5.3 %all-to-all-done.5 = bf16[64,2,128]{2,1,0:T(2,128)(2,1)S(1)} async-done(((bf16[64,2,128]{2,1,0:T(2,128)(2,1)}), bf16[64,2,128]{2,1,0:T(2,128)(2,1)S(1)}, u32[]{:S(2)}, u32[]{:S(2)}) %all-to-all-start.5) | async-done | bytes 32800 | tf_op jit(solution)/shard_map/all_to_all | solution.py:323
  151.2 4.9 %shard_map.65 = bf16[136,6144]{1,0:T(8,128)(2,1)} custom-call(s32[2]{0:T(128)S(1)} %pad_add_fusion.place_ref, f32[136,6144]{1,0:T(8,128)S(1)} %get-tuple-element.43.base, f32[136,128]{1,0:T(8,128)S(1)} %get-tuple-element.44.dk, f32[136,128]{1,0:T(8,128)S(1)} %get-tuple-element.45.dv, bf16[136,128]{1,0:T(8,128)(2,1)} %copy-done.1, ...), custom_call_target="tpu_custom_call" | custom-call | flops 427819008 | bytes 8159232 | tf_op jit(solution)/shard_map/pallas_call | solution.py:280
  (64 shorter events, 23.2 us)
Async XLA Ops:
  10.6 25.9 %all-to-all-start = ((bf16[64,24,128]{2,1,0:T(8,128)(2,1)}), bf16[64,24,128]{2,1,0:T(8,128)(2,1)S(1)}, u32[]{:S(2)}, u32[]{:S(2)}) async-start(bf16[64,24,128]{2,1,0:T(8,128)(2,1)} %broadcast_in_dim.6), calls=%async_computation | async-start | bytes 786432 | tf_op jit(solution)/shard_map/all_to_all | solution.py:343
  21.6 15.1 %collective-permute-start = (bf16[136,6144]{1,0:T(8,128)(2,1)}, bf16[136,6144]{1,0:T(8,128)(2,1)}, u32[]{:S(2)}, u32[]{:S(2)}) collective-permute-start(bf16[136,6144]{1,0:T(8,128)(2,1)} %bitcast.46), channel_id=1, source_target_pairs={{0,1},{1,0},{2,3},{3,2},{4,5},{5,4},{6,7},{7,6},{8,9},{9,8},{10,11... | collective-permute-start | bytes 5013512 | tf_op jit(solution)/shard_map/ppermute | solution.py:37
  24.1 12.5 %collective-permute-start.1 = (bf16[136,6144]{1,0:T(8,128)(2,1)}, bf16[136,6144]{1,0:T(8,128)(2,1)}, u32[]{:S(2)}, u32[]{:S(2)}) collective-permute-start(bf16[136,6144]{1,0:T(8,128)(2,1)} %bitcast.49), channel_id=1, source_target_pairs={{0,1},{1,0},{2,3},{3,2},{4,5},{5,4},{6,7},{7,6},{8,9},{9,8},{10,11... | collective-permute-start | bytes 5013512 | tf_op jit(solution)/shard_map/ppermute | solution.py:37
  36.6 21.7 %copy-start.4 = (bf16[1536,128]{1,0:T(8,128)(2,1)}, bf16[1536,128]{1,0:T(8,128)(2,1)S(1)}, u32[]{:S(2)}) copy-start(bf16[1536,128]{1,0:T(8,128)(2,1)S(1)} %shard_map.55) | copy-start | bytes 1179652
  37.5 20.8 %all-to-all-start.1 = ((bf16[64,24,128]{2,1,0:T(8,128)(2,1)}), bf16[64,24,128]{2,1,0:T(8,128)(2,1)S(1)}, u32[]{:S(2)}, u32[]{:S(2)}) async-start(bf16[64,24,128]{2,1,0:T(8,128)(2,1)} %broadcast_in_dim.7), calls=%async_computation.1 | async-start | bytes 786432 | tf_op jit(solution)/shard_map/all_to_all | solution.py:343
  44.1 21.7 %collective-permute-start.8 = (bf16[1536,128]{1,0:T(8,128)(2,1)S(1)}, bf16[1536,128]{1,0:T(8,128)(2,1)S(1)}, u32[]{:S(2)}, u32[]{:S(2)}) collective-permute-start(bf16[1536,128]{1,0:T(8,128)(2,1)S(1)} %shard_map.55), channel_id=1, source_target_pairs={{0,32},{16,48},{32,0},{48,16},{1,33},{17,49},{33,1},{49,17},{2,34}... | collective-permute-start | bytes 1179656 | tf_op jit(solution)/shard_map/ppermute | solution.py:346
  48.7 19.6 %collective-permute-start.7 = (bf16[1536,128]{1,0:T(8,128)(2,1)S(1)}, bf16[1536,128]{1,0:T(8,128)(2,1)S(1)}, u32[]{:S(2)}, u32[]{:S(2)}) collective-permute-start(bf16[1536,128]{1,0:T(8,128)(2,1)S(1)} %shard_map.55), channel_id=1, source_target_pairs={{0,48},{16,0},{32,16},{48,32},{1,49},{17,1},{33,17},{49,33},{2,50}... | collective-permute-start | bytes 1179656 | tf_op jit(solution)/shard_map/ppermute | solution.py:346
  51.5 16.9 %collective-permute-start.6 = (bf16[1536,128]{1,0:T(8,128)(2,1)S(1)}, bf16[1536,128]{1,0:T(8,128)(2,1)S(1)}, u32[]{:S(2)}, u32[]{:S(2)}) collective-permute-start(bf16[1536,128]{1,0:T(8,128)(2,1)S(1)} %shard_map.55), channel_id=1, source_target_pairs={{0,16},{16,32},{32,48},{48,0},{1,17},{17,33},{33,49},{49,1},{2,18}... | collective-permute-start | bytes 1179656 | tf_op jit(solution)/shard_map/ppermute | solution.py:346
  58.4 34.9 %collective-permute-start.4 = (bf16[1536,128]{1,0:T(8,128)(2,1)S(1)}, bf16[1536,128]{1,0:T(8,128)(2,1)S(1)}, u32[]{:S(2)}, u32[]{:S(2)}) collective-permute-start(bf16[1536,128]{1,0:T(8,128)(2,1)S(1)} %shard_map.56), channel_id=1, source_target_pairs={{0,32},{16,48},{32,0},{48,16},{1,33},{17,49},{33,1},{49,17},{2,34}... | collective-permute-start | bytes 1179656 | tf_op jit(solution)/shard_map/ppermute | solution.py:346
  63.0 30.2 %collective-permute-start.3 = (bf16[1536,128]{1,0:T(8,128)(2,1)S(1)}, bf16[1536,128]{1,0:T(8,128)(2,1)S(1)}, u32[]{:S(2)}, u32[]{:S(2)}) collective-permute-start(bf16[1536,128]{1,0:T(8,128)(2,1)S(1)} %shard_map.56), channel_id=1, source_target_pairs={{0,48},{16,0},{32,16},{48,32},{1,49},{17,1},{33,17},{49,33},{2,50}... | collective-permute-start | bytes 1179656 | tf_op jit(solution)/shard_map/ppermute | solution.py:346
  65.8 27.5 %collective-permute-start.2 = (bf16[1536,128]{1,0:T(8,128)(2,1)S(1)}, bf16[1536,128]{1,0:T(8,128)(2,1)}, u32[]{:S(2)}, u32[]{:S(2)}) collective-permute-start(bf16[1536,128]{1,0:T(8,128)(2,1)S(1)} %shard_map.56), channel_id=1, source_target_pairs={{0,16},{16,32},{32,48},{48,0},{1,17},{17,33},{33,49},{49,1},{2,18}... | collective-permute-start | bytes 1179656 | tf_op jit(solution)/shard_map/ppermute | solution.py:346
  73.4 36.2 %copy-start = (bf16[8,4,192,128]{3,2,1,0:T(8,128)(2,1)}, bf16[8,4,192,128]{3,2,1,0:T(8,128)(2,1)S(1)}, u32[]{:S(2)}) copy-start(bf16[8,4,192,128]{3,2,1,0:T(8,128)(2,1)S(1)} %get-tuple-element.38) | copy-start | bytes 4718596
  73.4 8.9 %collective-permute-start.9 = (bf16[136,128]{1,0:T(8,128)(2,1)S(1)}, bf16[136,128]{1,0:T(8,128)(2,1)S(1)}, u32[]{:S(2)}, u32[]{:S(2)}) collective-permute-start(bf16[136,128]{1,0:T(8,128)(2,1)S(1)} %get-tuple-element.32), channel_id=1, source_target_pairs={{0,1},{1,0},{2,3},{3,2},{4,5},{5,4},{6,7},{7,6},{8,9},{9,8},{10,11... | collective-permute-start | bytes 104456 | tf_op jit(solution)/shard_map/ppermute | solution.py:37
  83.7 35.2 %copy-start.1 = (bf16[136,128]{1,0:T(8,128)(2,1)}, bf16[136,128]{1,0:T(8,128)(2,1)S(1)}, u32[]{:S(2)}) copy-start(bf16[136,128]{1,0:T(8,128)(2,1)S(1)} %get-tuple-element.36.k_ref.refs_1_.k_any) | copy-start | bytes 104452
  83.7 35.2 %copy-start.2 = (bf16[136,128]{1,0:T(8,128)(2,1)}, bf16[136,128]{1,0:T(8,128)(2,1)S(1)}, u32[]{:S(2)}) copy-start(bf16[136,128]{1,0:T(8,128)(2,1)S(1)} %get-tuple-element.39.v_ref.refs_2_.v_any) | copy-start | bytes 104452
  83.7 18.8 %all-to-all-start.2 = ((bf16[64,2,128]{2,1,0:T(2,128)(2,1)}), bf16[64,2,128]{2,1,0:T(2,128)(2,1)S(1)}, u32[]{:S(2)}, u32[]{:S(2)}) async-start(bf16[64,2,128]{2,1,0:T(2,128)(2,1)} %bitcast.15), calls=%async_computation.2 | async-start | bytes 65536 | tf_op jit(solution)/shard_map/all_to_all | solution.py:323
  98.3 28.7 %copy-start.3 = (bf16[8,4,192,128]{3,2,1,0:T(8,128)(2,1)}, bf16[8,4,192,128]{3,2,1,0:T(8,128)(2,1)S(1)}, u32[]{:S(2)}) copy-start(bf16[8,4,192,128]{3,2,1,0:T(8,128)(2,1)S(1)} %get-tuple-element.42) | copy-start | bytes 4718596
  103.3 15.6 %all-to-all-start.3 = ((bf16[64,2,128]{2,1,0:T(2,128)(2,1)}), bf16[64,2,128]{2,1,0:T(2,128)(2,1)S(1)}, u32[]{:S(2)}, u32[]{:S(2)}) async-start(bf16[64,2,128]{2,1,0:T(2,128)(2,1)} %bitcast.17), calls=%async_computation.3 | async-start | bytes 65536 | tf_op jit(solution)/shard_map/all_to_all | solution.py:323
  109.6 9.3 %collective-permute-start.10 = (bf16[6144,128]{1,0:T(8,128)(2,1)S(1)}, bf16[6144,128]{1,0:T(8,128)(2,1)}, u32[]{:S(2)}, u32[]{:S(2)}) collective-permute-start(bf16[6144,128]{1,0:T(8,128)(2,1)S(1)} %bitcast.31), channel_id=1, source_target_pairs={{0,1},{1,0},{2,3},{3,2},{4,5},{5,4},{6,7},{7,6},{8,9},{9,8},{10,11... | collective-permute-start | bytes 4718600 | tf_op jit(solution)/shard_map/ppermute | solution.py:37
  111.9 6.9 %collective-permute-start.5 = (f32[136,128]{1,0:T(8,128)S(1)}, f32[136,128]{1,0:T(8,128)S(1)}, u32[]{:S(2)}, u32[]{:S(2)}) collective-permute-start(f32[136,128]{1,0:T(8,128)S(1)} %get-tuple-element.30), channel_id=1, source_target_pairs={{0,1},{1,0},{2,3},{3,2},{4,5},{5,4},{6,7},{7,6},{8,9},{9,8},{10,11... | collective-permute-start | bytes 208904 | tf_op jit(solution)/shard_map/ppermute | solution.py:37
  121.2 15.9 %copy-start.8 = (bf16[136,128]{1,0:T(8,128)(2,1)}, bf16[136,128]{1,0:T(8,128)(2,1)S(1)}, u32[]{:S(2)}) copy-start(bf16[136,128]{1,0:T(8,128)(2,1)S(1)} %get-tuple-element.41.refs_3_) | copy-start | bytes 104452
  121.2 15.2 %all-to-all-start.4 = ((bf16[64,2,128]{2,1,0:T(2,128)(2,1)}), bf16[64,2,128]{2,1,0:T(2,128)(2,1)S(1)}, u32[]{:S(2)}, u32[]{:S(2)}) async-start(bf16[64,2,128]{2,1,0:T(2,128)(2,1)} %bitcast.22), calls=%async_computation.4 | async-start | bytes 65536 | tf_op jit(solution)/shard_map/all_to_all | solution.py:323
  127.1 14.7 %collective-permute-start.11 = (bf16[6144,128]{1,0:T(8,128)(2,1)S(1)}, bf16[6144,128]{1,0:T(8,128)(2,1)S(1)}, u32[]{:S(2)}, u32[]{:S(2)}) collective-permute-start(bf16[6144,128]{1,0:T(8,128)(2,1)S(1)} %bitcast.39), channel_id=1, source_target_pairs={{0,1},{1,0},{2,3},{3,2},{4,5},{5,4},{6,7},{7,6},{8,9},{9,8},{10,11... | collective-permute-start | bytes 4718600 | tf_op jit(solution)/shard_map/ppermute | solution.py:37
  137.1 14.1 %all-to-all-start.5 = ((bf16[64,2,128]{2,1,0:T(2,128)(2,1)}), bf16[64,2,128]{2,1,0:T(2,128)(2,1)S(1)}, u32[]{:S(2)}, u32[]{:S(2)}) async-start(bf16[64,2,128]{2,1,0:T(2,128)(2,1)} %bitcast.24), calls=%async_computation.5 | async-start | bytes 65536 | tf_op jit(solution)/shard_map/all_to_all | solution.py:323
  (10 other events, 41.8 us)

commit v7 on v5

v7 whole, which is shorter than its diff:
```python
import functools

import jax
import jax.numpy as jnp
from jax import lax
from jax.experimental import pallas as pl
from jax.experimental.pallas import tpu as pltpu
from jax.sharding import Mesh
from jax.sharding import PartitionSpec as P

SEQ = ("x", "z", "core")
DP_SEQ = ("dp", "x", "z", "core")
ROWS = ("dp", "z")
BF16 = jnp.bfloat16
F32 = jnp.float32
LIMIT = 16 * 1024 * 1024
LONG = 30_000_000_000
ANY = pl.BlockSpec(memory_space=pl.ANY)
VMEM = pl.BlockSpec(memory_space=pltpu.VMEM)


def contract(left, right, left_dim, right_dim):
    return lax.dot_general(
        left, right, (((left_dim,), (right_dim,)), ((), ())), preferred_element_type=F32
    )


def cost(flops, moved):
    return pl.CostEstimate(flops=flops, bytes_accessed=moved, transcendentals=0)


def after(value, *events):
    return lax.optimization_barrier((value, *events))[0]


def core_swap(block):
    return lax.ppermute(block, "core", [(0, 1), (1, 0)])


def in_hbm(*values):
    return [pltpu.with_memory_space_constraint(v, pltpu.HBM) for v in values]


def project_kernel(shifts, *refs):
    tokens, blocks, outs, scratch = refs[:-11], refs[-11:-7], refs[-7:-4], refs[-4:]
    weight_ref, own_ref, send_ref = outs
    own_held, far_held, own_sem, far_sem = scratch
    rows = weight_ref.shape[0] // 32
    x, core = lax.axis_index("x"), lax.axis_index("core")

    def products(own, far):
        own_copy = pltpu.make_async_copy(own, own_held, own_sem)
        far_copy = pltpu.make_async_copy(far, far_held, far_sem)
        own_copy.start()
        far_copy.start()
        for k, ref in zip(shifts, blocks):
            source = lax.rem(x - k + 4, 4)
            for p in range(8):
                at = pl.multiple_of((p * 4 + source) * rows, 64)
                weight_ref[pl.ds(at, rows), :] = ref[p * rows : (p + 1) * rows, :]
        own_copy.wait()
        own_ref[...] = contract(own_held[...], weight_ref[...], 1, 0).astype(own_ref.dtype)
        far_copy.wait()
        send_ref[...] = contract(far_held[...], weight_ref[...], 1, 0).astype(send_ref.dtype)

    if len(tokens) == 2:
        products(*tokens)
    else:
        pl.when(core == 0)(lambda: products(*tokens[:2]))
        pl.when(core != 0)(lambda: products(*tokens[2:]))


def project(tokens, blocks, dtype):
    count, depth = tokens[0].shape
    row = jax.ShapeDtypeStruct((count, 128), dtype)
    return pl.pallas_call(
        functools.partial(project_kernel, tuple(blocks)),
        out_shape=[jax.ShapeDtypeStruct((depth, 128), BF16), row, row],
        in_specs=[ANY] * len(tokens) + [VMEM] * 4,
        out_specs=[VMEM] * 3,
        scratch_shapes=[pltpu.VMEM((count, depth), BF16)] * 2 + [pltpu.SemaphoreType.DMA] * 2,
        compiler_params=pltpu.CompilerParams(vmem_limit_bytes=LIMIT),
        cost_estimate=cost(LONG, 4 * count * depth + 4 * depth * 128),
    )(*in_hbm(*tokens), *blocks.values())


def state_kernel(own_ref, recv_ref, kv_ref, state_ref):
    own, recv = own_ref[...], recv_ref[...]
    first = lax.axis_index("core") == 0
    keys, values = jnp.where(first, own, recv), jnp.where(first, recv, own)
    kv_ref[:, :128] = keys
    kv_ref[:, 128:] = values
    state_ref[...] = contract(keys, values, 0, 0).astype(BF16)


def keys_values_state(own, recv):
    return pl.pallas_call(
        state_kernel,
        out_shape=[
            jax.ShapeDtypeStruct((own.shape[0], 256), BF16),
            jax.ShapeDtypeStruct((128, 128), BF16),
        ],
        in_specs=[VMEM] * 2,
        out_specs=[VMEM] * 2,
        compiler_params=pltpu.CompilerParams(vmem_limit_bytes=LIMIT),
        cost_estimate=cost(2 * own.size * 128, 8 * own.size),
    )(own, recv)


def gate_kernel(in_ref, out_ref):
    out_ref[...] = in_ref[...]


def gate(value):
    return pl.pallas_call(
        gate_kernel,
        out_shape=jax.ShapeDtypeStruct(value.shape, value.dtype),
        in_specs=[VMEM],
        out_specs=VMEM,
        compiler_params=pltpu.CompilerParams(vmem_limit_bytes=LIMIT),
        cost_estimate=cost(LONG, 4 * value.size),
    )(value)


def causal_of(count):
    rows = lax.broadcasted_iota(jnp.int32, (count, count), 0)
    return rows >= lax.broadcasted_iota(jnp.int32, (count, count), 1)


def grad_kernel(
    near_ref, far_ref, kv_ref, prior_ref, gain_ref, qa_ref, state_ref
):
    first = lax.axis_index("core") == 0
    near, far = near_ref[...], far_ref[...]
    queries = jnp.where(first, near, far).astype(BF16)
    head_grad = jnp.where(first, far, near)
    qa_ref[:, :128] = queries
    scores = contract(queries, kv_ref[:, :128], 1, 1)
    scores = jnp.where(causal_of(scores.shape[0]), scores, 0.0).astype(BF16)
    attended = contract(scores, kv_ref[:, 128:], 1, 0) + contract(queries, prior_ref[...], 1, 0)
    inv_rms = lax.rsqrt(jnp.mean(attended * attended, axis=-1, keepdims=True) + 1e-06)
    scaled = gain_ref[...] * head_grad
    mean = jnp.mean(attended * scaled, axis=-1, keepdims=True)
    attn_grad = inv_rms * scaled - attended * (inv_rms * inv_rms * inv_rms) * mean
    attn_grad = attn_grad.astype(BF16)
    qa_ref[:, 128:] = attn_grad
    state_ref[...] = contract(queries, attn_grad, 0, 0).astype(BF16)


def attention_grad(near, far, kv, prior, gain):
    count = kv.shape[0]
    return pl.pallas_call(
        grad_kernel,
        out_shape=[
            jax.ShapeDtypeStruct((count, 256), BF16),
            jax.ShapeDtypeStruct((128, 128), BF16),
        ],
        in_specs=[VMEM] * 5,
        out_specs=[VMEM] * 2,
        compiler_params=pltpu.CompilerParams(vmem_limit_bytes=LIMIT),
        cost_estimate=cost(LONG, 16 * count * 128),
    )(near, far, kv, prior, gain)


def inner_kernel(*refs):
    rows_any, (near_any, far_any), outs, scratch = refs[:3], refs[3:5], refs[5:8], refs[8:]
    base_ref, dk_ref, dv_ref = outs
    qa_ref, kv_ref, prior_ref, weight_ref, row_sems, weight_sem = scratch

    def body(weight_any):
        weight_copy = pltpu.make_async_copy(weight_any, weight_ref, weight_sem)
        copies = [
            pltpu.make_async_copy(source, target, row_sems.at[i])
            for i, (source, target) in enumerate(zip(rows_any, scratch[:3]))
        ]
        for copy in copies:
            copy.start()
        weight_copy.start()
        for copy in copies:
            copy.wait()
        attn_grad = qa_ref[:, 128:]
        causal = causal_of(attn_grad.shape[0])
        scores = contract(qa_ref[:, :128], kv_ref[:, :128], 1, 1)
        scores = jnp.where(causal, scores, 0.0).astype(BF16)
        prob = contract(attn_grad, kv_ref[:, 128:], 1, 1)
        prob = jnp.where(causal, prob, 0.0).astype(BF16)
        query_grad = contract(prob, kv_ref[:, :128], 1, 0) + contract(attn_grad, prior_ref[...], 1, 1)
        query_grad = query_grad.astype(BF16)
        dk_ref[...] = contract(prob, qa_ref[:, :128], 0, 0)
        dv_ref[...] = contract(scores, attn_grad, 0, 0)
        weight_copy.wait()
        part = weight_ref.shape[0] // 4
        for i in range(4):
            at = slice(i * part, (i + 1) * part)
            base_ref[:, at] = contract(query_grad, weight_ref[at, :], 1, 1)

    pl.when(lax.axis_index("core") == 0)(lambda: body(near_any))
    pl.when(lax.axis_index("core") != 0)(lambda: body(far_any))


def inner_grads(qa, kv, prior, near, far):
    count, depth = kv.shape[0], near.shape[0]
    rows = pltpu.VMEM((count, 256), BF16)
    return pl.pallas_call(
        inner_kernel,
        out_shape=[
            jax.ShapeDtypeStruct((count, depth), F32),
            jax.ShapeDtypeStruct((count, 128), F32),
            jax.ShapeDtypeStruct((count, 128), F32),
        ],
        in_specs=[ANY] * 5,
        out_specs=[VMEM] * 3,
        scratch_shapes=[
            rows,
            rows,
            pltpu.VMEM((128, 128), BF16),
            pltpu.VMEM((depth, 128), BF16),
            pltpu.SemaphoreType.DMA((3,)),
            pltpu.SemaphoreType.DMA,
        ],
        compiler_params=pltpu.CompilerParams(vmem_limit_bytes=LIMIT),
        cost_estimate=cost(LONG, 4 * count * depth + 4 * depth * 128),
    )(*in_hbm(qa, kv, prior, near, far))


def output_kernel(
    base, dk, dv, kv_any, later, near_any, far_any, out_any,
    kv_ref, near_ref, far_ref, out_ref, row_sem, weight_sems, out_sems,
):
    steps, _, part = out_ref.shape
    rows = [pltpu.make_async_copy(kv_any, kv_ref, row_sem)]
    weights = []
    for i in range(steps):
        at = pl.ds(i * part, part)
        for n, (source, target) in enumerate(((near_any, near_ref), (far_any, far_ref))):
            weights.append(
                pltpu.make_async_copy(source.at[at], target.at[at], weight_sems.at[2 * i + n])
            )
    for copy in rows + weights:
        copy.start()
    for copy in rows:
        copy.wait()
    first = lax.axis_index("core") == 0
    key_grad = (dk[...] + contract(kv_ref[:, 128:], later[...], 1, 1)).astype(BF16)
    value_grad = (dv[...] + contract(kv_ref[:, :128], later[...], 1, 0)).astype(BF16)
    near_grad = jnp.where(first, key_grad, value_grad)
    far_grad = jnp.where(first, value_grad, key_grad)
    joined = jnp.concatenate([near_grad, far_grad], axis=1)
    outs = []
    for i in range(steps):
        weights[2 * i].wait()
        weights[2 * i + 1].wait()
        at = slice(i * part, (i + 1) * part)
        weight = jnp.concatenate([near_ref[at, :], far_ref[at, :]], axis=1)
        out_ref[i] = (base[:, at] + contract(joined, weight, 1, 1)).astype(BF16)
        copy = pltpu.make_async_copy(
            out_ref.at[i], out_any.at[:, pl.ds(i * part, part)], out_sems.at[i]
        )
        copy.start()
        outs.append(copy)
    for copy in outs:
        copy.wait()


def output(base, dk, dv, kv, later, near, far):
    count, depth = base.shape
    steps = 4
    return pl.pallas_call(
        output_kernel,
        out_shape=jax.ShapeDtypeStruct((count, depth), BF16),
        in_specs=[VMEM] * 3 + [ANY] + [VMEM] + [ANY] * 2,
        out_specs=ANY,
        scratch_shapes=[
            pltpu.VMEM((count, 256), BF16),
            pltpu.VMEM((depth, 128), BF16),
            pltpu.VMEM((depth, 128), BF16),
            pltpu.VMEM((steps, count, depth // steps), BF16),
            pltpu.SemaphoreType.DMA,
            pltpu.SemaphoreType.DMA((2 * steps,)),
            pltpu.SemaphoreType.DMA((steps,)),
        ],
        compiler_params=pltpu.CompilerParams(vmem_limit_bytes=LIMIT),
        cost_estimate=cost(4 * count * depth * 128, 4 * depth * 128 + 6 * count * depth),
    )(base, dk, dv, *in_hbm(kv), later, *in_hbm(near, far))


def sums_kernel(reverse, in_ref, out_ref):
    each = in_ref.shape[0] // 64
    to = lax.broadcasted_iota(jnp.int32, (128, 128), 0)
    frm = lax.broadcasted_iota(jnp.int32, (128, 128), 1)
    others = (frm // each > to // each) if reverse else (frm // each < to // each)
    mask = jnp.where(others & (frm % each == to % each), 1.0, 0.0).astype(BF16)
    out_ref[...] = contract(mask, in_ref[...], 1, 0).astype(BF16)


def sums_of(pieces, reverse):
    return pl.pallas_call(
        functools.partial(sums_kernel, reverse),
        out_shape=jax.ShapeDtypeStruct(pieces.shape, BF16),
        in_specs=[VMEM],
        out_specs=VMEM,
        compiler_params=pltpu.CompilerParams(vmem_limit_bytes=LIMIT),
        cost_estimate=cost(LONG, 4 * pieces.size),
    )(pieces)


def exchange(state):
    peers, head = lax.axis_size(SEQ), state.shape[1]
    pieces = state.reshape(peers, -1, head)
    return lax.all_to_all(pieces, SEQ, 0, 0, tiled=True).reshape(state.shape)


def per_device(inputs, w_project, w_output, norm_gain, out_grad):
    tokens = inputs[0]
    grads_in = out_grad[0]
    head = w_output.shape[1]
    dps, zs, xs = lax.axis_size("dp"), lax.axis_size("z"), lax.axis_size("x")
    on_first = lax.axis_index("core") == 0

    rows = jnp.concatenate([w_project.reshape(-1, 3 * head), w_output], axis=1)
    rows = lax.all_gather(rows, "core", axis=0, tiled=True)
    kv_rows = jnp.where(on_first, rows[:, head : 2 * head], rows[:, 2 * head : 3 * head])
    qo_rows = jnp.where(on_first, rows[:, :head], rows[:, 3 * head :])

    def copied(block):
        return jnp.broadcast_to(block[None], (dps * zs, *block.shape))

    def over_planes(copies):
        return lax.all_to_all(copies, ROWS, 0, 0, tiled=True).reshape(-1, head)

    def over_x(block):
        shifts = {k: lax.ppermute(block, "x", [(i, (i + k) % xs) for i in range(xs)]) for k in (2, 1, 3)}
        return {1: shifts[1], 3: shifts[3], 2: shifts[2], 0: block}

    kv_copies = copied(kv_rows)
    tokens_far = core_swap(after(tokens, kv_copies))
    grads_far = core_swap(after(grads_in, kv_copies))
    kv_plane = over_planes(kv_copies)
    qo_plane = over_planes(copied(gate(after(qo_rows, kv_plane))))
    tokens_far = after(tokens_far, grads_far)
    kv_near, own, send = project((tokens, tokens_far), over_x(kv_plane), BF16)
    own, qo_plane = lax.optimization_barrier((own, qo_plane))
    kv, local_state = keys_values_state(own, core_swap(send))

    qo = over_x(after(qo_plane, local_state))
    prior_state = gate(exchange(sums_of(exchange(local_state), False)))
    qo_near, own, send = project(
        (tokens, tokens_far, grads_in, grads_far), qo, F32
    )
    recv = after(core_swap(send), prior_state)
    qa, local_grad = attention_grad(own, recv, kv, prior_state, norm_gain.reshape(1, head))
    kv_far = core_swap(kv_near)
    grad_pieces = exchange(local_grad)
    qo_far = core_swap(qo_near)
    base, *grads = inner_grads(qa, kv, prior_state, qo_near, qo_far)
    later_state = exchange(sums_of(grad_pieces, True))
    result = output(base, *grads, kv, later_state, kv_near, kv_far)
    return result[None]


def solution(mesh):
    split = Mesh(mesh.devices.reshape(mesh.shape["dp"], 4, 8, 2), DP_SEQ)
    in_specs = (P("dp", SEQ, None), P(DP_SEQ, None, None), P(DP_SEQ, None), P(), P("dp", SEQ, None))
    out_specs = P("dp", SEQ, None)
    return jax.shard_map(
        per_device, mesh=split, in_specs=in_specs, out_specs=out_specs, check_vma=False
    )
```

time: 152 us -> 150 us (0.987)
  Pallas kernels: 19.4 us -> 16.2 us
  waiting for transfers between devices: 30.2 us -> 31.9 us
  transfers between devices with their start and end apart: 18 -> 18, of which waited for: 9 -> 9; matrix products, arithmetic and copies ran while one was open for 1% -> 1% of each run, Pallas kernels for 8% -> 7%
where the time goes in v7:
time: 150 us; the launch traced here: 149 us
  starting transfers between devices  88 us (59%)
  waiting for transfers between devices  31.9 us (21%)
  Pallas kernels  16.2 us (11%)
  blocking collectives  8.36 us (6%)
  local copies, waits for them, and re-layouts  3.59 us (2%)
    all_to_all x4, starting transfers between devices, exchange(): return lax.all_to_all(pieces, SEQ, 0, 0, tiled=True).reshape(state.shape)  34.4 us
    ppermute x6, starting transfers between devices, over_x(): lax.ppermute(block, 'x', [(i, (i + k) % xs) for i in range(xs)])  20.1 us
    all_to_all x2, starting transfers between devices, over_planes(): return lax.all_to_all(copies, ROWS, 0, 0, tiled=True).reshape(-1, head)  17.4 us
    ppermute x6, starting transfers between devices, core_swap(): return lax.ppermute(block, 'core', [(0, 1), (1, 0)])  16 us
    all_to_all x4, waiting for transfers between devices, exchange(): return lax.all_to_all(pieces, SEQ, 0, 0, tiled=True).reshape(state.shape)  13.7 us
    all_to_all x2, waiting for transfers between devices, over_planes(): return lax.all_to_all(copies, ROWS, 0, 0, tiled=True).reshape(-1, head)  12.2 us
    all_gather x1, blocking collectives, per_device(): rows = lax.all_gather(rows, 'core', axis=0, tiled=True)  8.36 us
    ppermute x6, waiting for transfers between devices, over_x(): lax.ppermute(block, 'x', [(i, (i + k) % xs) for i in range(xs)])  6.04 us
  transfers between devices with their start and end apart: 18, of which 9 were waited for; matrix products, arithmetic and copies ran while one was open for 1% of the time, Pallas kernels for 7%

profile of v7, /device:TPU:1, one launch (start us, length us, event | category | flops | bytes accessed | tf_op | source)
XLA Modules:
  0.0 149.3 jit_solution(16307911659536420427)
XLA Ops:
  1.4 8.4 %all-gather = bf16[2,12,512]{2,1,0:T(8,128)(2,1)S(1)} all-gather(bf16[1,12,512]{2,1,0:T(8,128)(2,1)S(1)} %maximum_bitcast_fusion), channel_id=1, replica_groups=mesh['dp'=8,'x'=4,'z'=8,'core'=2] {'core'}, dimensions={0}, use_global_device_ids=true | all-gather | bytes 36864 | tf_op jit(solution)/shard_map/all_gather | solution.py:321
  10.6 10.9 %all-to-all-start = ((bf16[64,24,128]{2,1,0:T(8,128)(2,1)}), bf16[64,24,128]{2,1,0:T(8,128)(2,1)S(1)}, u32[]{:S(2)}, u32[]{:S(2)}) async-start(bf16[64,24,128]{2,1,0:T(8,128)(2,1)} %broadcast_in_dim.6), calls=%async_computation | async-start | bytes 786432 | tf_op jit(solution)/shard_map/all_to_all | solution.py:329
  21.6 2.5 %collective-permute-start = (bf16[136,6144]{1,0:T(8,128)(2,1)}, bf16[136,6144]{1,0:T(8,128)(2,1)}, u32[]{:S(2)}, u32[]{:S(2)}) collective-permute-start(bf16[136,6144]{1,0:T(8,128)(2,1)} %bitcast.34), channel_id=1, source_target_pairs={{0,1},{1,0},{2,3},{3,2},{4,5},{5,4},{6,7},{7,6},{8,9},{9,8},{10,11... | collective-permute-start | bytes 5013512 | tf_op jit(solution)/shard_map/ppermute | solution.py:37
  26.0 10.5 %all-to-all-done = bf16[64,24,128]{2,1,0:T(8,128)(2,1)S(1)} async-done(((bf16[64,24,128]{2,1,0:T(8,128)(2,1)}), bf16[64,24,128]{2,1,0:T(8,128)(2,1)S(1)}, u32[]{:S(2)}, u32[]{:S(2)}) %all-to-all-start) | async-done | bytes 393248 | tf_op jit(solution)/shard_map/all_to_all | solution.py:329
  36.6 4.6 %collective-permute-start.4 = (bf16[1536,128]{1,0:T(8,128)(2,1)S(1)}, bf16[1536,128]{1,0:T(8,128)(2,1)S(1)}, u32[]{:S(2)}, u32[]{:S(2)}) collective-permute-start(bf16[1536,128]{1,0:T(8,128)(2,1)S(1)} %bitcast.23), channel_id=1, source_target_pairs={{0,32},{16,48},{32,0},{48,16},{1,33},{17,49},{33,1},{49,17},{2,34}... | collective-permute-start | bytes 1179656 | tf_op jit(solution)/shard_map/ppermute | solution.py:332
  41.2 2.8 %collective-permute-start.3 = (bf16[1536,128]{1,0:T(8,128)(2,1)S(1)}, bf16[1536,128]{1,0:T(8,128)(2,1)S(1)}, u32[]{:S(2)}, u32[]{:S(2)}) collective-permute-start(bf16[1536,128]{1,0:T(8,128)(2,1)S(1)} %bitcast.24), channel_id=1, source_target_pairs={{0,48},{16,0},{32,16},{48,32},{1,49},{17,1},{33,17},{49,33},{2,50}... | collective-permute-start | bytes 1179656 | tf_op jit(solution)/shard_map/ppermute | solution.py:332
  44.0 2.5 %collective-permute-start.2 = (bf16[1536,128]{1,0:T(8,128)(2,1)S(1)}, bf16[1536,128]{1,0:T(8,128)(2,1)S(1)}, u32[]{:S(2)}, u32[]{:S(2)}) collective-permute-start(bf16[1536,128]{1,0:T(8,128)(2,1)S(1)} %bitcast.25), channel_id=1, source_target_pairs={{0,16},{16,32},{32,48},{48,0},{1,17},{17,33},{33,49},{49,1},{2,18}... | collective-permute-start | bytes 1179656 | tf_op jit(solution)/shard_map/ppermute | solution.py:332
  47.3 6.5 %all-to-all-start.1 = ((bf16[64,24,128]{2,1,0:T(8,128)(2,1)}), bf16[64,24,128]{2,1,0:T(8,128)(2,1)S(1)}, u32[]{:S(2)}, u32[]{:S(2)}) async-start(bf16[64,24,128]{2,1,0:T(8,128)(2,1)} %broadcast_in_dim.7), calls=%async_computation.1 | async-start | bytes 786432 | tf_op jit(solution)/shard_map/all_to_all | solution.py:329
  53.9 4.1 %collective-permute-done.3.refs_3_ = bf16[1536,128]{1,0:T(8,128)(2,1)S(1)} collective-permute-done((bf16[1536,128]{1,0:T(8,128)(2,1)S(1)}, bf16[1536,128]{1,0:T(8,128)(2,1)S(1)}, u32[]{:S(2)}, u32[]{:S(2)}) %collective-permute-start.3) | collective-permute-done | bytes 393248 | tf_op jit(solution)/shard_map/ppermute | solution.py:332
  58.2 3.2 %shard_map.55 = (bf16[6144,128]{1,0:T(8,128)(2,1)}, bf16[136,128]{1,0:T(8,128)(2,1)S(1)}, bf16[136,128]{1,0:T(8,128)(2,1)S(1)}) custom-call(bf16[136,6144]{1,0:T(8,128)(2,1)} %bitcast.35, bf16[136,6144]{1,0:T(8,128)(2,1)} %collective-permute-done.refs_1_, bf16[1536,128]{1,0:T(8,128)(2,1)S(1)} %collective-permute-done.2.refs_2_, ...), custom_call_target="tpu_custom_call" | custom-call | flops 30000001024 | bytes 6488064 | tf_op jit(solution)/shard_map/pallas_call | solution.py:76
  61.5 4.3 %collective-permute-start.5 = (bf16[136,128]{1,0:T(8,128)(2,1)S(1)}, bf16[136,128]{1,0:T(8,128)(2,1)S(1)}, u32[]{:S(2)}, u32[]{:S(2)}) collective-permute-start(bf16[136,128]{1,0:T(8,128)(2,1)S(1)} %get-tuple-element.33), channel_id=1, source_target_pairs={{0,1},{1,0},{2,3},{3,2},{4,5},{5,4},{6,7},{7,6},{8,9},{9,8},{10,11... | collective-permute-start | bytes 104456 | tf_op jit(solution)/shard_map/ppermute | solution.py:37
  68.2 10.4 %all-to-all-start.2 = ((bf16[64,2,128]{2,1,0:T(2,128)(2,1)}), bf16[64,2,128]{2,1,0:T(2,128)(2,1)S(1)}, u32[]{:S(2)}, u32[]{:S(2)}) async-start(bf16[64,2,128]{2,1,0:T(2,128)(2,1)} %bitcast.5), calls=%async_computation.2 | async-start | bytes 65536 | tf_op jit(solution)/shard_map/all_to_all | solution.py:310
  78.6 4.9 %collective-permute-start.8 = (bf16[1536,128]{1,0:T(8,128)(2,1)S(1)}, bf16[1536,128]{1,0:T(8,128)(2,1)S(1)}, u32[]{:S(2)}, u32[]{:S(2)}) collective-permute-start(bf16[1536,128]{1,0:T(8,128)(2,1)S(1)} %bitcast.19), channel_id=1, source_target_pairs={{0,32},{16,48},{32,0},{48,16},{1,33},{17,49},{33,1},{49,17},{2,34}... | collective-permute-start | bytes 1179656 | tf_op jit(solution)/shard_map/ppermute | solution.py:332
  83.5 2.7 %collective-permute-start.7 = (bf16[1536,128]{1,0:T(8,128)(2,1)S(1)}, bf16[1536,128]{1,0:T(8,128)(2,1)S(1)}, u32[]{:S(2)}, u32[]{:S(2)}) collective-permute-start(bf16[1536,128]{1,0:T(8,128)(2,1)S(1)} %bitcast.20), channel_id=1, source_target_pairs={{0,48},{16,0},{32,16},{48,32},{1,49},{17,1},{33,17},{49,33},{2,50}... | collective-permute-start | bytes 1179656 | tf_op jit(solution)/shard_map/ppermute | solution.py:332
  86.2 2.6 %collective-permute-start.6 = (bf16[1536,128]{1,0:T(8,128)(2,1)S(1)}, bf16[1536,128]{1,0:T(8,128)(2,1)S(1)}, u32[]{:S(2)}, u32[]{:S(2)}) collective-permute-start(bf16[1536,128]{1,0:T(8,128)(2,1)S(1)} %bitcast.21), channel_id=1, source_target_pairs={{0,16},{16,32},{32,48},{48,0},{1,17},{17,33},{33,49},{49,1},{2,18}... | collective-permute-start | bytes 1179656 | tf_op jit(solution)/shard_map/ppermute | solution.py:332
  89.6 10.2 %all-to-all-start.3 = ((bf16[64,2,128]{2,1,0:T(2,128)(2,1)}), bf16[64,2,128]{2,1,0:T(2,128)(2,1)S(1)}, u32[]{:S(2)}, u32[]{:S(2)}) async-start(bf16[64,2,128]{2,1,0:T(2,128)(2,1)} %bitcast.7), calls=%async_computation.3 | async-start | bytes 65536 | tf_op jit(solution)/shard_map/all_to_all | solution.py:310
  101.4 2.7 %shard_map.58 = (bf16[6144,128]{1,0:T(8,128)(2,1)S(1)}, f32[136,128]{1,0:T(8,128)S(1)}, f32[136,128]{1,0:T(8,128)S(1)}) custom-call(bf16[136,6144]{1,0:T(8,128)(2,1)} %bitcast.36, bf16[136,6144]{1,0:T(8,128)(2,1)} %collective-permute-done.refs_1_, bf16[136,6144]{1,0:T(8,128)(2,1)} %bitcast.38, bf16[136,6144]{1,0:T(8,128)(2,1)} %collective-permute-done.1.refs_3_, ...), custom_call_target="tpu_custom_call" | custom-call | flops 30000001024 | bytes 6488064 | tf_op jit(solution)/shard_map/pallas_call | solution.py:76
  104.2 3.0 %collective-permute-start.9 = (f32[136,128]{1,0:T(8,128)S(1)}, f32[136,128]{1,0:T(8,128)S(1)}, u32[]{:S(2)}, u32[]{:S(2)}) collective-permute-start(f32[136,128]{1,0:T(8,128)S(1)} %get-tuple-element.37), channel_id=1, source_target_pairs={{0,1},{1,0},{2,3},{3,2},{4,5},{5,4},{6,7},{7,6},{8,9},{9,8},{10,11... | collective-permute-start | bytes 208904 | tf_op jit(solution)/shard_map/ppermute | solution.py:37
  111.4 8.5 %all-to-all-start.4 = ((bf16[64,2,128]{2,1,0:T(2,128)(2,1)}), bf16[64,2,128]{2,1,0:T(2,128)(2,1)S(1)}, u32[]{:S(2)}, u32[]{:S(2)}) async-start(bf16[64,2,128]{2,1,0:T(2,128)(2,1)} %bitcast.10), calls=%async_computation.4 | async-start | bytes 65536 | tf_op jit(solution)/shard_map/all_to_all | solution.py:310
  124.3 4.9 %all-to-all-done.4 = bf16[64,2,128]{2,1,0:T(2,128)(2,1)S(1)} async-done(((bf16[64,2,128]{2,1,0:T(2,128)(2,1)}), bf16[64,2,128]{2,1,0:T(2,128)(2,1)S(1)}, u32[]{:S(2)}, u32[]{:S(2)}) %all-to-all-start.4) | async-done | bytes 32800 | tf_op jit(solution)/shard_map/all_to_all | solution.py:310
  130.0 5.4 %all-to-all-start.5 = ((bf16[64,2,128]{2,1,0:T(2,128)(2,1)}), bf16[64,2,128]{2,1,0:T(2,128)(2,1)S(1)}, u32[]{:S(2)}, u32[]{:S(2)}) async-start(bf16[64,2,128]{2,1,0:T(2,128)(2,1)} %bitcast.12), calls=%async_computation.5 | async-start | bytes 65536 | tf_op jit(solution)/shard_map/all_to_all | solution.py:310
  135.4 2.4 %shard_map.62 = (f32[136,6144]{1,0:T(8,128)S(1)}, f32[136,128]{1,0:T(8,128)S(1)}, f32[136,128]{1,0:T(8,128)S(1)}) custom-call(bf16[136,256]{1,0:T(8,128)(2,1)} %copy-done.3, bf16[136,256]{1,0:T(8,128)(2,1)} %copy-done, bf16[128,128]{1,0:T(8,128)(2,1)} %copy-done.4, bf16[6144,128]{1,0:T(8,128)(2,1)} %copy-done.1, ...), custom_call_target="tpu_custom_call" | custom-call | flops 30000001024 | bytes 6488064 | tf_op jit(solution)/shard_map/pallas_call | solution.py:204
  137.8 6.9 %all-to-all-done.5 = bf16[64,2,128]{2,1,0:T(2,128)(2,1)S(1)} async-done(((bf16[64,2,128]{2,1,0:T(2,128)(2,1)}), bf16[64,2,128]{2,1,0:T(2,128)(2,1)S(1)}, u32[]{:S(2)}, u32[]{:S(2)}) %all-to-all-start.5) | async-done | bytes 32800 | tf_op jit(solution)/shard_map/all_to_all | solution.py:310
  144.7 4.4 %shard_map.64 = bf16[136,6144]{1,0:T(8,128)(2,1)} custom-call(f32[136,6144]{1,0:T(8,128)S(1)} %get-tuple-element.42.base, f32[136,128]{1,0:T(8,128)S(1)} %get-tuple-element.43.dk, f32[136,128]{1,0:T(8,128)S(1)} %get-tuple-element.44.dv, bf16[136,256]{1,0:T(8,128)(2,1)} %copy-done, bf16[128,128]{1,0:T(8,128)(2,1)S(1)} %bitcast.27, ...), custom_call_target="tpu_custom_call" | custom-call | flops 427819008 | bytes 8159232 | tf_op jit(solution)/shard_map/pallas_call | solution.py:268
  (40 shorter events, 19.5 us)
Async XLA Ops:
  10.6 25.9 %all-to-all-start = ((bf16[64,24,128]{2,1,0:T(8,128)(2,1)}), bf16[64,24,128]{2,1,0:T(8,128)(2,1)S(1)}, u32[]{:S(2)}, u32[]{:S(2)}) async-start(bf16[64,24,128]{2,1,0:T(8,128)(2,1)} %broadcast_in_dim.6), calls=%async_computation | async-start | bytes 786432 | tf_op jit(solution)/shard_map/all_to_all | solution.py:329
  21.6 32.3 %collective-permute-start = (bf16[136,6144]{1,0:T(8,128)(2,1)}, bf16[136,6144]{1,0:T(8,128)(2,1)}, u32[]{:S(2)}, u32[]{:S(2)}) collective-permute-start(bf16[136,6144]{1,0:T(8,128)(2,1)} %bitcast.34), channel_id=1, source_target_pairs={{0,1},{1,0},{2,3},{3,2},{4,5},{5,4},{6,7},{7,6},{8,9},{9,8},{10,11... | collective-permute-start | bytes 5013512 | tf_op jit(solution)/shard_map/ppermute | solution.py:37
  24.1 29.7 %collective-permute-start.1 = (bf16[136,6144]{1,0:T(8,128)(2,1)}, bf16[136,6144]{1,0:T(8,128)(2,1)}, u32[]{:S(2)}, u32[]{:S(2)}) collective-permute-start(bf16[136,6144]{1,0:T(8,128)(2,1)} %bitcast.37), channel_id=1, source_target_pairs={{0,1},{1,0},{2,3},{3,2},{4,5},{5,4},{6,7},{7,6},{8,9},{9,8},{10,11... | collective-permute-start | bytes 5013512 | tf_op jit(solution)/shard_map/ppermute | solution.py:37
  36.6 17.3 %collective-permute-start.4 = (bf16[1536,128]{1,0:T(8,128)(2,1)S(1)}, bf16[1536,128]{1,0:T(8,128)(2,1)S(1)}, u32[]{:S(2)}, u32[]{:S(2)}) collective-permute-start(bf16[1536,128]{1,0:T(8,128)(2,1)S(1)} %bitcast.23), channel_id=1, source_target_pairs={{0,32},{16,48},{32,0},{48,16},{1,33},{17,49},{33,1},{49,17},{2,34}... | collective-permute-start | bytes 1179656 | tf_op jit(solution)/shard_map/ppermute | solution.py:332
  41.2 16.7 %collective-permute-start.3 = (bf16[1536,128]{1,0:T(8,128)(2,1)S(1)}, bf16[1536,128]{1,0:T(8,128)(2,1)S(1)}, u32[]{:S(2)}, u32[]{:S(2)}) collective-permute-start(bf16[1536,128]{1,0:T(8,128)(2,1)S(1)} %bitcast.24), channel_id=1, source_target_pairs={{0,48},{16,0},{32,16},{48,32},{1,49},{17,1},{33,17},{49,33},{2,50}... | collective-permute-start | bytes 1179656 | tf_op jit(solution)/shard_map/ppermute | solution.py:332
  44.0 14.3 %collective-permute-start.2 = (bf16[1536,128]{1,0:T(8,128)(2,1)S(1)}, bf16[1536,128]{1,0:T(8,128)(2,1)S(1)}, u32[]{:S(2)}, u32[]{:S(2)}) collective-permute-start(bf16[1536,128]{1,0:T(8,128)(2,1)S(1)} %bitcast.25), channel_id=1, source_target_pairs={{0,16},{16,32},{32,48},{48,0},{1,17},{17,33},{33,49},{49,1},{2,18}... | collective-permute-start | bytes 1179656 | tf_op jit(solution)/shard_map/ppermute | solution.py:332
  47.3 20.1 %all-to-all-start.1 = ((bf16[64,24,128]{2,1,0:T(8,128)(2,1)}), bf16[64,24,128]{2,1,0:T(8,128)(2,1)S(1)}, u32[]{:S(2)}, u32[]{:S(2)}) async-start(bf16[64,24,128]{2,1,0:T(8,128)(2,1)} %broadcast_in_dim.7), calls=%async_computation.1 | async-start | bytes 786432 | tf_op jit(solution)/shard_map/all_to_all | solution.py:329
  61.5 5.9 %collective-permute-start.5 = (bf16[136,128]{1,0:T(8,128)(2,1)S(1)}, bf16[136,128]{1,0:T(8,128)(2,1)S(1)}, u32[]{:S(2)}, u32[]{:S(2)}) collective-permute-start(bf16[136,128]{1,0:T(8,128)(2,1)S(1)} %get-tuple-element.33), channel_id=1, source_target_pairs={{0,1},{1,0},{2,3},{3,2},{4,5},{5,4},{6,7},{7,6},{8,9},{9,8},{10,11... | collective-permute-start | bytes 104456 | tf_op jit(solution)/shard_map/ppermute | solution.py:37
  68.2 40.8 %copy-start = (bf16[136,256]{1,0:T(8,128)(2,1)}, bf16[136,256]{1,0:T(8,128)(2,1)S(1)}, u32[]{:S(2)}) copy-start(bf16[136,256]{1,0:T(8,128)(2,1)S(1)} %get-tuple-element.39.kv_ref.refs_1_.kv_any) | copy-start | bytes 208900
  68.2 20.6 %all-to-all-start.2 = ((bf16[64,2,128]{2,1,0:T(2,128)(2,1)}), bf16[64,2,128]{2,1,0:T(2,128)(2,1)S(1)}, u32[]{:S(2)}, u32[]{:S(2)}) async-start(bf16[64,2,128]{2,1,0:T(2,128)(2,1)} %bitcast.5), calls=%async_computation.2 | async-start | bytes 65536 | tf_op jit(solution)/shard_map/all_to_all | solution.py:310
  78.6 21.1 %collective-permute-start.8 = (bf16[1536,128]{1,0:T(8,128)(2,1)S(1)}, bf16[1536,128]{1,0:T(8,128)(2,1)S(1)}, u32[]{:S(2)}, u32[]{:S(2)}) collective-permute-start(bf16[1536,128]{1,0:T(8,128)(2,1)S(1)} %bitcast.19), channel_id=1, source_target_pairs={{0,32},{16,48},{32,0},{48,16},{1,33},{17,49},{33,1},{49,17},{2,34}... | collective-permute-start | bytes 1179656 | tf_op jit(solution)/shard_map/ppermute | solution.py:332
  83.5 17.8 %collective-permute-start.7 = (bf16[1536,128]{1,0:T(8,128)(2,1)S(1)}, bf16[1536,128]{1,0:T(8,128)(2,1)S(1)}, u32[]{:S(2)}, u32[]{:S(2)}) collective-permute-start(bf16[1536,128]{1,0:T(8,128)(2,1)S(1)} %bitcast.20), channel_id=1, source_target_pairs={{0,48},{16,0},{32,16},{48,32},{1,49},{17,1},{33,17},{49,33},{2,50}... | collective-permute-start | bytes 1179656 | tf_op jit(solution)/shard_map/ppermute | solution.py:332
  86.2 15.2 %collective-permute-start.6 = (bf16[1536,128]{1,0:T(8,128)(2,1)S(1)}, bf16[1536,128]{1,0:T(8,128)(2,1)S(1)}, u32[]{:S(2)}, u32[]{:S(2)}) collective-permute-start(bf16[1536,128]{1,0:T(8,128)(2,1)S(1)} %bitcast.21), channel_id=1, source_target_pairs={{0,16},{16,32},{32,48},{48,0},{1,17},{17,33},{33,49},{49,1},{2,18}... | collective-permute-start | bytes 1179656 | tf_op jit(solution)/shard_map/ppermute | solution.py:332
  89.6 19.5 %all-to-all-start.3 = ((bf16[64,2,128]{2,1,0:T(2,128)(2,1)}), bf16[64,2,128]{2,1,0:T(2,128)(2,1)S(1)}, u32[]{:S(2)}, u32[]{:S(2)}) async-start(bf16[64,2,128]{2,1,0:T(2,128)(2,1)} %bitcast.7), calls=%async_computation.3 | async-start | bytes 65536 | tf_op jit(solution)/shard_map/all_to_all | solution.py:310
  104.1 18.2 %copy-start.1 = (bf16[6144,128]{1,0:T(8,128)(2,1)}, bf16[6144,128]{1,0:T(8,128)(2,1)S(1)}, u32[]{:S(2)}) copy-start(bf16[6144,128]{1,0:T(8,128)(2,1)S(1)} %get-tuple-element.41.refs_3_) | copy-start | bytes 4718596
  104.2 4.9 %collective-permute-start.9 = (f32[136,128]{1,0:T(8,128)S(1)}, f32[136,128]{1,0:T(8,128)S(1)}, u32[]{:S(2)}, u32[]{:S(2)}) collective-permute-start(f32[136,128]{1,0:T(8,128)S(1)} %get-tuple-element.37), channel_id=1, source_target_pairs={{0,1},{1,0},{2,3},{3,2},{4,5},{5,4},{6,7},{7,6},{8,9},{9,8},{10,11... | collective-permute-start | bytes 208904 | tf_op jit(solution)/shard_map/ppermute | solution.py:37
  109.0 0.7 copy-start.2
  109.0 1.8 %copy-start.4 = (bf16[128,128]{1,0:T(8,128)(2,1)}, bf16[128,128]{1,0:T(8,128)(2,1)S(1)}, u32[]{:S(2)}) copy-start(bf16[128,128]{1,0:T(8,128)(2,1)S(1)} %shard_map.60.prior_ref.refs_2_) | copy-start | bytes 98308
  110.8 0.6 copy-start.3
  111.4 17.8 %all-to-all-start.4 = ((bf16[64,2,128]{2,1,0:T(2,128)(2,1)}), bf16[64,2,128]{2,1,0:T(2,128)(2,1)S(1)}, u32[]{:S(2)}, u32[]{:S(2)}) async-start(bf16[64,2,128]{2,1,0:T(2,128)(2,1)} %bitcast.10), calls=%async_computation.4 | async-start | bytes 65536 | tf_op jit(solution)/shard_map/all_to_all | solution.py:310
  120.0 24.7 %collective-permute-start.11 = (bf16[6144,128]{1,0:T(8,128)(2,1)}, bf16[6144,128]{1,0:T(8,128)(2,1)}, u32[]{:S(2)}, u32[]{:S(2)}) collective-permute-start(bf16[6144,128]{1,0:T(8,128)(2,1)} %get-tuple-element.46.near_any), channel_id=1, source_target_pairs={{0,1},{1,0},{2,3},{3,2},{4,5},{5,4},{6,7},{7,6},{8,9},{9,8},{10,11... | collective-permute-start | bytes 4718600 | tf_op jit(solution)/shard_map/ppermute | solution.py:37
  122.3 13.1 %collective-permute-start.10 = (bf16[6144,128]{1,0:T(8,128)(2,1)S(1)}, bf16[6144,128]{1,0:T(8,128)(2,1)}, u32[]{:S(2)}, u32[]{:S(2)}) collective-permute-start(bf16[6144,128]{1,0:T(8,128)(2,1)S(1)} %get-tuple-element.41.refs_3_), channel_id=1, source_target_pairs={{0,1},{1,0},{2,3},{3,2},{4,5},{5,4},{6,7},{7,6},{8,9},{9,8},{10,11... | collective-permute-start | bytes 4718600 | tf_op jit(solution)/shard_map/ppermute | solution.py:37
  130.0 14.7 %all-to-all-start.5 = ((bf16[64,2,128]{2,1,0:T(2,128)(2,1)}), bf16[64,2,128]{2,1,0:T(2,128)(2,1)S(1)}, u32[]{:S(2)}, u32[]{:S(2)}) async-start(bf16[64,2,128]{2,1,0:T(2,128)(2,1)} %bitcast.12), calls=%async_computation.5 | async-start | bytes 65536 | tf_op jit(solution)/shard_map/all_to_all | solution.py:310

commit v8 on v7

--- a/solution.py
+++ b/solution.py
@@ -14,7 +14,7 @@
 BF16 = jnp.bfloat16
 F32 = jnp.float32
 LIMIT = 16 * 1024 * 1024
-LONG = 30_000_000_000
+LONG = 80_000_000_000
 ANY = pl.BlockSpec(memory_space=pl.ANY)
 VMEM = pl.BlockSpec(memory_space=pltpu.VMEM)
 
@@ -41,10 +41,11 @@
     return [pltpu.with_memory_space_constraint(v, pltpu.HBM) for v in values]
 
 
-def project_kernel(shifts, *refs):
-    tokens, blocks, outs, scratch = refs[:-11], refs[-11:-7], refs[-7:-4], refs[-4:]
-    weight_ref, own_ref, send_ref = outs
-    own_held, far_held, own_sem, far_sem = scratch
+def project_kernel(shifts, slot, *refs):
+    given, outs, scratch = refs[:-9], refs[-9:-6], refs[-6:]
+    tokens, blocks = given[: 2 + 2 * slot], given[2 + 2 * slot : 6 + 2 * slot]
+    weights_any, own_ref, send_ref = outs
+    own_held, far_held, weight_ref, own_sem, far_sem, weight_sem = scratch
     rows = weight_ref.shape[0] // 32
     x, core = lax.axis_index("x"), lax.axis_index("core")
 
@@ -58,10 +59,13 @@
             for p in range(8):
                 at = pl.multiple_of((p * 4 + source) * rows, 64)
                 weight_ref[pl.ds(at, rows), :] = ref[p * rows : (p + 1) * rows, :]
+        weight_copy = pltpu.make_async_copy(weight_ref, weights_any.at[slot], weight_sem)
+        weight_copy.start()
         own_copy.wait()
         own_ref[...] = contract(own_held[...], weight_ref[...], 1, 0).astype(own_ref.dtype)
         far_copy.wait()
         send_ref[...] = contract(far_held[...], weight_ref[...], 1, 0).astype(send_ref.dtype)
+        weight_copy.wait()
 
     if len(tokens) == 2:
         products(*tokens)
@@ -70,18 +74,25 @@
         pl.when(core != 0)(lambda: products(*tokens[2:]))
 
 
-def project(tokens, blocks, dtype):
+def project(tokens, blocks, dtype, *held):
     count, depth = tokens[0].shape
+    slot = len(held)
     row = jax.ShapeDtypeStruct((count, 128), dtype)
     return pl.pallas_call(
-        functools.partial(project_kernel, tuple(blocks)),
-        out_shape=[jax.ShapeDtypeStruct((depth, 128), BF16), row, row],
-        in_specs=[ANY] * len(tokens) + [VMEM] * 4,
-        out_specs=[VMEM] * 3,
-        scratch_shapes=[pltpu.VMEM((count, depth), BF16)] * 2 + [pltpu.SemaphoreType.DMA] * 2,
+        functools.partial(project_kernel, tuple(blocks), slot),
+        out_shape=[pltpu.HBM((2, depth, 128), BF16), row, row],
+        in_specs=[ANY] * len(tokens) + [VMEM] * 4 + [ANY] * slot,
+        out_specs=[ANY, VMEM, VMEM],
+        input_output_aliases={len(tokens) + 4: 0} if held else {},
+        scratch_shapes=[
+            pltpu.VMEM((count, depth), BF16),
+            pltpu.VMEM((count, depth), BF16),
+            pltpu.VMEM((depth, 128), BF16),
+            *[pltpu.SemaphoreType.DMA] * 3,
+        ],
         compiler_params=pltpu.CompilerParams(vmem_limit_bytes=LIMIT),
         cost_estimate=cost(LONG, 4 * count * depth + 4 * depth * 128),
-    )(*in_hbm(*tokens), *blocks.values())
+    )(*in_hbm(*tokens), *blocks.values(), *in_hbm(*held))
 
 
 def state_kernel(own_ref, recv_ref, kv_ref, state_ref):
@@ -120,6 +131,21 @@
         compiler_params=pltpu.CompilerParams(vmem_limit_bytes=LIMIT),
         cost_estimate=cost(LONG, 4 * value.size),
     )(value)
+
+
+def copies_kernel(in_ref, out_ref):
+    out_ref[...] = jnp.broadcast_to(in_ref[...][None], out_ref.shape)
+
+
+def gated_copies(block, peers):
+    return pl.pallas_call(
+        copies_kernel,
+        out_shape=jax.ShapeDtypeStruct((peers, *block.shape), block.dtype),
+        in_specs=[VMEM],
+        out_specs=VMEM,
+        compiler_params=pltpu.CompilerParams(vmem_limit_bytes=LIMIT),
+        cost_estimate=cost(LONG, 2 * peers * block.size),
+    )(block)
 
 
 def causal_of(count):
@@ -168,7 +194,7 @@
     qa_ref, kv_ref, prior_ref, weight_ref, row_sems, weight_sem = scratch
 
     def body(weight_any):
-        weight_copy = pltpu.make_async_copy(weight_any, weight_ref, weight_sem)
+        weight_copy = pltpu.make_async_copy(weight_any.at[1], weight_ref, weight_sem)
         copies = [
             pltpu.make_async_copy(source, target, row_sems.at[i])
             for i, (source, target) in enumerate(zip(rows_any, scratch[:3]))
@@ -199,7 +225,7 @@
 
 
 def inner_grads(qa, kv, prior, near, far):
-    count, depth = kv.shape[0], near.shape[0]
+    count, depth = kv.shape[0], near.shape[1]
     rows = pltpu.VMEM((count, 256), BF16)
     return pl.pallas_call(
         inner_kernel,
@@ -234,7 +260,7 @@
         at = pl.ds(i * part, part)
         for n, (source, target) in enumerate(((near_any, near_ref), (far_any, far_ref))):
             weights.append(
-                pltpu.make_async_copy(source.at[at], target.at[at], weight_sems.at[2 * i + n])
+                pltpu.make_async_copy(source.at[0, at], target.at[at], weight_sems.at[2 * i + n])
             )
     for copy in rows + weights:
         copy.start()
@@ -336,25 +362,24 @@
     tokens_far = core_swap(after(tokens, kv_copies))
     grads_far = core_swap(after(grads_in, kv_copies))
     kv_plane = over_planes(kv_copies)
-    qo_plane = over_planes(copied(gate(after(qo_rows, kv_plane))))
+    qo_plane = over_planes(gated_copies(after(qo_rows, kv_plane), dps * zs))
     tokens_far = after(tokens_far, grads_far)
-    kv_near, own, send = project((tokens, tokens_far), over_x(kv_plane), BF16)
+    weights, own, send = project((tokens, tokens_far), over_x(kv_plane), BF16)
     own, qo_plane = lax.optimization_barrier((own, qo_plane))
     kv, local_state = keys_values_state(own, core_swap(send))
 
     qo = over_x(after(qo_plane, local_state))
     prior_state = gate(exchange(sums_of(exchange(local_state), False)))
-    qo_near, own, send = project(
-        (tokens, tokens_far, grads_in, grads_far), qo, F32
+    weights, own, send = project(
+        (tokens, tokens_far, grads_in, grads_far), qo, F32, weights
     )
     recv = after(core_swap(send), prior_state)
     qa, local_grad = attention_grad(own, recv, kv, prior_state, norm_gain.reshape(1, head))
-    kv_far = core_swap(kv_near)
     grad_pieces = exchange(local_grad)
-    qo_far = core_swap(qo_near)
-    base, *grads = inner_grads(qa, kv, prior_state, qo_near, qo_far)
+    weights_far = core_swap(weights)
+    base, *grads = inner_grads(qa, kv, prior_state, weights, weights_far)
     later_state = exchange(sums_of(grad_pieces, True))
-    result = output(base, *grads, kv, later_state, kv_near, kv_far)
+    result = output(base, *grads, kv, later_state, weights, weights_far)
     return result[None]
 
 

time: 150 us -> 150 us (level)
  starting transfers between devices: 88 us -> 85.9 us
    ppermute x6 -> x5, starting transfers between devices: 16 us -> 14.1 us  [core_swap(): return lax.ppermute(block, 'core', [(0, 1), (1, 0)])]
    unnamed x13, local copies, waits for them, and re-layouts: 1.99 us -> 3.68 us
    pallas_call x2 -> x3, Pallas kernels: 5.99 us -> 7.39 us  [the longest x2 6.59 us: project(): pl.pallas_call(functools.partial(project_kernel, tuple(blocks), slot), ou...]
  transfers between devices with their start and end apart: 18 -> 17, of which waited for: 9 -> 9; matrix products, arithmetic and copies ran while one was open for 1% -> 0% of each run, Pallas kernels for 7% -> 7%
where the time goes in v8:
time: 150 us; the launch traced here: 149 us
  starting transfers between devices  85.9 us (57%)
  waiting for transfers between devices  31.8 us (21%)
  Pallas kernels  17.4 us (12%)
  blocking collectives  8.36 us (6%)
  local copies, waits for them, and re-layouts  4.48 us (3%)
    all_to_all x4, starting transfers between devices, exchange(): return lax.all_to_all(pieces, SEQ, 0, 0, tiled=True).reshape(state.shape)  34.3 us
    ppermute x6, starting transfers between devices, over_x(): lax.ppermute(block, 'x', [(i, (i + k) % xs) for i in range(xs)])  20.1 us
    all_to_all x2, starting transfers between devices, over_planes(): return lax.all_to_all(copies, ROWS, 0, 0, tiled=True).reshape(-1, head)  17.4 us
    ppermute x5, starting transfers between devices, core_swap(): return lax.ppermute(block, 'core', [(0, 1), (1, 0)])  14.1 us
    all_to_all x4, waiting for transfers between devices, exchange(): return lax.all_to_all(pieces, SEQ, 0, 0, tiled=True).reshape(state.shape)  13.6 us
    all_to_all x2, waiting for transfers between devices, over_planes(): return lax.all_to_all(copies, ROWS, 0, 0, tiled=True).reshape(-1, head)  12.1 us
    all_gather x1, blocking collectives, per_device(): rows = lax.all_gather(rows, 'core', axis=0, tiled=True)  8.36 us
    pallas_call x2, Pallas kernels, project(): pl.pallas_call(functools.partial(project_kernel, tuple(blocks), slot), ou...  6.59 us
  transfers between devices with their start and end apart: 17, of which 9 were waited for; matrix products, arithmetic and copies ran while one was open for 0% of the time, Pallas kernels for 7%

profile of v8, /device:TPU:1, one launch (start us, length us, event | category | flops | bytes accessed | tf_op | source)
XLA Modules:
  0.0 149.1 jit_solution(12993807129024999691)
XLA Ops:
  1.4 8.4 %all-gather = bf16[2,12,512]{2,1,0:T(8,128)(2,1)S(1)} all-gather(bf16[1,12,512]{2,1,0:T(8,128)(2,1)S(1)} %maximum_bitcast_fusion), channel_id=1, replica_groups=mesh['dp'=8,'x'=4,'z'=8,'core'=2] {'core'}, dimensions={0}, use_global_device_ids=true | all-gather | bytes 36864 | tf_op jit(solution)/shard_map/all_gather | solution.py:347
  10.6 10.9 %all-to-all-start = ((bf16[64,24,128]{2,1,0:T(8,128)(2,1)}), bf16[64,24,128]{2,1,0:T(8,128)(2,1)S(1)}, u32[]{:S(2)}, u32[]{:S(2)}) async-start(bf16[64,24,128]{2,1,0:T(8,128)(2,1)} %broadcast_in_dim.4), calls=%async_computation | async-start | bytes 786432 | tf_op jit(solution)/shard_map/all_to_all | solution.py:355
  21.6 2.5 %collective-permute-start = (bf16[136,6144]{1,0:T(8,128)(2,1)}, bf16[136,6144]{1,0:T(8,128)(2,1)}, u32[]{:S(2)}, u32[]{:S(2)}) collective-permute-start(bf16[136,6144]{1,0:T(8,128)(2,1)} %bitcast.34), channel_id=1, source_target_pairs={{0,1},{1,0},{2,3},{3,2},{4,5},{5,4},{6,7},{7,6},{8,9},{9,8},{10,11... | collective-permute-start | bytes 5013512 | tf_op jit(solution)/shard_map/ppermute | solution.py:37
  26.0 10.5 %all-to-all-done = bf16[64,24,128]{2,1,0:T(8,128)(2,1)S(1)} async-done(((bf16[64,24,128]{2,1,0:T(8,128)(2,1)}), bf16[64,24,128]{2,1,0:T(8,128)(2,1)S(1)}, u32[]{:S(2)}, u32[]{:S(2)}) %all-to-all-start) | async-done | bytes 393248 | tf_op jit(solution)/shard_map/all_to_all | solution.py:355
  36.6 4.6 %collective-permute-start.4 = (bf16[1536,128]{1,0:T(8,128)(2,1)S(1)}, bf16[1536,128]{1,0:T(8,128)(2,1)S(1)}, u32[]{:S(2)}, u32[]{:S(2)}) collective-permute-start(bf16[1536,128]{1,0:T(8,128)(2,1)S(1)} %bitcast.23), channel_id=1, source_target_pairs={{0,32},{16,48},{32,0},{48,16},{1,33},{17,49},{33,1},{49,17},{2,34}... | collective-permute-start | bytes 1179656 | tf_op jit(solution)/shard_map/ppermute | solution.py:358
  41.2 2.8 %collective-permute-start.3 = (bf16[1536,128]{1,0:T(8,128)(2,1)S(1)}, bf16[1536,128]{1,0:T(8,128)(2,1)S(1)}, u32[]{:S(2)}, u32[]{:S(2)}) collective-permute-start(bf16[1536,128]{1,0:T(8,128)(2,1)S(1)} %bitcast.24), channel_id=1, source_target_pairs={{0,48},{16,0},{32,16},{48,32},{1,49},{17,1},{33,17},{49,33},{2,50}... | collective-permute-start | bytes 1179656 | tf_op jit(solution)/shard_map/ppermute | solution.py:358
  44.0 2.5 %collective-permute-start.2 = (bf16[1536,128]{1,0:T(8,128)(2,1)S(1)}, bf16[1536,128]{1,0:T(8,128)(2,1)S(1)}, u32[]{:S(2)}, u32[]{:S(2)}) collective-permute-start(bf16[1536,128]{1,0:T(8,128)(2,1)S(1)} %bitcast.25), channel_id=1, source_target_pairs={{0,16},{16,32},{32,48},{48,0},{1,17},{17,33},{33,49},{49,1},{2,18}... | collective-permute-start | bytes 1179656 | tf_op jit(solution)/shard_map/ppermute | solution.py:358
  47.3 6.5 %all-to-all-start.1 = ((bf16[64,24,128]{2,1,0:T(8,128)(2,1)}), bf16[64,24,128]{2,1,0:T(8,128)(2,1)S(1)}, u32[]{:S(2)}, u32[]{:S(2)}) async-start(bf16[64,24,128]{2,1,0:T(8,128)(2,1)} %shard_map.56), calls=%async_computation.1 | async-start | bytes 786432 | tf_op jit(solution)/shard_map/all_to_all | solution.py:355
  53.8 4.1 %collective-permute-done.3.refs_3_ = bf16[1536,128]{1,0:T(8,128)(2,1)S(1)} collective-permute-done((bf16[1536,128]{1,0:T(8,128)(2,1)S(1)}, bf16[1536,128]{1,0:T(8,128)(2,1)S(1)}, u32[]{:S(2)}, u32[]{:S(2)}) %collective-permute-start.3) | collective-permute-done | bytes 393248 | tf_op jit(solution)/shard_map/ppermute | solution.py:358
  58.2 3.3 %shard_map.55 = (bf16[2,6144,128]{2,1,0:T(8,128)(2,1)}, bf16[136,128]{1,0:T(8,128)(2,1)S(1)}, bf16[136,128]{1,0:T(8,128)(2,1)S(1)}) custom-call(bf16[136,6144]{1,0:T(8,128)(2,1)} %bitcast.35, bf16[136,6144]{1,0:T(8,128)(2,1)} %collective-permute-done.refs_1_, bf16[1536,128]{1,0:T(8,128)(2,1)S(1)} %collective-permute-done.2.refs_2_, ...), custom_call_target="tpu_custom_call" | custom-call | flops 80000000000 | bytes 6488064 | tf_op jit(solution)/shard_map/pallas_call | solution.py:81
  61.5 4.2 %collective-permute-start.5 = (bf16[136,128]{1,0:T(8,128)(2,1)S(1)}, bf16[136,128]{1,0:T(8,128)(2,1)S(1)}, u32[]{:S(2)}, u32[]{:S(2)}) collective-permute-start(bf16[136,128]{1,0:T(8,128)(2,1)S(1)} %get-tuple-element.33), channel_id=1, source_target_pairs={{0,1},{1,0},{2,3},{3,2},{4,5},{5,4},{6,7},{7,6},{8,9},{9,8},{10,11... | collective-permute-start | bytes 104456 | tf_op jit(solution)/shard_map/ppermute | solution.py:37
  68.2 10.4 %all-to-all-start.2 = ((bf16[64,2,128]{2,1,0:T(2,128)(2,1)}), bf16[64,2,128]{2,1,0:T(2,128)(2,1)S(1)}, u32[]{:S(2)}, u32[]{:S(2)}) async-start(bf16[64,2,128]{2,1,0:T(2,128)(2,1)} %bitcast.5), calls=%async_computation.2 | async-start | bytes 65536 | tf_op jit(solution)/shard_map/all_to_all | solution.py:336
  78.6 4.9 %collective-permute-start.8 = (bf16[1536,128]{1,0:T(8,128)(2,1)S(1)}, bf16[1536,128]{1,0:T(8,128)(2,1)S(1)}, u32[]{:S(2)}, u32[]{:S(2)}) collective-permute-start(bf16[1536,128]{1,0:T(8,128)(2,1)S(1)} %bitcast.19), channel_id=1, source_target_pairs={{0,32},{16,48},{32,0},{48,16},{1,33},{17,49},{33,1},{49,17},{2,34}... | collective-permute-start | bytes 1179656 | tf_op jit(solution)/shard_map/ppermute | solution.py:358
  83.5 2.7 %collective-permute-start.7 = (bf16[1536,128]{1,0:T(8,128)(2,1)S(1)}, bf16[1536,128]{1,0:T(8,128)(2,1)S(1)}, u32[]{:S(2)}, u32[]{:S(2)}) collective-permute-start(bf16[1536,128]{1,0:T(8,128)(2,1)S(1)} %bitcast.20), channel_id=1, source_target_pairs={{0,48},{16,0},{32,16},{48,32},{1,49},{17,1},{33,17},{49,33},{2,50}... | collective-permute-start | bytes 1179656 | tf_op jit(solution)/shard_map/ppermute | solution.py:358
  86.2 2.6 %collective-permute-start.6 = (bf16[1536,128]{1,0:T(8,128)(2,1)S(1)}, bf16[1536,128]{1,0:T(8,128)(2,1)S(1)}, u32[]{:S(2)}, u32[]{:S(2)}) collective-permute-start(bf16[1536,128]{1,0:T(8,128)(2,1)S(1)} %bitcast.21), channel_id=1, source_target_pairs={{0,16},{16,32},{32,48},{48,0},{1,17},{17,33},{33,49},{49,1},{2,18}... | collective-permute-start | bytes 1179656 | tf_op jit(solution)/shard_map/ppermute | solution.py:358
  89.6 10.2 %all-to-all-start.3 = ((bf16[64,2,128]{2,1,0:T(2,128)(2,1)}), bf16[64,2,128]{2,1,0:T(2,128)(2,1)S(1)}, u32[]{:S(2)}, u32[]{:S(2)}) async-start(bf16[64,2,128]{2,1,0:T(2,128)(2,1)} %bitcast.7), calls=%async_computation.3 | async-start | bytes 65536 | tf_op jit(solution)/shard_map/all_to_all | solution.py:336
  101.4 3.3 %shard_map.58 = (bf16[2,6144,128]{2,1,0:T(8,128)(2,1)}, f32[136,128]{1,0:T(8,128)S(1)}, f32[136,128]{1,0:T(8,128)S(1)}) custom-call(bf16[136,6144]{1,0:T(8,128)(2,1)} %bitcast.36, bf16[136,6144]{1,0:T(8,128)(2,1)} %collective-permute-done.refs_1_, bf16[136,6144]{1,0:T(8,128)(2,1)} %bitcast.38, ...), custom_call_target="tpu_custom_call", output_to_operand_aliasing={{0}: (8, {})} | custom-call | flops 80000000000 | bytes 6488064 | tf_op jit(solution)/shard_map/pallas_call | solution.py:81
  104.7 3.0 %collective-permute-start.9 = (f32[136,128]{1,0:T(8,128)S(1)}, f32[136,128]{1,0:T(8,128)S(1)}, u32[]{:S(2)}, u32[]{:S(2)}) collective-permute-start(f32[136,128]{1,0:T(8,128)S(1)} %get-tuple-element.38), channel_id=1, source_target_pairs={{0,1},{1,0},{2,3},{3,2},{4,5},{5,4},{6,7},{7,6},{8,9},{9,8},{10,11... | collective-permute-start | bytes 208904 | tf_op jit(solution)/shard_map/ppermute | solution.py:37
  111.4 9.1 %all-to-all-start.4 = ((bf16[64,2,128]{2,1,0:T(2,128)(2,1)}), bf16[64,2,128]{2,1,0:T(2,128)(2,1)S(1)}, u32[]{:S(2)}, u32[]{:S(2)}) async-start(bf16[64,2,128]{2,1,0:T(2,128)(2,1)} %bitcast.10), calls=%async_computation.4 | async-start | bytes 65536 | tf_op jit(solution)/shard_map/all_to_all | solution.py:336
  120.5 2.4 %collective-permute-start.10 = (bf16[2,6144,128]{2,1,0:T(8,128)(2,1)}, bf16[2,6144,128]{2,1,0:T(8,128)(2,1)S(1)}, u32[]{:S(2)}, u32[]{:S(2)}) collective-permute-start(bf16[2,6144,128]{2,1,0:T(8,128)(2,1)} %get-tuple-element.42.refs_3_.near_any), channel_id=1, source_target_pairs={{0,1},{1,0},{2,3},{3,2},{4,5},{5,4},{6,7},{7,6},{8,9},{9,8},{10,11... | collective-permute-start | bytes 9437192 | tf_op jit(solution)/shard_map/ppermute | solution.py:37
  122.9 6.9 %all-to-all-done.4 = bf16[64,2,128]{2,1,0:T(2,128)(2,1)S(1)} async-done(((bf16[64,2,128]{2,1,0:T(2,128)(2,1)}), bf16[64,2,128]{2,1,0:T(2,128)(2,1)S(1)}, u32[]{:S(2)}, u32[]{:S(2)}) %all-to-all-start.4) | async-done | bytes 32800 | tf_op jit(solution)/shard_map/all_to_all | solution.py:336
  130.6 4.6 %all-to-all-start.5 = ((bf16[64,2,128]{2,1,0:T(2,128)(2,1)}), bf16[64,2,128]{2,1,0:T(2,128)(2,1)S(1)}, u32[]{:S(2)}, u32[]{:S(2)}) async-start(bf16[64,2,128]{2,1,0:T(2,128)(2,1)} %bitcast.12), calls=%async_computation.5 | async-start | bytes 65536 | tf_op jit(solution)/shard_map/all_to_all | solution.py:336
  139.1 5.5 %all-to-all-done.5 = bf16[64,2,128]{2,1,0:T(2,128)(2,1)S(1)} async-done(((bf16[64,2,128]{2,1,0:T(2,128)(2,1)}), bf16[64,2,128]{2,1,0:T(2,128)(2,1)S(1)}, u32[]{:S(2)}, u32[]{:S(2)}) %all-to-all-start.5) | async-done | bytes 32800 | tf_op jit(solution)/shard_map/all_to_all | solution.py:336
  144.6 4.4 %shard_map.64 = bf16[136,6144]{1,0:T(8,128)(2,1)} custom-call(f32[136,6144]{1,0:T(8,128)S(1)} %get-tuple-element.43.base, f32[136,128]{1,0:T(8,128)S(1)} %get-tuple-element.44.dk, f32[136,128]{1,0:T(8,128)S(1)} %get-tuple-element.45.dv, bf16[136,256]{1,0:T(8,128)(2,1)} %copy-done, bf16[128,128]{1,0:T(8,128)(2,1)S(1)} %bitcast.27, ...), custom_call_target="tpu_custom_call" | custom-call | flops 427819008 | bytes 8159232 | tf_op jit(solution)/shard_map/pallas_call | solution.py:294
  (37 shorter events, 18.3 us)
Async XLA Ops:
  10.6 25.9 %all-to-all-start = ((bf16[64,24,128]{2,1,0:T(8,128)(2,1)}), bf16[64,24,128]{2,1,0:T(8,128)(2,1)S(1)}, u32[]{:S(2)}, u32[]{:S(2)}) async-start(bf16[64,24,128]{2,1,0:T(8,128)(2,1)} %broadcast_in_dim.4), calls=%async_computation | async-start | bytes 786432 | tf_op jit(solution)/shard_map/all_to_all | solution.py:355
  21.6 32.3 %collective-permute-start = (bf16[136,6144]{1,0:T(8,128)(2,1)}, bf16[136,6144]{1,0:T(8,128)(2,1)}, u32[]{:S(2)}, u32[]{:S(2)}) collective-permute-start(bf16[136,6144]{1,0:T(8,128)(2,1)} %bitcast.34), channel_id=1, source_target_pairs={{0,1},{1,0},{2,3},{3,2},{4,5},{5,4},{6,7},{7,6},{8,9},{9,8},{10,11... | collective-permute-start | bytes 5013512 | tf_op jit(solution)/shard_map/ppermute | solution.py:37
  24.1 29.7 %collective-permute-start.1 = (bf16[136,6144]{1,0:T(8,128)(2,1)}, bf16[136,6144]{1,0:T(8,128)(2,1)}, u32[]{:S(2)}, u32[]{:S(2)}) collective-permute-start(bf16[136,6144]{1,0:T(8,128)(2,1)} %bitcast.37), channel_id=1, source_target_pairs={{0,1},{1,0},{2,3},{3,2},{4,5},{5,4},{6,7},{7,6},{8,9},{9,8},{10,11... | collective-permute-start | bytes 5013512 | tf_op jit(solution)/shard_map/ppermute | solution.py:37
  36.6 17.3 %collective-permute-start.4 = (bf16[1536,128]{1,0:T(8,128)(2,1)S(1)}, bf16[1536,128]{1,0:T(8,128)(2,1)S(1)}, u32[]{:S(2)}, u32[]{:S(2)}) collective-permute-start(bf16[1536,128]{1,0:T(8,128)(2,1)S(1)} %bitcast.23), channel_id=1, source_target_pairs={{0,32},{16,48},{32,0},{48,16},{1,33},{17,49},{33,1},{49,17},{2,34}... | collective-permute-start | bytes 1179656 | tf_op jit(solution)/shard_map/ppermute | solution.py:358
  41.2 16.7 %collective-permute-start.3 = (bf16[1536,128]{1,0:T(8,128)(2,1)S(1)}, bf16[1536,128]{1,0:T(8,128)(2,1)S(1)}, u32[]{:S(2)}, u32[]{:S(2)}) collective-permute-start(bf16[1536,128]{1,0:T(8,128)(2,1)S(1)} %bitcast.24), channel_id=1, source_target_pairs={{0,48},{16,0},{32,16},{48,32},{1,49},{17,1},{33,17},{49,33},{2,50}... | collective-permute-start | bytes 1179656 | tf_op jit(solution)/shard_map/ppermute | solution.py:358
  44.0 14.3 %collective-permute-start.2 = (bf16[1536,128]{1,0:T(8,128)(2,1)S(1)}, bf16[1536,128]{1,0:T(8,128)(2,1)S(1)}, u32[]{:S(2)}, u32[]{:S(2)}) collective-permute-start(bf16[1536,128]{1,0:T(8,128)(2,1)S(1)} %bitcast.25), channel_id=1, source_target_pairs={{0,16},{16,32},{32,48},{48,0},{1,17},{17,33},{33,49},{49,1},{2,18}... | collective-permute-start | bytes 1179656 | tf_op jit(solution)/shard_map/ppermute | solution.py:358
  47.3 20.1 %all-to-all-start.1 = ((bf16[64,24,128]{2,1,0:T(8,128)(2,1)}), bf16[64,24,128]{2,1,0:T(8,128)(2,1)S(1)}, u32[]{:S(2)}, u32[]{:S(2)}) async-start(bf16[64,24,128]{2,1,0:T(8,128)(2,1)} %shard_map.56), calls=%async_computation.1 | async-start | bytes 786432 | tf_op jit(solution)/shard_map/all_to_all | solution.py:355
  61.5 5.9 %collective-permute-start.5 = (bf16[136,128]{1,0:T(8,128)(2,1)S(1)}, bf16[136,128]{1,0:T(8,128)(2,1)S(1)}, u32[]{:S(2)}, u32[]{:S(2)}) collective-permute-start(bf16[136,128]{1,0:T(8,128)(2,1)S(1)} %get-tuple-element.33), channel_id=1, source_target_pairs={{0,1},{1,0},{2,3},{3,2},{4,5},{5,4},{6,7},{7,6},{8,9},{9,8},{10,11... | collective-permute-start | bytes 104456 | tf_op jit(solution)/shard_map/ppermute | solution.py:37
  68.2 40.7 %copy-start = (bf16[136,256]{1,0:T(8,128)(2,1)}, bf16[136,256]{1,0:T(8,128)(2,1)S(1)}, u32[]{:S(2)}) copy-start(bf16[136,256]{1,0:T(8,128)(2,1)S(1)} %get-tuple-element.40.kv_ref.refs_1_.kv_any) | copy-start | bytes 208900
  68.2 20.6 %all-to-all-start.2 = ((bf16[64,2,128]{2,1,0:T(2,128)(2,1)}), bf16[64,2,128]{2,1,0:T(2,128)(2,1)S(1)}, u32[]{:S(2)}, u32[]{:S(2)}) async-start(bf16[64,2,128]{2,1,0:T(2,128)(2,1)} %bitcast.5), calls=%async_computation.2 | async-start | bytes 65536 | tf_op jit(solution)/shard_map/all_to_all | solution.py:336
  78.6 21.1 %collective-permute-start.8 = (bf16[1536,128]{1,0:T(8,128)(2,1)S(1)}, bf16[1536,128]{1,0:T(8,128)(2,1)S(1)}, u32[]{:S(2)}, u32[]{:S(2)}) collective-permute-start(bf16[1536,128]{1,0:T(8,128)(2,1)S(1)} %bitcast.19), channel_id=1, source_target_pairs={{0,32},{16,48},{32,0},{48,16},{1,33},{17,49},{33,1},{49,17},{2,34}... | collective-permute-start | bytes 1179656 | tf_op jit(solution)/shard_map/ppermute | solution.py:358
  83.5 17.8 %collective-permute-start.7 = (bf16[1536,128]{1,0:T(8,128)(2,1)S(1)}, bf16[1536,128]{1,0:T(8,128)(2,1)S(1)}, u32[]{:S(2)}, u32[]{:S(2)}) collective-permute-start(bf16[1536,128]{1,0:T(8,128)(2,1)S(1)} %bitcast.20), channel_id=1, source_target_pairs={{0,48},{16,0},{32,16},{48,32},{1,49},{17,1},{33,17},{49,33},{2,50}... | collective-permute-start | bytes 1179656 | tf_op jit(solution)/shard_map/ppermute | solution.py:358
  86.2 15.2 %collective-permute-start.6 = (bf16[1536,128]{1,0:T(8,128)(2,1)S(1)}, bf16[1536,128]{1,0:T(8,128)(2,1)S(1)}, u32[]{:S(2)}, u32[]{:S(2)}) collective-permute-start(bf16[1536,128]{1,0:T(8,128)(2,1)S(1)} %bitcast.21), channel_id=1, source_target_pairs={{0,16},{16,32},{32,48},{48,0},{1,17},{17,33},{33,49},{49,1},{2,18}... | collective-permute-start | bytes 1179656 | tf_op jit(solution)/shard_map/ppermute | solution.py:358
  89.6 19.4 %all-to-all-start.3 = ((bf16[64,2,128]{2,1,0:T(2,128)(2,1)}), bf16[64,2,128]{2,1,0:T(2,128)(2,1)S(1)}, u32[]{:S(2)}, u32[]{:S(2)}) async-start(bf16[64,2,128]{2,1,0:T(2,128)(2,1)} %bitcast.7), calls=%async_computation.3 | async-start | bytes 65536 | tf_op jit(solution)/shard_map/all_to_all | solution.py:336
  104.7 4.2 %collective-permute-start.9 = (f32[136,128]{1,0:T(8,128)S(1)}, f32[136,128]{1,0:T(8,128)S(1)}, u32[]{:S(2)}, u32[]{:S(2)}) collective-permute-start(f32[136,128]{1,0:T(8,128)S(1)} %get-tuple-element.38), channel_id=1, source_target_pairs={{0,1},{1,0},{2,3},{3,2},{4,5},{5,4},{6,7},{7,6},{8,9},{9,8},{10,11... | collective-permute-start | bytes 208904 | tf_op jit(solution)/shard_map/ppermute | solution.py:37
  108.9 0.7 copy-start.1
  109.0 1.8 %copy-start.3 = (bf16[128,128]{1,0:T(8,128)(2,1)}, bf16[128,128]{1,0:T(8,128)(2,1)S(1)}, u32[]{:S(2)}) copy-start(bf16[128,128]{1,0:T(8,128)(2,1)S(1)} %shard_map.60.prior_ref.refs_2_) | copy-start | bytes 98308
  110.8 0.6 copy-start.2
  111.4 18.4 %all-to-all-start.4 = ((bf16[64,2,128]{2,1,0:T(2,128)(2,1)}), bf16[64,2,128]{2,1,0:T(2,128)(2,1)S(1)}, u32[]{:S(2)}, u32[]{:S(2)}) async-start(bf16[64,2,128]{2,1,0:T(2,128)(2,1)} %bitcast.10), calls=%async_computation.4 | async-start | bytes 65536 | tf_op jit(solution)/shard_map/all_to_all | solution.py:336
  120.5 14.7 %collective-permute-start.10 = (bf16[2,6144,128]{2,1,0:T(8,128)(2,1)}, bf16[2,6144,128]{2,1,0:T(8,128)(2,1)S(1)}, u32[]{:S(2)}, u32[]{:S(2)}) collective-permute-start(bf16[2,6144,128]{2,1,0:T(8,128)(2,1)} %get-tuple-element.42.refs_3_.near_any), channel_id=1, source_target_pairs={{0,1},{1,0},{2,3},{3,2},{4,5},{5,4},{6,7},{7,6},{8,9},{9,8},{10,11... | collective-permute-start | bytes 9437192 | tf_op jit(solution)/shard_map/ppermute | solution.py:37
  130.6 14.0 %all-to-all-start.5 = ((bf16[64,2,128]{2,1,0:T(2,128)(2,1)}), bf16[64,2,128]{2,1,0:T(2,128)(2,1)S(1)}, u32[]{:S(2)}, u32[]{:S(2)}) async-start(bf16[64,2,128]{2,1,0:T(2,128)(2,1)} %bitcast.12), calls=%async_computation.5 | async-start | bytes 65536 | tf_op jit(solution)/shard_map/all_to_all | solution.py:336
  135.2 1.7 %copy-start.4 = (bf16[2,6144,128]{2,1,0:T(8,128)(2,1)}, bf16[2,6144,128]{2,1,0:T(8,128)(2,1)S(1)}, u32[]{:S(2)}) copy-start(bf16[2,6144,128]{2,1,0:T(8,128)(2,1)S(1)} %collective-permute-done.10.refs_4_.far_any) | copy-start | bytes 9437188

commit v9 on v8

--- a/solution.py
+++ b/solution.py
@@ -154,7 +154,7 @@
 
 
 def grad_kernel(
-    near_ref, far_ref, kv_ref, prior_ref, gain_ref, qa_ref, state_ref
+    near_ref, far_ref, kv_ref, prior_ref, gain_ref, qa_any, state_ref, qa_ref, qa_sem
 ):
     first = lax.axis_index("core") == 0
     near, far = near_ref[...], far_ref[...]
@@ -170,7 +170,10 @@
     attn_grad = inv_rms * scaled - attended * (inv_rms * inv_rms * inv_rms) * mean
     attn_grad = attn_grad.astype(BF16)
     qa_ref[:, 128:] = attn_grad
+    copy = pltpu.make_async_copy(qa_ref, qa_any, qa_sem)
+    copy.start()
     state_ref[...] = contract(queries, attn_grad, 0, 0).astype(BF16)
+    copy.wait()
 
 
 def attention_grad(near, far, kv, prior, gain):
@@ -178,11 +181,12 @@
     return pl.pallas_call(
         grad_kernel,
         out_shape=[
-            jax.ShapeDtypeStruct((count, 256), BF16),
+            pltpu.HBM((count, 256), BF16),
             jax.ShapeDtypeStruct((128, 128), BF16),
         ],
         in_specs=[VMEM] * 5,
-        out_specs=[VMEM] * 2,
+        out_specs=[ANY, VMEM],
+        scratch_shapes=[pltpu.VMEM((count, 256), BF16), pltpu.SemaphoreType.DMA],
         compiler_params=pltpu.CompilerParams(vmem_limit_bytes=LIMIT),
         cost_estimate=cost(LONG, 16 * count * 128),
     )(near, far, kv, prior, gain)
@@ -290,7 +294,7 @@
 
 def output(base, dk, dv, kv, later, near, far):
     count, depth = base.shape
-    steps = 4
+    steps = 2
     return pl.pallas_call(
         output_kernel,
         out_shape=jax.ShapeDtypeStruct((count, depth), BF16),

time: 150 us -> 150 us (level)
    unnamed x13 -> x11, local copies, waits for them, and re-layouts: 3.68 us -> 3.04 us
where the time goes in v9:
time: 150 us; the launch traced here: 149 us
  starting transfers between devices  85.9 us (57%)
  waiting for transfers between devices  31.9 us (21%)
  Pallas kernels  17.6 us (12%)
  blocking collectives  8.36 us (6%)
  local copies, waits for them, and re-layouts  3.84 us (3%)
    all_to_all x4, starting transfers between devices, exchange(): return lax.all_to_all(pieces, SEQ, 0, 0, tiled=True).reshape(state.shape)  34.3 us
    ppermute x6, starting transfers between devices, over_x(): lax.ppermute(block, 'x', [(i, (i + k) % xs) for i in range(xs)])  20.1 us
    all_to_all x2, starting transfers between devices, over_planes(): return lax.all_to_all(copies, ROWS, 0, 0, tiled=True).reshape(-1, head)  17.4 us
    ppermute x5, starting transfers between devices, core_swap(): return lax.ppermute(block, 'core', [(0, 1), (1, 0)])  14.1 us
    all_to_all x4, waiting for transfers between devices, exchange(): return lax.all_to_all(pieces, SEQ, 0, 0, tiled=True).reshape(state.shape)  13.7 us
    all_to_all x2, waiting for transfers between devices, over_planes(): return lax.all_to_all(copies, ROWS, 0, 0, tiled=True).reshape(-1, head)  12.1 us
    all_gather x1, blocking collectives, per_device(): rows = lax.all_gather(rows, 'core', axis=0, tiled=True)  8.36 us
    pallas_call x2, Pallas kernels, project(): pl.pallas_call(functools.partial(project_kernel, tuple(blocks), slot), ou...  6.59 us
  transfers between devices with their start and end apart: 17, of which 9 were waited for; matrix products, arithmetic and copies ran while one was open for 0% of the time, Pallas kernels for 7%

profile of v9, /device:TPU:1, one launch (start us, length us, event | category | flops | bytes accessed | tf_op | source)
XLA Modules:
  0.0 148.7 jit_solution(15656214131373771858)
XLA Ops:
  1.4 8.4 %all-gather = bf16[2,12,512]{2,1,0:T(8,128)(2,1)S(1)} all-gather(bf16[1,12,512]{2,1,0:T(8,128)(2,1)S(1)} %maximum_bitcast_fusion), channel_id=1, replica_groups=mesh['dp'=8,'x'=4,'z'=8,'core'=2] {'core'}, dimensions={0}, use_global_device_ids=true | all-gather | bytes 36864 | tf_op jit(solution)/shard_map/all_gather | solution.py:351
  10.6 10.9 %all-to-all-start = ((bf16[64,24,128]{2,1,0:T(8,128)(2,1)}), bf16[64,24,128]{2,1,0:T(8,128)(2,1)S(1)}, u32[]{:S(2)}, u32[]{:S(2)}) async-start(bf16[64,24,128]{2,1,0:T(8,128)(2,1)} %broadcast_in_dim.4), calls=%async_computation | async-start | bytes 786432 | tf_op jit(solution)/shard_map/all_to_all | solution.py:359
  21.6 2.5 %collective-permute-start = (bf16[136,6144]{1,0:T(8,128)(2,1)}, bf16[136,6144]{1,0:T(8,128)(2,1)}, u32[]{:S(2)}, u32[]{:S(2)}) collective-permute-start(bf16[136,6144]{1,0:T(8,128)(2,1)} %bitcast.34), channel_id=1, source_target_pairs={{0,1},{1,0},{2,3},{3,2},{4,5},{5,4},{6,7},{7,6},{8,9},{9,8},{10,11... | collective-permute-start | bytes 5013512 | tf_op jit(solution)/shard_map/ppermute | solution.py:37
  26.0 10.5 %all-to-all-done = bf16[64,24,128]{2,1,0:T(8,128)(2,1)S(1)} async-done(((bf16[64,24,128]{2,1,0:T(8,128)(2,1)}), bf16[64,24,128]{2,1,0:T(8,128)(2,1)S(1)}, u32[]{:S(2)}, u32[]{:S(2)}) %all-to-all-start) | async-done | bytes 393248 | tf_op jit(solution)/shard_map/all_to_all | solution.py:359
  36.6 4.6 %collective-permute-start.4 = (bf16[1536,128]{1,0:T(8,128)(2,1)S(1)}, bf16[1536,128]{1,0:T(8,128)(2,1)S(1)}, u32[]{:S(2)}, u32[]{:S(2)}) collective-permute-start(bf16[1536,128]{1,0:T(8,128)(2,1)S(1)} %bitcast.23), channel_id=1, source_target_pairs={{0,32},{16,48},{32,0},{48,16},{1,33},{17,49},{33,1},{49,17},{2,34}... | collective-permute-start | bytes 1179656 | tf_op jit(solution)/shard_map/ppermute | solution.py:362
  41.2 2.8 %collective-permute-start.3 = (bf16[1536,128]{1,0:T(8,128)(2,1)S(1)}, bf16[1536,128]{1,0:T(8,128)(2,1)S(1)}, u32[]{:S(2)}, u32[]{:S(2)}) collective-permute-start(bf16[1536,128]{1,0:T(8,128)(2,1)S(1)} %bitcast.24), channel_id=1, source_target_pairs={{0,48},{16,0},{32,16},{48,32},{1,49},{17,1},{33,17},{49,33},{2,50}... | collective-permute-start | bytes 1179656 | tf_op jit(solution)/shard_map/ppermute | solution.py:362
  44.0 2.5 %collective-permute-start.2 = (bf16[1536,128]{1,0:T(8,128)(2,1)S(1)}, bf16[1536,128]{1,0:T(8,128)(2,1)S(1)}, u32[]{:S(2)}, u32[]{:S(2)}) collective-permute-start(bf16[1536,128]{1,0:T(8,128)(2,1)S(1)} %bitcast.25), channel_id=1, source_target_pairs={{0,16},{16,32},{32,48},{48,0},{1,17},{17,33},{33,49},{49,1},{2,18}... | collective-permute-start | bytes 1179656 | tf_op jit(solution)/shard_map/ppermute | solution.py:362
  47.3 6.5 %all-to-all-start.1 = ((bf16[64,24,128]{2,1,0:T(8,128)(2,1)}), bf16[64,24,128]{2,1,0:T(8,128)(2,1)S(1)}, u32[]{:S(2)}, u32[]{:S(2)}) async-start(bf16[64,24,128]{2,1,0:T(8,128)(2,1)} %shard_map.56), calls=%async_computation.1 | async-start | bytes 786432 | tf_op jit(solution)/shard_map/all_to_all | solution.py:359
  53.8 4.1 %collective-permute-done.3.refs_3_ = bf16[1536,128]{1,0:T(8,128)(2,1)S(1)} collective-permute-done((bf16[1536,128]{1,0:T(8,128)(2,1)S(1)}, bf16[1536,128]{1,0:T(8,128)(2,1)S(1)}, u32[]{:S(2)}, u32[]{:S(2)}) %collective-permute-start.3) | collective-permute-done | bytes 393248 | tf_op jit(solution)/shard_map/ppermute | solution.py:362
  58.2 3.3 %shard_map.55 = (bf16[2,6144,128]{2,1,0:T(8,128)(2,1)}, bf16[136,128]{1,0:T(8,128)(2,1)S(1)}, bf16[136,128]{1,0:T(8,128)(2,1)S(1)}) custom-call(bf16[136,6144]{1,0:T(8,128)(2,1)} %bitcast.35, bf16[136,6144]{1,0:T(8,128)(2,1)} %collective-permute-done.refs_1_, bf16[1536,128]{1,0:T(8,128)(2,1)S(1)} %collective-permute-done.2.refs_2_, ...), custom_call_target="tpu_custom_call" | custom-call | flops 80000000000 | bytes 6488064 | tf_op jit(solution)/shard_map/pallas_call | solution.py:81
  61.5 4.2 %collective-permute-start.5 = (bf16[136,128]{1,0:T(8,128)(2,1)S(1)}, bf16[136,128]{1,0:T(8,128)(2,1)S(1)}, u32[]{:S(2)}, u32[]{:S(2)}) collective-permute-start(bf16[136,128]{1,0:T(8,128)(2,1)S(1)} %get-tuple-element.33), channel_id=1, source_target_pairs={{0,1},{1,0},{2,3},{3,2},{4,5},{5,4},{6,7},{7,6},{8,9},{9,8},{10,11... | collective-permute-start | bytes 104456 | tf_op jit(solution)/shard_map/ppermute | solution.py:37
  68.2 10.4 %all-to-all-start.2 = ((bf16[64,2,128]{2,1,0:T(2,128)(2,1)}), bf16[64,2,128]{2,1,0:T(2,128)(2,1)S(1)}, u32[]{:S(2)}, u32[]{:S(2)}) async-start(bf16[64,2,128]{2,1,0:T(2,128)(2,1)} %bitcast.5), calls=%async_computation.2 | async-start | bytes 65536 | tf_op jit(solution)/shard_map/all_to_all | solution.py:340
  78.6 4.9 %collective-permute-start.8 = (bf16[1536,128]{1,0:T(8,128)(2,1)S(1)}, bf16[1536,128]{1,0:T(8,128)(2,1)S(1)}, u32[]{:S(2)}, u32[]{:S(2)}) collective-permute-start(bf16[1536,128]{1,0:T(8,128)(2,1)S(1)} %bitcast.19), channel_id=1, source_target_pairs={{0,32},{16,48},{32,0},{48,16},{1,33},{17,49},{33,1},{49,17},{2,34}... | collective-permute-start | bytes 1179656 | tf_op jit(solution)/shard_map/ppermute | solution.py:362
  83.5 2.7 %collective-permute-start.7 = (bf16[1536,128]{1,0:T(8,128)(2,1)S(1)}, bf16[1536,128]{1,0:T(8,128)(2,1)S(1)}, u32[]{:S(2)}, u32[]{:S(2)}) collective-permute-start(bf16[1536,128]{1,0:T(8,128)(2,1)S(1)} %bitcast.20), channel_id=1, source_target_pairs={{0,48},{16,0},{32,16},{48,32},{1,49},{17,1},{33,17},{49,33},{2,50}... | collective-permute-start | bytes 1179656 | tf_op jit(solution)/shard_map/ppermute | solution.py:362
  86.2 2.6 %collective-permute-start.6 = (bf16[1536,128]{1,0:T(8,128)(2,1)S(1)}, bf16[1536,128]{1,0:T(8,128)(2,1)S(1)}, u32[]{:S(2)}, u32[]{:S(2)}) collective-permute-start(bf16[1536,128]{1,0:T(8,128)(2,1)S(1)} %bitcast.21), channel_id=1, source_target_pairs={{0,16},{16,32},{32,48},{48,0},{1,17},{17,33},{33,49},{49,1},{2,18}... | collective-permute-start | bytes 1179656 | tf_op jit(solution)/shard_map/ppermute | solution.py:362
  89.6 10.2 %all-to-all-start.3 = ((bf16[64,2,128]{2,1,0:T(2,128)(2,1)}), bf16[64,2,128]{2,1,0:T(2,128)(2,1)S(1)}, u32[]{:S(2)}, u32[]{:S(2)}) async-start(bf16[64,2,128]{2,1,0:T(2,128)(2,1)} %bitcast.7), calls=%async_computation.3 | async-start | bytes 65536 | tf_op jit(solution)/shard_map/all_to_all | solution.py:340
  101.4 3.3 %shard_map.58 = (bf16[2,6144,128]{2,1,0:T(8,128)(2,1)}, f32[136,128]{1,0:T(8,128)S(1)}, f32[136,128]{1,0:T(8,128)S(1)}) custom-call(bf16[136,6144]{1,0:T(8,128)(2,1)} %bitcast.36, bf16[136,6144]{1,0:T(8,128)(2,1)} %collective-permute-done.refs_1_, bf16[136,6144]{1,0:T(8,128)(2,1)} %bitcast.38, ...), custom_call_target="tpu_custom_call", output_to_operand_aliasing={{0}: (8, {})} | custom-call | flops 80000000000 | bytes 6488064 | tf_op jit(solution)/shard_map/pallas_call | solution.py:81
  104.7 3.0 %collective-permute-start.9 = (f32[136,128]{1,0:T(8,128)S(1)}, f32[136,128]{1,0:T(8,128)S(1)}, u32[]{:S(2)}, u32[]{:S(2)}) collective-permute-start(f32[136,128]{1,0:T(8,128)S(1)} %get-tuple-element.38), channel_id=1, source_target_pairs={{0,1},{1,0},{2,3},{3,2},{4,5},{5,4},{6,7},{7,6},{8,9},{9,8},{10,11... | collective-permute-start | bytes 208904 | tf_op jit(solution)/shard_map/ppermute | solution.py:37
  111.3 9.2 %all-to-all-start.4 = ((bf16[64,2,128]{2,1,0:T(2,128)(2,1)}), bf16[64,2,128]{2,1,0:T(2,128)(2,1)S(1)}, u32[]{:S(2)}, u32[]{:S(2)}) async-start(bf16[64,2,128]{2,1,0:T(2,128)(2,1)} %bitcast.10), calls=%async_computation.4 | async-start | bytes 65536 | tf_op jit(solution)/shard_map/all_to_all | solution.py:340
  120.4 2.4 %collective-permute-start.10 = (bf16[2,6144,128]{2,1,0:T(8,128)(2,1)}, bf16[2,6144,128]{2,1,0:T(8,128)(2,1)S(1)}, u32[]{:S(2)}, u32[]{:S(2)}) collective-permute-start(bf16[2,6144,128]{2,1,0:T(8,128)(2,1)} %get-tuple-element.42.refs_3_.near_any), channel_id=1, source_target_pairs={{0,1},{1,0},{2,3},{3,2},{4,5},{5,4},{6,7},{7,6},{8,9},{9,8},{10,11... | collective-permute-start | bytes 9437192 | tf_op jit(solution)/shard_map/ppermute | solution.py:37
  122.8 6.9 %all-to-all-done.4 = bf16[64,2,128]{2,1,0:T(2,128)(2,1)S(1)} async-done(((bf16[64,2,128]{2,1,0:T(2,128)(2,1)}), bf16[64,2,128]{2,1,0:T(2,128)(2,1)S(1)}, u32[]{:S(2)}, u32[]{:S(2)}) %all-to-all-start.4) | async-done | bytes 32800 | tf_op jit(solution)/shard_map/all_to_all | solution.py:340
  130.5 4.6 %all-to-all-start.5 = ((bf16[64,2,128]{2,1,0:T(2,128)(2,1)}), bf16[64,2,128]{2,1,0:T(2,128)(2,1)S(1)}, u32[]{:S(2)}, u32[]{:S(2)}) async-start(bf16[64,2,128]{2,1,0:T(2,128)(2,1)} %bitcast.12), calls=%async_computation.5 | async-start | bytes 65536 | tf_op jit(solution)/shard_map/all_to_all | solution.py:340
  139.0 5.5 %all-to-all-done.5 = bf16[64,2,128]{2,1,0:T(2,128)(2,1)S(1)} async-done(((bf16[64,2,128]{2,1,0:T(2,128)(2,1)}), bf16[64,2,128]{2,1,0:T(2,128)(2,1)S(1)}, u32[]{:S(2)}, u32[]{:S(2)}) %all-to-all-start.5) | async-done | bytes 32800 | tf_op jit(solution)/shard_map/all_to_all | solution.py:340
  144.5 4.1 %shard_map.64 = bf16[136,6144]{1,0:T(8,128)(2,1)} custom-call(f32[136,6144]{1,0:T(8,128)S(1)} %get-tuple-element.43.base, f32[136,128]{1,0:T(8,128)S(1)} %get-tuple-element.44.dk, f32[136,128]{1,0:T(8,128)S(1)} %get-tuple-element.45.dv, bf16[136,256]{1,0:T(8,128)(2,1)} %copy-done, bf16[128,128]{1,0:T(8,128)(2,1)S(1)} %bitcast.27, ...), custom_call_target="tpu_custom_call" | custom-call | flops 427819008 | bytes 8159232 | tf_op jit(solution)/shard_map/pallas_call | solution.py:298
  (35 shorter events, 18.2 us)
Async XLA Ops:
  10.6 25.9 %all-to-all-start = ((bf16[64,24,128]{2,1,0:T(8,128)(2,1)}), bf16[64,24,128]{2,1,0:T(8,128)(2,1)S(1)}, u32[]{:S(2)}, u32[]{:S(2)}) async-start(bf16[64,24,128]{2,1,0:T(8,128)(2,1)} %broadcast_in_dim.4), calls=%async_computation | async-start | bytes 786432 | tf_op jit(solution)/shard_map/all_to_all | solution.py:359
  21.6 32.3 %collective-permute-start = (bf16[136,6144]{1,0:T(8,128)(2,1)}, bf16[136,6144]{1,0:T(8,128)(2,1)}, u32[]{:S(2)}, u32[]{:S(2)}) collective-permute-start(bf16[136,6144]{1,0:T(8,128)(2,1)} %bitcast.34), channel_id=1, source_target_pairs={{0,1},{1,0},{2,3},{3,2},{4,5},{5,4},{6,7},{7,6},{8,9},{9,8},{10,11... | collective-permute-start | bytes 5013512 | tf_op jit(solution)/shard_map/ppermute | solution.py:37
  24.1 29.7 %collective-permute-start.1 = (bf16[136,6144]{1,0:T(8,128)(2,1)}, bf16[136,6144]{1,0:T(8,128)(2,1)}, u32[]{:S(2)}, u32[]{:S(2)}) collective-permute-start(bf16[136,6144]{1,0:T(8,128)(2,1)} %bitcast.37), channel_id=1, source_target_pairs={{0,1},{1,0},{2,3},{3,2},{4,5},{5,4},{6,7},{7,6},{8,9},{9,8},{10,11... | collective-permute-start | bytes 5013512 | tf_op jit(solution)/shard_map/ppermute | solution.py:37
  36.6 17.3 %collective-permute-start.4 = (bf16[1536,128]{1,0:T(8,128)(2,1)S(1)}, bf16[1536,128]{1,0:T(8,128)(2,1)S(1)}, u32[]{:S(2)}, u32[]{:S(2)}) collective-permute-start(bf16[1536,128]{1,0:T(8,128)(2,1)S(1)} %bitcast.23), channel_id=1, source_target_pairs={{0,32},{16,48},{32,0},{48,16},{1,33},{17,49},{33,1},{49,17},{2,34}... | collective-permute-start | bytes 1179656 | tf_op jit(solution)/shard_map/ppermute | solution.py:362
  41.2 16.7 %collective-permute-start.3 = (bf16[1536,128]{1,0:T(8,128)(2,1)S(1)}, bf16[1536,128]{1,0:T(8,128)(2,1)S(1)}, u32[]{:S(2)}, u32[]{:S(2)}) collective-permute-start(bf16[1536,128]{1,0:T(8,128)(2,1)S(1)} %bitcast.24), channel_id=1, source_target_pairs={{0,48},{16,0},{32,16},{48,32},{1,49},{17,1},{33,17},{49,33},{2,50}... | collective-permute-start | bytes 1179656 | tf_op jit(solution)/shard_map/ppermute | solution.py:362
  44.0 14.3 %collective-permute-start.2 = (bf16[1536,128]{1,0:T(8,128)(2,1)S(1)}, bf16[1536,128]{1,0:T(8,128)(2,1)S(1)}, u32[]{:S(2)}, u32[]{:S(2)}) collective-permute-start(bf16[1536,128]{1,0:T(8,128)(2,1)S(1)} %bitcast.25), channel_id=1, source_target_pairs={{0,16},{16,32},{32,48},{48,0},{1,17},{17,33},{33,49},{49,1},{2,18}... | collective-permute-start | bytes 1179656 | tf_op jit(solution)/shard_map/ppermute | solution.py:362
  47.3 20.1 %all-to-all-start.1 = ((bf16[64,24,128]{2,1,0:T(8,128)(2,1)}), bf16[64,24,128]{2,1,0:T(8,128)(2,1)S(1)}, u32[]{:S(2)}, u32[]{:S(2)}) async-start(bf16[64,24,128]{2,1,0:T(8,128)(2,1)} %shard_map.56), calls=%async_computation.1 | async-start | bytes 786432 | tf_op jit(solution)/shard_map/all_to_all | solution.py:359
  61.5 5.9 %collective-permute-start.5 = (bf16[136,128]{1,0:T(8,128)(2,1)S(1)}, bf16[136,128]{1,0:T(8,128)(2,1)S(1)}, u32[]{:S(2)}, u32[]{:S(2)}) collective-permute-start(bf16[136,128]{1,0:T(8,128)(2,1)S(1)} %get-tuple-element.33), channel_id=1, source_target_pairs={{0,1},{1,0},{2,3},{3,2},{4,5},{5,4},{6,7},{7,6},{8,9},{9,8},{10,11... | collective-permute-start | bytes 104456 | tf_op jit(solution)/shard_map/ppermute | solution.py:37
  68.2 40.7 %copy-start = (bf16[136,256]{1,0:T(8,128)(2,1)}, bf16[136,256]{1,0:T(8,128)(2,1)S(1)}, u32[]{:S(2)}) copy-start(bf16[136,256]{1,0:T(8,128)(2,1)S(1)} %get-tuple-element.40.kv_ref.refs_1_.kv_any) | copy-start | bytes 208900
  68.2 20.6 %all-to-all-start.2 = ((bf16[64,2,128]{2,1,0:T(2,128)(2,1)}), bf16[64,2,128]{2,1,0:T(2,128)(2,1)S(1)}, u32[]{:S(2)}, u32[]{:S(2)}) async-start(bf16[64,2,128]{2,1,0:T(2,128)(2,1)} %bitcast.5), calls=%async_computation.2 | async-start | bytes 65536 | tf_op jit(solution)/shard_map/all_to_all | solution.py:340
  78.6 21.1 %collective-permute-start.8 = (bf16[1536,128]{1,0:T(8,128)(2,1)S(1)}, bf16[1536,128]{1,0:T(8,128)(2,1)S(1)}, u32[]{:S(2)}, u32[]{:S(2)}) collective-permute-start(bf16[1536,128]{1,0:T(8,128)(2,1)S(1)} %bitcast.19), channel_id=1, source_target_pairs={{0,32},{16,48},{32,0},{48,16},{1,33},{17,49},{33,1},{49,17},{2,34}... | collective-permute-start | bytes 1179656 | tf_op jit(solution)/shard_map/ppermute | solution.py:362
  83.5 17.8 %collective-permute-start.7 = (bf16[1536,128]{1,0:T(8,128)(2,1)S(1)}, bf16[1536,128]{1,0:T(8,128)(2,1)S(1)}, u32[]{:S(2)}, u32[]{:S(2)}) collective-permute-start(bf16[1536,128]{1,0:T(8,128)(2,1)S(1)} %bitcast.20), channel_id=1, source_target_pairs={{0,48},{16,0},{32,16},{48,32},{1,49},{17,1},{33,17},{49,33},{2,50}... | collective-permute-start | bytes 1179656 | tf_op jit(solution)/shard_map/ppermute | solution.py:362
  86.2 15.2 %collective-permute-start.6 = (bf16[1536,128]{1,0:T(8,128)(2,1)S(1)}, bf16[1536,128]{1,0:T(8,128)(2,1)S(1)}, u32[]{:S(2)}, u32[]{:S(2)}) collective-permute-start(bf16[1536,128]{1,0:T(8,128)(2,1)S(1)} %bitcast.21), channel_id=1, source_target_pairs={{0,16},{16,32},{32,48},{48,0},{1,17},{17,33},{33,49},{49,1},{2,18}... | collective-permute-start | bytes 1179656 | tf_op jit(solution)/shard_map/ppermute | solution.py:362
  89.6 19.4 %all-to-all-start.3 = ((bf16[64,2,128]{2,1,0:T(2,128)(2,1)}), bf16[64,2,128]{2,1,0:T(2,128)(2,1)S(1)}, u32[]{:S(2)}, u32[]{:S(2)}) async-start(bf16[64,2,128]{2,1,0:T(2,128)(2,1)} %bitcast.7), calls=%async_computation.3 | async-start | bytes 65536 | tf_op jit(solution)/shard_map/all_to_all | solution.py:340
  104.7 4.2 %collective-permute-start.9 = (f32[136,128]{1,0:T(8,128)S(1)}, f32[136,128]{1,0:T(8,128)S(1)}, u32[]{:S(2)}, u32[]{:S(2)}) collective-permute-start(f32[136,128]{1,0:T(8,128)S(1)} %get-tuple-element.38), channel_id=1, source_target_pairs={{0,1},{1,0},{2,3},{3,2},{4,5},{5,4},{6,7},{7,6},{8,9},{9,8},{10,11... | collective-permute-start | bytes 208904 | tf_op jit(solution)/shard_map/ppermute | solution.py:37
  108.9 0.7 copy-start.1
  109.0 2.3 %copy-start.2 = (bf16[128,128]{1,0:T(8,128)(2,1)}, bf16[128,128]{1,0:T(8,128)(2,1)S(1)}, u32[]{:S(2)}) copy-start(bf16[128,128]{1,0:T(8,128)(2,1)S(1)} %shard_map.60.prior_ref.refs_2_) | copy-start | bytes 98308
  111.3 18.4 %all-to-all-start.4 = ((bf16[64,2,128]{2,1,0:T(2,128)(2,1)}), bf16[64,2,128]{2,1,0:T(2,128)(2,1)S(1)}, u32[]{:S(2)}, u32[]{:S(2)}) async-start(bf16[64,2,128]{2,1,0:T(2,128)(2,1)} %bitcast.10), calls=%async_computation.4 | async-start | bytes 65536 | tf_op jit(solution)/shard_map/all_to_all | solution.py:340
  120.4 14.7 %collective-permute-start.10 = (bf16[2,6144,128]{2,1,0:T(8,128)(2,1)}, bf16[2,6144,128]{2,1,0:T(8,128)(2,1)S(1)}, u32[]{:S(2)}, u32[]{:S(2)}) collective-permute-start(bf16[2,6144,128]{2,1,0:T(8,128)(2,1)} %get-tuple-element.42.refs_3_.near_any), channel_id=1, source_target_pairs={{0,1},{1,0},{2,3},{3,2},{4,5},{5,4},{6,7},{7,6},{8,9},{9,8},{10,11... | collective-permute-start | bytes 9437192 | tf_op jit(solution)/shard_map/ppermute | solution.py:37
  130.5 14.0 %all-to-all-start.5 = ((bf16[64,2,128]{2,1,0:T(2,128)(2,1)}), bf16[64,2,128]{2,1,0:T(2,128)(2,1)S(1)}, u32[]{:S(2)}, u32[]{:S(2)}) async-start(bf16[64,2,128]{2,1,0:T(2,128)(2,1)} %bitcast.12), calls=%async_computation.5 | async-start | bytes 65536 | tf_op jit(solution)/shard_map/all_to_all | solution.py:340
  135.1 1.7 %copy-start.3 = (bf16[2,6144,128]{2,1,0:T(8,128)(2,1)}, bf16[2,6144,128]{2,1,0:T(8,128)(2,1)S(1)}, u32[]{:S(2)}) copy-start(bf16[2,6144,128]{2,1,0:T(8,128)(2,1)S(1)} %collective-permute-done.10.refs_4_.far_any) | copy-start | bytes 9437188
